TPU v7x, 32 devices: a whole 2x2x4 slice. The times are simulated.
32 devices in a mesh: tile: 8 (over z, y), cuts: 4 (over x, core).
Axes of the slice: x: 2, y: 2, z: 4, core: 2. Of those that a mesh axis runs over, the one named last changes fastest.
Arguments:
- transmission: float32 [4, 2, 2048, 1024], P('cuts', None, 'tile')
- probe: float32 [2, 256, 256], replicated, may hold values from -6 to 6
- prop_phase: float32 [256, 256], replicated, may hold values from -3.140625 to 3.140625
- row_off: int32 [8], P('tile'), may hold values from 0 to 255
- col_off: int32 [8], P('tile'), may hold values from 0 to 768
- measured: float32 [8, 256, 256], P('tile'), may hold values from 0 to 1.6
Outputs:
- obj_grad: float32 [4, 2, 2048, 1024], P('cuts', None, 'tile')
All inputs are finite; a program needn't handle non-finite values.
Results may differ from a plain program's by a relative error of at most 0.0003.
Values sent between devices are 32-bit elements; how exact they have to be, the bound alone decides.
No kernel may reach another device: no remote copies, remote signals or barrier semaphores. Data moves between devices by JAX's collectives and lax.ppermute only.
A program may use at most 64 MiB of HBM per device.

v0:
```python
import jax
import jax.numpy as jnp
from jax import lax
from jax.sharding import PartitionSpec as P

precise = lax.Precision.HIGHEST


def shifted(value, axis, by):
    devices = lax.axis_size(axis)
    pairs = [(i, i + by) for i in range(devices) if 0 <= i + by < devices]
    return lax.ppermute(value, axis, pairs)


def dft_tables(length):
    index = lax.iota(jnp.int32, length)
    product = index[:, None] * index[None, :] % length
    angle = product.astype(jnp.float32) * (2.0 * jnp.pi / length)
    factor = 1.0 / jnp.sqrt(jnp.float32(length))
    return (jnp.cos(angle) * factor, jnp.sin(angle) * factor)


def transform(real_part, imag_part, tables, direction):
    cosines = tables[0]
    signed = tables[1] * direction

    def left(matrix, block):
        return jnp.einsum("jk,bkl->bjl", matrix, block, precision=precise)

    def right(block, matrix):
        return jnp.einsum("bjk,kl->bjl", block, matrix, precision=precise)

    middle_real = left(cosines, real_part) - left(signed, imag_part)
    middle_imag = left(cosines, imag_part) + left(signed, real_part)
    out_real = right(middle_real, cosines) - right(middle_imag, signed)
    out_imag = right(middle_imag, cosines) + right(middle_real, signed)
    return (out_real, out_imag)


def propagate(real_part, imag_part, tables, kernel_real, kernel_imag):
    freq_real, freq_imag = transform(real_part, imag_part, tables, -1.0)
    prod_real = freq_real * kernel_real - freq_imag * kernel_imag
    prod_imag = freq_real * kernel_imag + freq_imag * kernel_real
    return transform(prod_real, prod_imag, tables, 1.0)


def forward_group(wave_real, wave_imag, patch_real, patch_imag, tables, kernel):
    saved_real = [wave_real]
    saved_imag = [wave_imag]
    layer_real = patch_real[:, 0]
    layer_imag = patch_imag[:, 0]
    mixed_real = wave_real * layer_real - wave_imag * layer_imag
    mixed_imag = wave_real * layer_imag + wave_imag * layer_real
    wave_real, wave_imag = propagate(mixed_real, mixed_imag, tables, kernel[0], kernel[1])
    return (wave_real, wave_imag, jnp.stack(saved_real, axis=1), jnp.stack(saved_imag, axis=1))


def far_field(wave_real, wave_imag, observed, tables):
    far_real, far_imag = transform(wave_real, wave_imag, tables, -1.0)
    residual = far_real * far_real + far_imag * far_imag - observed
    return transform(residual * far_real, residual * far_imag, tables, 1.0)


def backward_group(
    grad_real, grad_imag, saved_real, saved_imag, patch_real, patch_imag, tables, kernel
):
    layers = patch_real.shape[1]
    pieces_real = [None] * layers
    pieces_imag = [None] * layers
    inner_real, inner_imag = propagate(grad_real, grad_imag, tables, kernel[0], -kernel[1])
    wave_real = saved_real[:, 0]
    wave_imag = saved_imag[:, 0]
    pieces_real[0] = wave_real * inner_real + wave_imag * inner_imag
    pieces_imag[0] = wave_real * inner_imag - wave_imag * inner_real
    layer_real = patch_real[:, 0]
    layer_imag = patch_imag[:, 0]
    grad_real = layer_real * inner_real + layer_imag * inner_imag
    grad_imag = layer_real * inner_imag - layer_imag * inner_real
    return (grad_real, grad_imag, jnp.stack(pieces_real, axis=1), jnp.stack(pieces_imag, axis=1))


def per_device(transmission, probe, prop_phase, row_off, col_off, measured):
    layers = transmission.shape[0]
    rows = transmission.shape[2]
    columns = transmission.shape[3]
    width = probe.shape[1]
    count = row_off.shape[0]
    tables = dft_tables(width)
    kernel = (jnp.cos(prop_phase), jnp.sin(prop_phase))
    zero = jnp.zeros((), jnp.int32)
    band = shifted(transmission, "tile", -1)
    whole = jnp.concatenate([transmission, band], axis=2)

    def cut_patch(row, column):
        return lax.dynamic_slice(whole, (zero, zero, row, column), (layers, 2, width, width))

    patches = jax.vmap(cut_patch)(row_off, col_off)
    patch_real = patches[:, :, 0]
    patch_imag = patches[:, :, 1]
    cut_index = lax.axis_index("cuts")
    sections = lax.axis_size("cuts")
    final_section = sections - 1
    empty_saved = jnp.zeros((count, layers, width, width), jnp.float32)
    wave_real = jnp.broadcast_to(probe[0], (count, width, width))
    wave_imag = jnp.broadcast_to(probe[1], (count, width, width))
    saved_real = empty_saved
    saved_imag = empty_saved
    for section in range(sections):
        if section > 0:
            wave_real, wave_imag = shifted((wave_real, wave_imag), "cuts", 1)
        state = (wave_real, wave_imag, saved_real, saved_imag)
        wave_real, wave_imag, saved_real, saved_imag = lax.cond(
            cut_index == section,
            lambda values: forward_group(
                values[0], values[1], patch_real, patch_imag, tables, kernel
            ),
            lambda values: values,
            state,
        )
    grad_real, grad_imag = lax.cond(
        cut_index == final_section,
        lambda values: far_field(values[0], values[1], measured, tables),
        lambda values: (jnp.zeros_like(values[0]), jnp.zeros_like(values[1])),
        (wave_real, wave_imag),
    )
    piece_real = empty_saved
    piece_imag = empty_saved
    for section in range(final_section, -1, -1):
        if section < final_section:
            grad_real, grad_imag = shifted((grad_real, grad_imag), "cuts", -1)
        state = (grad_real, grad_imag, piece_real, piece_imag)
        grad_real, grad_imag, piece_real, piece_imag = lax.cond(
            cut_index == section,
            lambda values: backward_group(
                values[0], values[1], saved_real, saved_imag, patch_real, patch_imag, tables, kernel
            ),
            lambda values: values,
            state,
        )
    buffer = jnp.zeros((layers, 2, rows + width, columns), jnp.float32)

    def add_patch(position, totals):
        corner = (zero, zero, row_off[position], col_off[position])
        piece = jnp.stack([piece_real[position], piece_imag[position]], axis=1)
        current = lax.dynamic_slice(totals, corner, piece.shape)
        return lax.dynamic_update_slice(totals, current + piece, corner)

    buffer = lax.fori_loop(0, count, add_patch, buffer)
    returned = shifted(buffer[:, :, rows:, :], "tile", 1)
    result_grad = buffer[:, :, :rows, :] + returned
    return result_grad


def solution(mesh):
    placed = (P("cuts", None, "tile", None), P(), P(), P("tile"), P("tile"), P("tile", None, None))
    return jax.shard_map(
        per_device,
        mesh=mesh,
        in_specs=placed,
        out_specs=P("cuts", None, "tile", None),
        check_vma=False,
    )
```

profile of v0, /device:TPU:0, one launch (start us, length us, event | category | flops | bytes accessed | tf_op | source)
XLA Modules:
  0.0 241.7 jit_solution(15601848371198366516)
XLA Ops:
  4.9 1.9 fusion.270
  6.7 44.1 %collective-permute-done = f32[1,2,256,1024]{3,2,1,0:T(8,128)} collective-permute-done((f32[1,2,256,1024]{3,2,1,0:T(8,128)}, f32[1,2,256,1024]{3,2,1,0:T(8,128)}, u32[]{:S(2)}, u32[]{:S(2)}) %collective-permute-start) | collective-permute-done | bytes 2097184 | tf_op jit(solution)/shard_map/ppermute | solution.py:12
  50.8 1.3 fusion.261
  52.1 10.0 %conditional.9 = (f32[1,256,256]{2,1,0:T(8,128)S(1)}, f32[1,256,256]{2,1,0:T(8,128)S(1)}, f32[1,1,256,256]{3,2,1,0:T(8,128)S(1)}, f32[1,1,256,256]{3,2,1,0:T(8,128)S(1)}) conditional(s32[]{:T(128)} %convert_element_type.306, (f32[1,256,256]{2,1,0:T(8,128)S(1)}, f32[1,256,256]{2,1,0:T(8,128)S(1)}) %tuple.73, (f32[1,1,1,256,256]{4,3,2,1,0:T(8,128)S(1)}, ...), branch_computations={%region_0.1_spmd, %region_1.2_spmd} | conditional | flops 3222798336 | bytes 17301536 | solution.py:112
  62.2 1.3 collective-permute-start.1
  63.5 1.3 collective-permute-start.2
  66.2 12.0 %collective-permute-start.3 = (f32[1,256,256]{2,1,0:T(8,128)S(1)}, f32[1,256,256]{2,1,0:T(8,128)S(1)}, u32[]{:S(2)}, u32[]{:S(2)}) collective-permute-start(f32[1,256,256]{2,1,0:T(8,128)S(1)} %get-tuple-element.595), channel_id=1, source_target_pairs={{0,1},{1,2},{2,3},{4,5},{5,6},{6,7},{8,9},{9,10},{10,11},{12,13},{... | collective-permute-start | bytes 786440 | tf_op jit(solution)/shard_map/ppermute | solution.py:12
  78.2 1.9 collective-permute-start.4
  81.8 5.0 %collective-permute-start.5 = (f32[1,256,256]{2,1,0:T(8,128)S(1)}, f32[1,256,256]{2,1,0:T(8,128)S(1)}, u32[]{:S(2)}, u32[]{:S(2)}) collective-permute-start(f32[1,256,256]{2,1,0:T(8,128)S(1)} %get-tuple-element.599), channel_id=1, source_target_pairs={{0,1},{1,2},{2,3},{4,5},{5,6},{6,7},{8,9},{9,10},{10,11},{12,13},{... | collective-permute-start | bytes 786440 | tf_op jit(solution)/shard_map/ppermute | solution.py:12
  86.7 14.1 %collective-permute-start.6 = (f32[1,256,256]{2,1,0:T(8,128)S(1)}, f32[1,256,256]{2,1,0:T(8,128)S(1)}, u32[]{:S(2)}, u32[]{:S(2)}) collective-permute-start(f32[1,256,256]{2,1,0:T(8,128)S(1)} %get-tuple-element.600), channel_id=1, source_target_pairs={{0,1},{1,2},{2,3},{4,5},{5,6},{6,7},{8,9},{9,10},{10,11},{12,13},{... | collective-permute-start | bytes 786440 | tf_op jit(solution)/shard_map/ppermute | solution.py:12
  103.0 6.3 %conditional.13 = (f32[1,256,256]{2,1,0:T(8,128)S(1)}, f32[1,256,256]{2,1,0:T(8,128)S(1)}) conditional(s32[]{:T(128)} %convert_element_type.309, () %tuple.72, (f32[1,256,256]{2,1,0:T(8,128)S(1)}, f32[256,256]{1,0:T(8,128)S(1)}, f32[256,256]{1,0:T(8,128)S(1)}, f32[256,256]{1,0:T(8,128)S(1)}, f32[256,256]{1,0:T(8,128)S(1)}, ...), branch_computations={%region_8.9_spmd, %region_9.10_spmd} | conditional | flops 3223322624 | bytes 16777232 | solution.py:120
  109.2 7.4 %conditional.14 = (f32[1,256,256]{2,1,0:T(8,128)S(1)}, f32[1,256,256]{2,1,0:T(8,128)S(1)}, f32[1,1,256,256]{3,2,1,0:T(8,128)}, f32[1,1,256,256]{3,2,1,0:T(8,128)}) conditional(s32[]{:T(128)} %convert_element_type.309, (f32[1,256,256]{2,1,0:T(8,128)S(1)}, f32[1,256,256]{2,1,0:T(8,128)S(1)}) %conditional.13, (f32[1,1,1,256,256]{4,3,2,1,0:T(8,128)S(1)}, ...), branch_computations={%region_10.11_spmd, %region_11.12_spmd} | conditional | flops 3223257088 | bytes 17825824 | solution.py:132
  116.6 1.3 collective-permute-start.7
  117.9 1.3 collective-permute-start.8
  119.2 3.4 %collective-permute-done.7 = f32[1,256,256]{2,1,0:T(8,128)S(1)} collective-permute-done((f32[1,256,256]{2,1,0:T(8,128)S(1)}, f32[1,256,256]{2,1,0:T(8,128)S(1)}, u32[]{:S(2)}, u32[]{:S(2)}) %collective-permute-start.7) | collective-permute-done | bytes 262176 | tf_op jit(solution)/shard_map/ppermute | solution.py:12
  122.6 1.9 collective-permute-done.8
  124.7 1.3 collective-permute-start.9
  126.0 1.3 collective-permute-start.10
  127.3 6.7 %collective-permute-done.9 = f32[1,256,256]{2,1,0:T(8,128)S(1)} collective-permute-done((f32[1,256,256]{2,1,0:T(8,128)S(1)}, f32[1,256,256]{2,1,0:T(8,128)S(1)}, u32[]{:S(2)}, u32[]{:S(2)}) %collective-permute-start.9) | collective-permute-done | bytes 262176 | tf_op jit(solution)/shard_map/ppermute | solution.py:12
  134.0 1.9 collective-permute-done.10
  136.1 1.3 collective-permute-start.11
  137.4 1.3 collective-permute-start.12
  138.7 31.5 %collective-permute-done.11 = f32[1,256,256]{2,1,0:T(8,128)S(1)} collective-permute-done((f32[1,256,256]{2,1,0:T(8,128)S(1)}, f32[1,256,256]{2,1,0:T(8,128)S(1)}, u32[]{:S(2)}, u32[]{:S(2)}) %collective-permute-start.11) | collective-permute-done | bytes 262176 | tf_op jit(solution)/shard_map/ppermute | solution.py:12
  170.2 1.9 collective-permute-done.12
  172.1 10.8 %conditional.17 = ((f32[1,1,256,256]{3,2,1,0:T(8,128)}, f32[1,1,256,256]{3,2,1,0:T(8,128)})) conditional(s32[]{:T(128)} %convert_element_type.306, (f32[1,1,256,256]{3,2,1,0:T(8,128)}, f32[1,1,256,256]{3,2,1,0:T(8,128)}) %tuple.87, (f32[1,1,256,256]{3,2,1,0:T(8,128)S(1)}, f32[1,256,256]{2,1,0:T(8,128)S(1)}, f32[256,256]{1,0:T(8,128)S(1)}, ...), branch_computations={%region_16.17_spmd, %region_17.18_spmd} | conditional | flops 3222863872 | bytes 16777240 | solution.py:132
  181.5 1.4 fusion.241
  184.0 2.5 %broadcast_in_dim.15 = f32[1,2,512,1024]{3,2,1,0:T(8,128)} broadcast(f32[]{:T(128)} %constant.38.clone.1), dimensions={} | broadcast | bytes 4194308 | tf_op jit(solution)/shard_map/broadcast_in_dim | solution.py:140
  186.5 6.7 %dynamic_update_slice.4 = f32[1,2,512,1024]{3,2,1,0:T(8,128)} dynamic-update-slice(f32[1,2,512,1024]{3,2,1,0:T(8,128)} %broadcast_in_dim.15, f32[1,2,256,256]{3,2,1,0:T(8,128)S(1)} %pad_maximum_fusion, s32[]{:T(128)} %constant.42.clone.1, s32[]{:T(128)} %constant.42.clone.1, s32[]{:T(128)S(6)} %select_n.317, s32[]{:T(128)S(6)} %select_n.318) | dynamic-update-slice | bytes 1048580 | tf_op jit(solution)/shard_map/while/body/eval_jaxpr/dynamic_update_slice | solution.py:146
  193.2 1.9 slice.48
  195.1 4.6 %collective-permute-start.13 = (f32[1,2,256,1024]{3,2,1,0:T(8,128)S(1)}, f32[1,2,256,1024]{3,2,1,0:T(8,128)S(1)}, u32[]{:S(2)}, u32[]{:S(2)}) collective-permute-start(f32[1,2,256,1024]{3,2,1,0:T(8,128)S(1)} %slice.48), channel_id=1, source_target_pairs={{0,4},{4,8},{8,12},{12,16},{16,20},{20,24},{24,28},{1,5},{5,9},{9,... | collective-permute-start | bytes 6291464 | tf_op jit(solution)/shard_map/ppermute | solution.py:12
  199.7 40.0 %collective-permute-done.13 = f32[1,2,256,1024]{3,2,1,0:T(8,128)S(1)} collective-permute-done((f32[1,2,256,1024]{3,2,1,0:T(8,128)S(1)}, f32[1,2,256,1024]{3,2,1,0:T(8,128)S(1)}, u32[]{:S(2)}, u32[]{:S(2)}) %collective-permute-start.13) | collective-permute-done | bytes 2097184 | tf_op jit(solution)/shard_map/ppermute | solution.py:12
  239.7 1.7 slice_add_fusion
  (62 shorter events, 30.1 us)
Async XLA Ops:
  0.0 50.8 %collective-permute-start = (f32[1,2,256,1024]{3,2,1,0:T(8,128)}, f32[1,2,256,1024]{3,2,1,0:T(8,128)}, u32[]{:S(2)}, u32[]{:S(2)}) collective-permute-start(f32[1,2,256,1024]{3,2,1,0:T(8,128)} %param.24), channel_id=1, source_target_pairs={{4,0},{8,4},{12,8},{16,12},{20,16},{24,20},{28,24},{5,1},{9,5},{13... | collective-permute-start | bytes 6291464 | tf_op jit(solution)/shard_map/ppermute | solution.py:12
  1.3 49.5 %copy-start.2 = (f32[1,2,256,1024]{3,2,1,0:T(8,128)S(1)}, f32[1,2,256,1024]{3,2,1,0:T(8,128)}, u32[]{:S(2)}) copy-start(f32[1,2,256,1024]{3,2,1,0:T(8,128)} %param.24) | copy-start | bytes 6291460
  62.2 2.6 %collective-permute-start.1 = (f32[1,256,256]{2,1,0:T(8,128)S(1)}, f32[1,256,256]{2,1,0:T(8,128)S(1)}, u32[]{:S(2)}, u32[]{:S(2)}) collective-permute-start(f32[1,256,256]{2,1,0:T(8,128)S(1)} %get-tuple-element.591), channel_id=1, source_target_pairs={{0,1},{1,2},{2,3},{4,5},{5,6},{6,7},{8,9},{9,10},{10,11},{12,13},{... | collective-permute-start | bytes 786440 | tf_op jit(solution)/shard_map/ppermute | solution.py:12
  63.5 2.4 %collective-permute-start.2 = (f32[1,256,256]{2,1,0:T(8,128)S(1)}, f32[1,256,256]{2,1,0:T(8,128)S(1)}, u32[]{:S(2)}, u32[]{:S(2)}) collective-permute-start(f32[1,256,256]{2,1,0:T(8,128)S(1)} %get-tuple-element.592), channel_id=1, source_target_pairs={{0,1},{1,2},{2,3},{4,5},{5,6},{6,7},{8,9},{9,10},{10,11},{12,13},{... | collective-permute-start | bytes 786440 | tf_op jit(solution)/shard_map/ppermute | solution.py:12
  66.2 14.0 %collective-permute-start.3 = (f32[1,256,256]{2,1,0:T(8,128)S(1)}, f32[1,256,256]{2,1,0:T(8,128)S(1)}, u32[]{:S(2)}, u32[]{:S(2)}) collective-permute-start(f32[1,256,256]{2,1,0:T(8,128)S(1)} %get-tuple-element.595), channel_id=1, source_target_pairs={{0,1},{1,2},{2,3},{4,5},{5,6},{6,7},{8,9},{9,10},{10,11},{12,13},{... | collective-permute-start | bytes 786440 | tf_op jit(solution)/shard_map/ppermute | solution.py:12
  78.2 3.1 %collective-permute-start.4 = (f32[1,256,256]{2,1,0:T(8,128)S(1)}, f32[1,256,256]{2,1,0:T(8,128)S(1)}, u32[]{:S(2)}, u32[]{:S(2)}) collective-permute-start(f32[1,256,256]{2,1,0:T(8,128)S(1)} %get-tuple-element.596), channel_id=1, source_target_pairs={{0,1},{1,2},{2,3},{4,5},{5,6},{6,7},{8,9},{9,10},{10,11},{12,13},{... | collective-permute-start | bytes 786440 | tf_op jit(solution)/shard_map/ppermute | solution.py:12
  81.8 19.1 %collective-permute-start.5 = (f32[1,256,256]{2,1,0:T(8,128)S(1)}, f32[1,256,256]{2,1,0:T(8,128)S(1)}, u32[]{:S(2)}, u32[]{:S(2)}) collective-permute-start(f32[1,256,256]{2,1,0:T(8,128)S(1)} %get-tuple-element.599), channel_id=1, source_target_pairs={{0,1},{1,2},{2,3},{4,5},{5,6},{6,7},{8,9},{9,10},{10,11},{12,13},{... | collective-permute-start | bytes 786440 | tf_op jit(solution)/shard_map/ppermute | solution.py:12
  86.7 15.3 %collective-permute-start.6 = (f32[1,256,256]{2,1,0:T(8,128)S(1)}, f32[1,256,256]{2,1,0:T(8,128)S(1)}, u32[]{:S(2)}, u32[]{:S(2)}) collective-permute-start(f32[1,256,256]{2,1,0:T(8,128)S(1)} %get-tuple-element.600), channel_id=1, source_target_pairs={{0,1},{1,2},{2,3},{4,5},{5,6},{6,7},{8,9},{9,10},{10,11},{12,13},{... | collective-permute-start | bytes 786440 | tf_op jit(solution)/shard_map/ppermute | solution.py:12
  102.0 0.9 copy-start.1
  116.6 6.0 %collective-permute-start.7 = (f32[1,256,256]{2,1,0:T(8,128)S(1)}, f32[1,256,256]{2,1,0:T(8,128)S(1)}, u32[]{:S(2)}, u32[]{:S(2)}) collective-permute-start(f32[1,256,256]{2,1,0:T(8,128)S(1)} %get-tuple-element.609), channel_id=1, source_target_pairs={{1,0},{2,1},{3,2},{5,4},{6,5},{7,6},{9,8},{10,9},{11,10},{13,12},{... | collective-permute-start | bytes 786440 | tf_op jit(solution)/shard_map/ppermute | solution.py:12
  117.9 6.6 %collective-permute-start.8 = (f32[1,256,256]{2,1,0:T(8,128)S(1)}, f32[1,256,256]{2,1,0:T(8,128)S(1)}, u32[]{:S(2)}, u32[]{:S(2)}) collective-permute-start(f32[1,256,256]{2,1,0:T(8,128)S(1)} %get-tuple-element.610), channel_id=1, source_target_pairs={{1,0},{2,1},{3,2},{5,4},{6,5},{7,6},{9,8},{10,9},{11,10},{13,12},{... | collective-permute-start | bytes 786440 | tf_op jit(solution)/shard_map/ppermute | solution.py:12
  124.7 9.3 %collective-permute-start.9 = (f32[1,256,256]{2,1,0:T(8,128)S(1)}, f32[1,256,256]{2,1,0:T(8,128)S(1)}, u32[]{:S(2)}, u32[]{:S(2)}) collective-permute-start(f32[1,256,256]{2,1,0:T(8,128)S(1)} %get-tuple-element.613), channel_id=1, source_target_pairs={{1,0},{2,1},{3,2},{5,4},{6,5},{7,6},{9,8},{10,9},{11,10},{13,12},{... | collective-permute-start | bytes 786440 | tf_op jit(solution)/shard_map/ppermute | solution.py:12
  126.0 9.9 %collective-permute-start.10 = (f32[1,256,256]{2,1,0:T(8,128)S(1)}, f32[1,256,256]{2,1,0:T(8,128)S(1)}, u32[]{:S(2)}, u32[]{:S(2)}) collective-permute-start(f32[1,256,256]{2,1,0:T(8,128)S(1)} %get-tuple-element.614), channel_id=1, source_target_pairs={{1,0},{2,1},{3,2},{5,4},{6,5},{7,6},{9,8},{10,9},{11,10},{13,12},{... | collective-permute-start | bytes 786440 | tf_op jit(solution)/shard_map/ppermute | solution.py:12
  136.1 34.1 %collective-permute-start.11 = (f32[1,256,256]{2,1,0:T(8,128)S(1)}, f32[1,256,256]{2,1,0:T(8,128)S(1)}, u32[]{:S(2)}, u32[]{:S(2)}) collective-permute-start(f32[1,256,256]{2,1,0:T(8,128)S(1)} %get-tuple-element.619), channel_id=1, source_target_pairs={{1,0},{2,1},{3,2},{5,4},{6,5},{7,6},{9,8},{10,9},{11,10},{13,12},{... | collective-permute-start | bytes 786440 | tf_op jit(solution)/shard_map/ppermute | solution.py:12
  137.4 34.7 %collective-permute-start.12 = (f32[1,256,256]{2,1,0:T(8,128)S(1)}, f32[1,256,256]{2,1,0:T(8,128)S(1)}, u32[]{:S(2)}, u32[]{:S(2)}) collective-permute-start(f32[1,256,256]{2,1,0:T(8,128)S(1)} %get-tuple-element.620), channel_id=1, source_target_pairs={{1,0},{2,1},{3,2},{5,4},{6,5},{7,6},{9,8},{10,9},{11,10},{13,12},{... | collective-permute-start | bytes 786440 | tf_op jit(solution)/shard_map/ppermute | solution.py:12
  193.2 46.5 %copy-start = (f32[1,2,512,1024]{3,2,1,0:T(8,128)S(1)}, f32[1,2,512,1024]{3,2,1,0:T(8,128)}, u32[]{:S(2)}) copy-start(f32[1,2,512,1024]{3,2,1,0:T(8,128)} %dynamic_update_slice.4) | copy-start | bytes 12582916
  195.1 44.6 %collective-permute-start.13 = (f32[1,2,256,1024]{3,2,1,0:T(8,128)S(1)}, f32[1,2,256,1024]{3,2,1,0:T(8,128)S(1)}, u32[]{:S(2)}, u32[]{:S(2)}) collective-permute-start(f32[1,2,256,1024]{3,2,1,0:T(8,128)S(1)} %slice.48), channel_id=1, source_target_pairs={{0,4},{4,8},{8,12},{12,16},{16,20},{20,24},{24,28},{1,5},{5,9},{9,... | collective-permute-start | bytes 6291464 | tf_op jit(solution)/shard_map/ppermute | solution.py:12
where the time goes:
time: 245 us; the launch traced here: 242 us
  waiting for transfers between devices  135 us (55%)
  starting transfers between devices  49.3 us (20%)
  matrix products  20 us (8%)
  local copies, waits for them, and re-layouts  16.4 us (7%)
  loops' own time  13.9 us (6%)
  other arithmetic  5.2 us (2%)
    ppermute x14, waiting for transfers between devices, shifted(): return lax.ppermute(value, axis, pairs)  135 us
    ppermute x14, starting transfers between devices, shifted(): return lax.ppermute(value, axis, pairs)  49.3 us
    dot_general x16, matrix products, right(): return jnp.einsum('bjk,kl->bjl', block, matrix, precision=precise)  10.5 us
    dot_general x16, matrix products, left(): return jnp.einsum('jk,bkl->bjl', matrix, block, precision=precise)  9.56 us
    dynamic_update_slice x1, local copies, waits for them, and re-layouts, add_patch(): return lax.dynamic_update_slice(totals, current + piece, corner)  6.68 us
    another operation x4, loops' own time, per_device(): lax.cond(cut_index == section, lambda values: backward_group(values[0], v...  6.6 us
    another operation x1, loops' own time, per_device(): lax.cond(cut_index == final_section, lambda values: far_field(values[0],...  6.22 us
  transfers between devices with their start and end apart: 14, of which 11 were waited for; matrix products, arithmetic and copies ran while one was open for 2% of the time, Pallas kernels for 0%

commit v1 on v0

v1 whole, which is shorter than its diff:
```python
import jax
import jax.numpy as jnp
import ml_dtypes
import numpy as np
from jax import lax
from jax.experimental import pallas as pl
from jax.experimental.pallas import tpu as pltpu
from jax.sharding import PartitionSpec as P

f32, bf16 = jnp.float32, jnp.bfloat16
LANE = 128
VMEM = pl.BlockSpec(memory_space=pltpu.VMEM)
SMEM = pl.BlockSpec(memory_space=pltpu.SMEM)
ANY = pl.BlockSpec(memory_space=pl.ANY)
PARAMS = pltpu.CompilerParams(vmem_limit_bytes=48 << 20)


def dft_tables(n):
    half = n // 2
    k = np.arange(half)[:, None]
    m = np.arange(half)[None, :]

    def real_form(odd):
        angle = -2 * np.pi * ((k * (2 * m + odd)) % n) / n
        c, s = np.cos(angle) / np.sqrt(n), np.sin(angle) / np.sqrt(n)
        return np.block([[c, s], [-s, c]])

    def parts(matrix, axis):
        high = matrix.astype(np.float32).astype(ml_dtypes.bfloat16)
        low = (matrix - high.astype(np.float64)).astype(np.float32).astype(ml_dtypes.bfloat16)
        return np.concatenate([high, high, low], axis=axis)

    even, odd = real_form(0), real_form(1)
    right_fwd = np.stack([parts(even, 0), parts(odd, 0)])
    left_fwd = np.stack([parts(even.T, 1), parts(odd.T, 1)])
    left_inv = np.stack([parts(even, 1), parts(odd, 1)])
    right_inv = np.stack([parts(even.T, 0), parts(odd.T, 0)])
    return right_fwd, left_fwd, left_inv, right_inv


def split(x, axis):
    high = x.astype(bf16)
    low = (x - high.astype(f32)).astype(bf16)
    return jnp.concatenate([high, low, high], axis=axis)


def right_dot(x, table):
    return jnp.dot(split(x, 1), table, preferred_element_type=f32)


def left_dot(table, x):
    return jnp.dot(table, split(x, 0), preferred_element_type=f32)


def to_rows(a, b):
    h = a.shape[0] // 2

    def one(r):
        re = jnp.concatenate([a[r : r + h, :h], b[r : r + h, :h]], 1)
        im = jnp.concatenate([a[r : r + h, h:], b[r : r + h, h:]], 1)
        return jnp.concatenate([re, im], 0)

    return one(0), one(h)


def to_columns(a, b):
    h = a.shape[0] // 2

    def one(c):
        top = jnp.concatenate([a[:h, c : c + h], a[h:, c : c + h]], 1)
        bottom = jnp.concatenate([b[:h, c : c + h], b[h:, c : c + h]], 1)
        return jnp.concatenate([top, bottom], 0)

    return one(0), one(h)


def columns_of(re, im):
    h = re.shape[1] // 2
    return (
        jnp.concatenate([re[:, :h], im[:, :h]], 1),
        jnp.concatenate([re[:, h:], im[:, h:]], 1),
    )


def planes_of(a, b):
    h = a.shape[1] // 2
    return (
        jnp.concatenate([a[:, :h], b[:, :h]], 1),
        jnp.concatenate([a[:, h:], b[:, h:]], 1),
    )


def forward(re, im, right, left):
    a, b = columns_of(re, im)
    a, b = to_rows(right_dot(a + b, right[0]), right_dot(a - b, right[1]))
    return left_dot(left[0], a + b), left_dot(left[1], a - b)


def inverse(a, b, left, right):
    p, q = left_dot(left[0], a), left_dot(left[1], b)
    a, b = to_columns(p + q, p - q)
    p, q = right_dot(a, right[0]), right_dot(b, right[1])
    return planes_of(p + q, p - q)


def times(ar, ai, br, bi):
    return ar * br - ai * bi, ar * bi + ai * br


def conj_times(ar, ai, br, bi):
    return ar * br + ai * bi, ar * bi - ai * br


def by_phase(a, b, cosine, sine):
    h = a.shape[0] // 2
    out = []
    for i, x in enumerate((a, b)):
        at = slice(i * h, (i + 1) * h)
        re, im = times(x[:h], x[h:], cosine[at], sine[at])
        out.append(jnp.concatenate([re, im], 0))
    return out


def by_residual(a, b, observed):
    h = a.shape[0] // 2
    out = []
    for i, x in enumerate((a, b)):
        re, im = x[:h], x[h:]
        residual = re * re + im * im - observed[i * h : (i + 1) * h]
        out.append(jnp.concatenate([residual * re, residual * im], 0))
    return out


def chain(cut, patches, probe, cosine, sine, observed, tables):
    n = probe.shape[1]
    sections = len(patches)

    def kernel(cut_ref, *refs):
        sources = refs[:sections]
        probe, cosine, sine, observed, rf, lf, li, ri, out, patch, waves, sems = refs[sections:]
        me = cut_ref[0]

        def fetch(i):
            to = me ^ i
            return pltpu.make_async_copy(sources[i], patch.at[to], sems.at[to])

        for i in range(sections):
            fetch(i).start()

        def wave(s):
            return (probe[0], probe[1]) if s == 0 else (waves[s - 1, 0], waves[s - 1, 1])

        for s in range(sections):
            pltpu.make_async_copy(sources[0], patch.at[s], sems.at[s]).wait()
            re, im = times(*wave(s), patch[s, 0], patch[s, 1])
            a, b = forward(re, im, rf, lf)
            if s < sections - 1:
                a, b = by_phase(a, b, cosine[...], sine[...])
                re, im = inverse(a, b, li, ri)
                waves[s, 0] = re
                waves[s, 1] = im
        a, b = by_residual(a, b, observed)
        re, im = inverse(a, b, li, ri)
        for s in range(sections - 1, -1, -1):

            @pl.when(me == s)
            def _(s=s, re=re, im=im):
                out[0], out[1] = conj_times(*wave(s), re, im)

            if s > 0:
                re, im = conj_times(patch[s, 0], patch[s, 1], re, im)
                a, b = forward(re, im, rf, lf)
                a, b = by_phase(a, b, cosine[...], -sine[...])
                re, im = inverse(a, b, li, ri)

    return pl.pallas_call(
        kernel,
        out_shape=jax.ShapeDtypeStruct((2, n, n), f32),
        in_specs=[SMEM] + [ANY] * sections + [VMEM] * 8,
        out_specs=VMEM,
        scratch_shapes=[
            pltpu.VMEM((sections, 2, n, n), f32),
            pltpu.VMEM((sections - 1, 2, n, n), f32),
            pltpu.SemaphoreType.DMA((sections,)),
        ],
        compiler_params=PARAMS,
    )(cut, *patches, probe, cosine, sine, observed, *tables)


def window_start(column, width, columns):
    start = jnp.minimum(column // LANE * LANE, columns - width - LANE)
    return pl.multiple_of(start, LANE), column - start


def cut_window(offsets, strip, width):
    _, _, rows, columns = strip.shape

    def kernel(offsets, strip, out, wide, sem):
        row, column = offsets[0], offsets[1]
        start, shift = window_start(column, width, columns)
        copy = pltpu.make_async_copy(strip.at[0, :, :, pl.ds(start, width + LANE)], wide, sem)
        copy.start()
        copy.wait()
        for c in range(2):
            x = pltpu.roll(wide[c], lax.rem(width + LANE - shift, width + LANE), 1)[:, :width]
            out[c] = pltpu.roll(x, lax.rem(rows - row, rows), 0)

    return pl.pallas_call(
        kernel,
        out_shape=jax.ShapeDtypeStruct((2, rows, width), f32),
        in_specs=[SMEM, ANY],
        out_specs=VMEM,
        scratch_shapes=[pltpu.VMEM((2, rows, width + LANE), f32), pltpu.SemaphoreType.DMA],
        compiler_params=PARAMS,
    )(offsets, strip)


def place(own_offsets, came_offsets, own, came, columns):
    _, rows, width = own.shape

    def kernel(own_offsets, came_offsets, own, came, out):
        index = lax.broadcasted_iota(jnp.int32, (rows, width), 0)
        out[...] = jnp.zeros_like(out)
        for offsets, piece, is_own in ((own_offsets, own, True), (came_offsets, came, False)):
            row, column = offsets[0], offsets[1]
            start, shift = window_start(column, width, columns)
            keep = index >= row if is_own else index < row
            for c in range(2):
                x = jnp.where(keep, pltpu.roll(piece[c], row, 0), 0.0)
                x = jnp.concatenate([x, jnp.zeros((rows, LANE), f32)], 1)
                at = (0, c, slice(None), pl.ds(start, width + LANE))
                out[at] = out[at] + pltpu.roll(x, shift, 1)

    return pl.pallas_call(
        kernel,
        out_shape=jax.ShapeDtypeStruct((1, 2, rows, columns), f32),
        in_specs=[SMEM, SMEM, VMEM, VMEM],
        out_specs=VMEM,
        compiler_params=PARAMS,
    )(own_offsets, came_offsets, own, came)


def shifted(value, by):
    devices = lax.axis_size("tile")
    pairs = [(i, i + by) for i in range(devices) if 0 <= i + by < devices]
    return lax.ppermute(value, "tile", pairs)


def swapped(value, bit):
    devices = lax.axis_size("cuts")
    return lax.ppermute(value, "cuts", [(i, i ^ bit) for i in range(devices)])


def by_parity(x):
    n = x.shape[-1]
    return x.reshape(n // 2, 2, n // 2, 2).transpose(1, 0, 3, 2).reshape(n, n)


def per_device(transmission, probe, prop_phase, row_off, col_off, measured):
    columns = transmission.shape[3]
    width = probe.shape[1]
    offsets = jnp.concatenate([row_off, col_off])
    came_offsets = shifted(offsets, 1)
    own = cut_window(offsets, transmission, width)
    tables = [jnp.asarray(t) for t in dft_tables(width)]
    phase = by_parity(prop_phase)
    cosine, sine = jnp.cos(phase), jnp.sin(phase)
    observed = by_parity(measured[0])
    band = shifted(cut_window(came_offsets, transmission, width), -1)
    index = lax.broadcasted_iota(jnp.int32, own.shape, 1)
    patch = jnp.where(index < own.shape[1] - row_off[0], own, band)
    across = swapped(patch, 2)
    patches = [patch, swapped(patch, 1), across, swapped(across, 1)]
    cut = lax.axis_index("cuts").astype(jnp.int32).reshape(1)
    piece = chain(cut, patches, probe, cosine, sine, observed, tables)
    came = shifted(piece, 1)
    return place(offsets, came_offsets, piece, came, columns)


def solution(mesh):
    placed = (P("cuts", None, "tile", None), P(), P(), P("tile"), P("tile"), P("tile", None, None))
    return jax.shard_map(
        per_device,
        mesh=mesh,
        in_specs=placed,
        out_specs=P("cuts", None, "tile", None),
        check_vma=False,
    )
```

time: 245 us -> 158 us (0.64)
  waiting for transfers between devices: 135 us -> 34.4 us
  local copies, waits for them, and re-layouts: 16.4 us -> 90.7 us
  starting transfers between devices: 49.3 us -> 12 us
  matrix products: 20 us -> 0 us
  Pallas kernels: 0 us -> 17.5 us
  loops' own time: 13.9 us -> 0 us
  other arithmetic: 5.2 us -> 0.19 us
    ppermute x14 -> x6, waiting for transfers between devices: 135 us -> 34.4 us  [the longest x3 24.1 us: shifted(): return lax.ppermute(value, 'tile', pairs)]
    ppermute x14 -> x6, starting transfers between devices: 49.3 us -> 12 us  [the longest x3 10.4 us: shifted(): return lax.ppermute(value, 'tile', pairs)]
    cos x0 -> x2, local copies, waits for them, and re-layouts: none -> 27.9 us  [per_device(): cosine, sine = (jnp.cos(phase), jnp.sin(phase))]
    sin x1 -> x3, local copies, waits for them, and re-layouts: 1.86 us -> 29.7 us  [per_device(): cosine, sine = (jnp.cos(phase), jnp.sin(phase))]
    dot_general x32 -> x0, matrix products: 20 us -> none  [the longest x16 10.5 us: right(): return jnp.einsum('bjk,kl->bjl', block, matrix, precision=precise)]
    another operation x2 -> x1, local copies, waits for them, and re-layouts: 0.04 us -> 18 us  [by_parity(): return x.reshape(n // 2, 2, n // 2, 2).transpose(1, 0, 3, 2).reshape(n, n)]
    pallas_call x0 -> x4, Pallas kernels: none -> 17.5 us  [the longest x1 12.6 us: chain(): pl.pallas_call(kernel, out_shape=jax.ShapeDtypeStruct((2, n, n), f32), in...]
    another operation x9 -> x0, loops' own time: 13.9 us -> none  [the longest x4 6.6 us: per_device(): lax.cond(cut_index == section, lambda values: backward_group(values[0], v...]
  transfers between devices with their start and end apart: 14 -> 6, of which waited for: 11 -> 4; matrix products, arithmetic and copies ran while one was open for 2% -> 56% of each run, Pallas kernels for 0% -> 1%
where the time goes in v1:
time: 158 us; the launch traced here: 156 us
  local copies, waits for them, and re-layouts  90.7 us (57%)
  waiting for transfers between devices  34.4 us (22%)
  Pallas kernels  17.5 us (11%)
  starting transfers between devices  12 us (8%)
    sin x3, local copies, waits for them, and re-layouts, per_device(): cosine, sine = (jnp.cos(phase), jnp.sin(phase))  29.7 us
    cos x2, local copies, waits for them, and re-layouts, per_device(): cosine, sine = (jnp.cos(phase), jnp.sin(phase))  27.9 us
    ppermute x3, waiting for transfers between devices, shifted(): return lax.ppermute(value, 'tile', pairs)  24.1 us
    another operation x1, local copies, waits for them, and re-layouts, by_parity(): return x.reshape(n // 2, 2, n // 2, 2).transpose(1, 0, 3, 2).reshape(n, n)  18 us
    pallas_call x1, Pallas kernels, chain(): pl.pallas_call(kernel, out_shape=jax.ShapeDtypeStruct((2, n, n), f32), in...  12.6 us
    ppermute x3, starting transfers between devices, shifted(): return lax.ppermute(value, 'tile', pairs)  10.4 us
    ppermute x3, waiting for transfers between devices, swapped(): return lax.ppermute(value, 'cuts', [(i, i ^ bit) for i in range(devices)])  10.4 us
    transpose x1, local copies, waits for them, and re-layouts, by_parity(): return x.reshape(n // 2, 2, n // 2, 2).transpose(1, 0, 3, 2).reshape(n, n)  9.79 us
  transfers between devices with their start and end apart: 6, of which 4 were waited for; matrix products, arithmetic and copies ran while one was open for 56% of the time, Pallas kernels for 1%

profile of v1, /device:TPU:0, one launch (start us, length us, event | category | flops | bytes accessed | tf_op | source)
XLA Modules:
  0.0 156.2 jit_solution(7160435412316976308)
XLA Ops:
  1.3 0.1 pad_add_fusion.offsets.own_offsets
  1.4 4.9 %collective-permute-start = (s32[2]{0:T(128)S(1)}, s32[2]{0:T(128)S(1)}, u32[]{:S(2)}, u32[]{:S(2)}) collective-permute-start(s32[2]{0:T(128)S(1)} %pad_add_fusion.offsets.own_offsets), channel_id=1, source_target_pairs={{0,4},{4,8},{8,12},{12,16},{16,20},{20,24},{24,28},{1,5},{5,9},{9,... | collective-permute-start | bytes 32 | tf_op jit(solution)/shard_map/ppermute | solution.py:246
  6.2 1.3 collective-permute-done.offsets.came_offsets
  7.5 1.6 %copy-done = f32[1,2,256,1024]{3,2,1,0:T(8,128)S(1)} copy-done((f32[1,2,256,1024]{3,2,1,0:T(8,128)S(1)}, f32[1,2,256,1024]{3,2,1,0:T(8,128)}, u32[]{:S(2)}) %copy-start) | copy-done | bytes 2097176
  9.1 1.0 shard_map.101
  10.2 1.3 collective-permute-start.1
  11.5 0.0 copy-start.1
  11.5 1.6 %copy-done.1 = f32[1,2,256,1024]{3,2,1,0:T(8,128)S(1)} copy-done((f32[1,2,256,1024]{3,2,1,0:T(8,128)S(1)}, f32[1,2,256,1024]{3,2,1,0:T(8,128)}, u32[]{:S(2)}) %copy-start.1) | copy-done | bytes 2097176
  13.1 1.0 shard_map.100
  14.1 11.0 %collective-permute-done.1 = f32[2,256,256]{2,1,0:T(8,128)S(1)} collective-permute-done((f32[2,256,256]{2,1,0:T(8,128)S(1)}, f32[2,256,256]{2,1,0:T(8,128)S(1)}, u32[]{:S(2)}, u32[]{:S(2)}) %collective-permute-start.1) | collective-permute-done | bytes 524320 | tf_op jit(solution)/shard_map/ppermute | solution.py:246
  25.1 0.1 broadcast_select_fusion.refs_0_
  25.2 1.6 collective-permute-start.3
  26.8 0.0 collective-permute-start.2
  26.8 10.4 %collective-permute-done.3.refs_2_ = f32[2,256,256]{2,1,0:T(8,128)S(1)} collective-permute-done((f32[2,256,256]{2,1,0:T(8,128)S(1)}, f32[2,256,256]{2,1,0:T(8,128)S(1)}, u32[]{:S(2)}, u32[]{:S(2)}) %collective-permute-start.3) | collective-permute-done | bytes 524320 | tf_op jit(solution)/shard_map/ppermute | solution.py:251
  37.1 0.0 collective-permute-start.4
  37.1 1.9 %fusion = (f32[256,256]{1,0:T(8,128)S(1)}, f32[256,256]{1,0:T(8,128)S(1)}) fusion(f32[256,256]{1,0:T(8,128)} %param.12), kind=kLoop, calls=%fused_computation.6 | loop fusion | bytes 786432 | tf_op jit(solution)/shard_map/sin | solution.py:267
  39.0 0.0 copy-start.5
  39.0 18.1 %sin.10 = f32[128,2,128,2]{3,2,1,0:T(8,128)} reshape(f32[256,256]{1,0:T(8,128)S(1)} %get-tuple-element.5) | data formatting | bytes 524288 | tf_op jit(solution)/shard_map/sin | solution.py:267
  57.1 9.8 %copy.15 = f32[2,128,2,128]{3,2,1,0:T(2,128)} copy(f32[2,128,2,128]{2,3,0,1:T(8,128)} %bitcast.19) | data formatting | bytes 524288 | tf_op jit(solution)/shard_map/sin | solution.py:267
  66.9 0.0 copy-done.5
  66.9 18.0 %reshape_squeeze.3 = f32[128,2,128,2]{3,2,1,0:T(8,128)} reshape(f32[1,256,256]{2,1,0:T(8,128)S(1)} %copy-done.5) | data formatting | bytes 524288 | tf_op jit(solution)/shard_map/reshape;squeeze | solution.py:256
  84.9 9.8 %copy.16 = f32[2,128,2,128]{3,2,1,0:T(2,128)} copy(f32[2,128,2,128]{2,3,0,1:T(8,128)} %bitcast.21) | data formatting | bytes 524288 | tf_op jit(solution)/shard_map/transpose | solution.py:256
  94.7 18.1 %cos.10 = f32[128,2,128,2]{3,2,1,0:T(8,128)} reshape(f32[256,256]{1,0:T(8,128)S(1)} %get-tuple-element.6) | data formatting | bytes 524288 | tf_op jit(solution)/shard_map/cos | solution.py:267
  112.8 9.8 %copy.14 = f32[2,128,2,128]{3,2,1,0:T(2,128)} copy(f32[2,128,2,128]{2,3,0,1:T(8,128)} %bitcast.20) | data formatting | bytes 524288 | tf_op jit(solution)/shard_map/cos | solution.py:267
  122.6 1.0 copy.23
  123.6 1.1 copy_bitcast_fusion
  124.6 0.0 collective-permute-done.2.refs_1_
  124.7 0.0 collective-permute-done.4.refs_3_
  124.7 12.6 %shard_map.102.own = f32[2,256,256]{2,1,0:T(8,128)S(1)} custom-call(s32[1]{0:T(128)} %bitcast.cut_ref, f32[2,256,256]{2,1,0:T(8,128)S(1)} %broadcast_select_fusion.refs_0_, f32[2,256,256]{2,1,0:T(8,128)} %collective-permute-done.2.refs_1_, f32[2,256,256]{2,1,0:T(8,128)S(1)} %collective-permute-done.3.refs_2_, f32[2,256,256]{2,1,0:T(8,128)} %collective-permute-done.4.refs_3_, ...), custom_call_target="tpu_custom_call" | custom-call | tf_op jit(solution)/shard_map/pallas_call | solution.py:176
  137.3 4.3 %collective-permute-start.5 = (f32[2,256,256]{2,1,0:T(8,128)S(1)}, f32[2,256,256]{2,1,0:T(8,128)S(1)}, u32[]{:S(2)}, u32[]{:S(2)}) collective-permute-start(f32[2,256,256]{2,1,0:T(8,128)S(1)} %shard_map.102.own), channel_id=1, source_target_pairs={{0,4},{4,8},{8,12},{12,16},{16,20},{20,24},{24,28},{1,5},{5,9},{9,... | collective-permute-start | bytes 1572872 | tf_op jit(solution)/shard_map/ppermute | solution.py:246
  141.6 11.8 %collective-permute-done.5.came = f32[2,256,256]{2,1,0:T(8,128)S(1)} collective-permute-done((f32[2,256,256]{2,1,0:T(8,128)S(1)}, f32[2,256,256]{2,1,0:T(8,128)S(1)}, u32[]{:S(2)}, u32[]{:S(2)}) %collective-permute-start.5) | collective-permute-done | bytes 524320 | tf_op jit(solution)/shard_map/ppermute | solution.py:246
  153.4 2.8 %shard_map.103 = f32[1,2,256,1024]{3,2,1,0:T(8,128)} custom-call(s32[2]{0:T(128)S(1)} %pad_add_fusion.offsets.own_offsets, s32[2]{0:T(128)S(1)} %collective-permute-done.offsets.came_offsets, f32[2,256,256]{2,1,0:T(8,128)S(1)} %shard_map.102.own, f32[2,256,256]{2,1,0:T(8,128)S(1)} %collective-permute-done.5.came), custom_call_target="tpu_custom_call" | custom-call | tf_op jit(solution)/shard_map/pallas_call | solution.py:234
  (8 shorter events, 0.0 us)
Async XLA Ops:
  1.4 6.1 %collective-permute-start = (s32[2]{0:T(128)S(1)}, s32[2]{0:T(128)S(1)}, u32[]{:S(2)}, u32[]{:S(2)}) collective-permute-start(s32[2]{0:T(128)S(1)} %pad_add_fusion.offsets.own_offsets), channel_id=1, source_target_pairs={{0,4},{4,8},{8,12},{12,16},{16,20},{20,24},{24,28},{1,5},{5,9},{9,... | collective-permute-start | bytes 32 | tf_op jit(solution)/shard_map/ppermute | solution.py:246
  7.5 1.6 %copy-start = (f32[1,2,256,1024]{3,2,1,0:T(8,128)S(1)}, f32[1,2,256,1024]{3,2,1,0:T(8,128)}, u32[]{:S(2)}) copy-start(f32[1,2,256,1024]{3,2,1,0:T(8,128)} %strip.3) | copy-start | bytes 6291460
  10.2 14.9 %collective-permute-start.1 = (f32[2,256,256]{2,1,0:T(8,128)S(1)}, f32[2,256,256]{2,1,0:T(8,128)S(1)}, u32[]{:S(2)}, u32[]{:S(2)}) collective-permute-start(f32[2,256,256]{2,1,0:T(8,128)S(1)} %shard_map.101), channel_id=1, source_target_pairs={{4,0},{8,4},{12,8},{16,12},{20,16},{24,20},{28,24},{5,1},{9,5},{13... | collective-permute-start | bytes 1572872 | tf_op jit(solution)/shard_map/ppermute | solution.py:246
  11.5 1.6 %copy-start.1 = (f32[1,2,256,1024]{3,2,1,0:T(8,128)S(1)}, f32[1,2,256,1024]{3,2,1,0:T(8,128)}, u32[]{:S(2)}) copy-start(f32[1,2,256,1024]{3,2,1,0:T(8,128)} %strip.3) | copy-start | bytes 6291460
  25.2 11.9 %collective-permute-start.3 = (f32[2,256,256]{2,1,0:T(8,128)S(1)}, f32[2,256,256]{2,1,0:T(8,128)S(1)}, u32[]{:S(2)}, u32[]{:S(2)}) collective-permute-start(f32[2,256,256]{2,1,0:T(8,128)S(1)} %broadcast_select_fusion.refs_0_), channel_id=1, source_target_pairs={{0,2},{1,3},{2,0},{3,1},{4,6},{5,7},{6,4},{7,5},{8,10},{9,11},{10,... | collective-permute-start | bytes 1572872 | tf_op jit(solution)/shard_map/ppermute | solution.py:251
  26.8 97.9 %collective-permute-start.2 = (f32[2,256,256]{2,1,0:T(8,128)S(1)}, f32[2,256,256]{2,1,0:T(8,128)}, u32[]{:S(2)}, u32[]{:S(2)}) collective-permute-start(f32[2,256,256]{2,1,0:T(8,128)S(1)} %broadcast_select_fusion.refs_0_), channel_id=1, source_target_pairs={{0,1},{1,0},{2,3},{3,2},{4,5},{5,4},{6,7},{7,6},{8,9},{9,8},{10,11... | collective-permute-start | bytes 1572872 | tf_op jit(solution)/shard_map/ppermute | solution.py:251
  37.1 87.5 %collective-permute-start.4 = (f32[2,256,256]{2,1,0:T(8,128)S(1)}, f32[2,256,256]{2,1,0:T(8,128)}, u32[]{:S(2)}, u32[]{:S(2)}) collective-permute-start(f32[2,256,256]{2,1,0:T(8,128)S(1)} %collective-permute-done.3.refs_2_), channel_id=1, source_target_pairs={{0,1},{1,0},{2,3},{3,2},{4,5},{5,4},{6,7},{7,6},{8,9},{9,8},{10,11... | collective-permute-start | bytes 1572872 | tf_op jit(solution)/shard_map/ppermute | solution.py:251
  39.0 27.9 %copy-start.5 = (f32[1,256,256]{2,1,0:T(8,128)S(1)}, f32[1,256,256]{2,1,0:T(8,128)}, u32[]{:S(2)}) copy-start(f32[1,256,256]{2,1,0:T(8,128)} %param.15) | copy-start | bytes 786436
  94.7 29.9 %copy-start.2 = (bf16[2,768,256]{2,1,0:T(8,128)(2,1)S(1)}, bf16[2,768,256]{2,1,0:T(8,128)(2,1)}, u32[]{:S(2)}) copy-start(bf16[2,768,256]{2,1,0:T(8,128)(2,1)} %constant.15.clone.refs_8_) | copy-start | bytes 2359300
  94.7 29.9 %copy-start.3 = (bf16[2,256,768]{2,1,0:T(8,128)(2,1)S(1)}, bf16[2,256,768]{2,1,0:T(8,128)(2,1)}, u32[]{:S(2)}) copy-start(bf16[2,256,768]{2,1,0:T(8,128)(2,1)} %constant.16.clone.refs_9_) | copy-start | bytes 2359300
  94.7 30.0 %copy-start.4 = (f32[2,256,256]{2,1,0:T(8,128)S(1)}, f32[2,256,256]{2,1,0:T(8,128)}, u32[]{:S(2)}) copy-start(f32[2,256,256]{2,1,0:T(8,128)} %refs_4_.1) | copy-start | bytes 1572868
  137.3 16.1 %collective-permute-start.5 = (f32[2,256,256]{2,1,0:T(8,128)S(1)}, f32[2,256,256]{2,1,0:T(8,128)S(1)}, u32[]{:S(2)}, u32[]{:S(2)}) collective-permute-start(f32[2,256,256]{2,1,0:T(8,128)S(1)} %shard_map.102.own), channel_id=1, source_target_pairs={{0,4},{4,8},{8,12},{12,16},{16,20},{20,24},{24,28},{1,5},{5,9},{9,... | collective-permute-start | bytes 1572872 | tf_op jit(solution)/shard_map/ppermute | solution.py:246

commit v2 on v1

v2 whole, which is shorter than its diff:
```python
import jax
import jax.numpy as jnp
import numpy as np
from jax import lax
from jax.experimental import pallas as pl
from jax.experimental.pallas import tpu as pltpu
from jax.sharding import PartitionSpec as P

f32, bf16 = jnp.float32, jnp.bfloat16
LANE = 128
VMEM = pl.BlockSpec(memory_space=pltpu.VMEM)
SMEM = pl.BlockSpec(memory_space=pltpu.SMEM)
ANY = pl.BlockSpec(memory_space=pl.ANY)
HBM = pl.BlockSpec(memory_space=pltpu.HBM)
SHORT = pl.CostEstimate(flops=1 << 16, bytes_accessed=1 << 12, transcendentals=0)
PARAMS = pltpu.CompilerParams(vmem_limit_bytes=12 << 20)


def dft_tables(n):
    half = n // 2
    k = np.arange(half)[:, None]
    m = np.arange(half)[None, :]

    def real_form(odd):
        angle = -2 * np.pi * ((k * (2 * m + odd)) % n) / n
        c, s = np.cos(angle) / np.sqrt(n), np.sin(angle) / np.sqrt(n)
        return np.block([[c, s], [-s, c]])

    def parts(matrix, axis):
        high = matrix.astype(np.float32).astype(jnp.bfloat16)
        low = (matrix - high.astype(np.float64)).astype(np.float32).astype(jnp.bfloat16)
        return np.concatenate([high, high, low], axis=axis)

    even, odd = real_form(0), real_form(1)
    right = np.stack([parts(m, 0) for m in (even, odd, even.T, odd.T)])
    left = np.stack([parts(m, 1) for m in (even.T, odd.T, even, odd)])
    return right, left


def pinned(x):
    return pltpu.with_memory_space_constraint(x, pltpu.HBM)


def split(x, axis):
    high = x.astype(bf16)
    low = (x - high.astype(f32)).astype(bf16)
    return jnp.concatenate([high, low, high], axis=axis)


def right_dot(x, table):
    return jnp.dot(split(x, 1), table, preferred_element_type=f32)


def left_dot(table, x):
    return jnp.dot(table, split(x, 0), preferred_element_type=f32)


def to_rows(a, b):
    h = a.shape[0] // 2

    def one(r):
        re = jnp.concatenate([a[r : r + h, :h], b[r : r + h, :h]], 1)
        im = jnp.concatenate([a[r : r + h, h:], b[r : r + h, h:]], 1)
        return jnp.concatenate([re, im], 0)

    return one(0), one(h)


def to_columns(a, b):
    h = a.shape[0] // 2

    def one(c):
        top = jnp.concatenate([a[:h, c : c + h], a[h:, c : c + h]], 1)
        bottom = jnp.concatenate([b[:h, c : c + h], b[h:, c : c + h]], 1)
        return jnp.concatenate([top, bottom], 0)

    return one(0), one(h)


def columns_of(re, im):
    h = re.shape[1] // 2
    return (
        jnp.concatenate([re[:, :h], im[:, :h]], 1),
        jnp.concatenate([re[:, h:], im[:, h:]], 1),
    )


def planes_of(a, b):
    h = a.shape[1] // 2
    return (
        jnp.concatenate([a[:, :h], b[:, :h]], 1),
        jnp.concatenate([a[:, h:], b[:, h:]], 1),
    )


def forward(re, im, tables):
    right, left = tables
    a, b = columns_of(re, im)
    a, b = to_rows(right_dot(a + b, right[0]), right_dot(a - b, right[1]))
    return left_dot(left[0], a + b), left_dot(left[1], a - b)


def inverse(a, b, tables):
    right, left = tables
    p, q = left_dot(left[2], a), left_dot(left[3], b)
    a, b = to_columns(p + q, p - q)
    p, q = right_dot(a, right[2]), right_dot(b, right[3])
    return planes_of(p + q, p - q)


def times(ar, ai, br, bi):
    return ar * br - ai * bi, ar * bi + ai * br


def conj_times(ar, ai, br, bi):
    return ar * br + ai * bi, ar * bi - ai * br


def by_phase(a, b, cosine, sine):
    h = a.shape[0] // 2
    out = []
    for i, x in enumerate((a, b)):
        at = slice(i * h, (i + 1) * h)
        re, im = times(x[:h], x[h:], cosine[at], sine[at])
        out.append(jnp.concatenate([re, im], 0))
    return out


def by_residual(a, b, observed):
    h = a.shape[0] // 2
    out = []
    for i, x in enumerate((a, b)):
        re, im = x[:h], x[h:]
        residual = re * re + im * im - observed[i * h : (i + 1) * h]
        out.append(jnp.concatenate([residual * re, residual * im], 0))
    return out


def prepare(prop_phase, *patterns):
    n = prop_phase.shape[0]

    def kernel(phase, *refs):
        observed, outs, (held, sem) = refs[: len(patterns)], refs[len(patterns) : -2], refs[-2:]
        row = lax.broadcasted_iota(jnp.int32, (n, n), 0)
        column = lax.broadcasted_iota(jnp.int32, (n, n), 1)
        half = n // 2
        from_row = jnp.where(row < half, 2 * row, 2 * (row - half) + 1)
        from_column = jnp.where(column < half, 2 * column, 2 * (column - half) + 1)
        left = jnp.where(column == from_row, 1.0, 0.0).astype(bf16)
        right = jnp.where(row == from_column, 1.0, 0.0).astype(bf16)

        def reorder(x):
            for side in (0, 1):
                total = None
                for _ in range(3):
                    part = x.astype(bf16)
                    x = x - part.astype(f32)
                    pair = (left, part) if side == 0 else (part, right)
                    moved = jnp.dot(*pair, preferred_element_type=f32)
                    total = moved if total is None else total + moved
                x = total
            return x

        angle = reorder(phase[...])
        copies = [pltpu.make_async_copy(held.at[i], out, sem.at[i]) for i, out in enumerate(outs)]
        values = [lambda: jnp.cos(angle), lambda: jnp.sin(angle)] + [lambda x=x: reorder(x[0]) for x in observed]
        for i, value in enumerate(values):
            held[i] = value()
            copies[i].start()
        for copy in copies:
            copy.wait()

    count = 2 + len(patterns)
    return pl.pallas_call(
        kernel,
        out_shape=[pltpu.HBM((n, n), f32)] * count,
        in_specs=[VMEM] * (1 + len(patterns)),
        out_specs=[ANY] * count,
        scratch_shapes=[pltpu.VMEM((count, n, n), f32), pltpu.SemaphoreType.DMA((count,))],
        compiler_params=PARAMS,
        cost_estimate=pl.CostEstimate(flops=36 * n**3, bytes_accessed=30 * n * n, transcendentals=2 * n * n),
    )(prop_phase, *patterns)


def run_forward(s, before, patch, after, cosine, sine, tables):
    re, im = times(before[0], before[1], patch[0], patch[1])
    a, b = forward(re, im, tables)
    a, b = by_phase(a, b, cosine[...], sine[...])
    re, im = inverse(a, b, tables)
    after[0] = re
    after[1] = im


def start_chunks(sources, patch, slot, sem):
    top = 0
    for source in sources:
        rows = source.shape[1]
        pltpu.make_async_copy(source, patch.at[slot, :, pl.ds(top, rows), :], sem).start()
        top += rows


def wait_slot(patch, slot, sem):
    pltpu.make_async_copy(patch.at[slot], patch.at[slot], sem).wait()


def fetch_patches(me, sources, patch, sems):
    for i, chunks in enumerate(sources):
        start_chunks(chunks, patch, me ^ i, sems.at[me ^ i])


def grouped(refs, patches, chunks):
    return [refs[i * chunks : (i + 1) * chunks] for i in range(patches)], refs[patches * chunks :]


def early_waves(cut, patches, probe, cosine, sine, tables):
    n = probe.shape[1]
    chunks = len(patches[0])

    def kernel(cut_ref, *refs):
        sources, rest = grouped(refs, 2, chunks)
        probe, cosine, sine, right, left, waves, patch, first, phase, sems, phase_sem = rest
        me = cut_ref[0]
        pairs = ((probe, first), (cosine, phase.at[0]), (sine, phase.at[1]))
        copies = [pltpu.make_async_copy(x, y, phase_sem.at[i]) for i, (x, y) in enumerate(pairs)]

        @pl.when(me < 2)
        def _():
            fetch_patches(me, sources, patch, sems)
            for copy in copies:
                copy.start()
            before = first
            for s in range(2):
                wait_slot(patch, s, sems.at[s])
                if s == 0:
                    for copy in copies:
                        copy.wait()
                run_forward(s, before, patch.at[s], waves.at[s], phase.at[0], phase.at[1], (right, left))
                before = waves.at[s]

    return pl.pallas_call(
        kernel,
        out_shape=jax.ShapeDtypeStruct((2, 2, n, n), f32),
        in_specs=[SMEM] + [ANY] * (2 * chunks + 3) + [VMEM] * 2,
        out_specs=VMEM,
        scratch_shapes=[
            pltpu.VMEM((2, 2, n, n), f32),
            pltpu.VMEM((2, n, n), f32),
            pltpu.VMEM((2, n, n), f32),
            pltpu.SemaphoreType.DMA((2,)),
            pltpu.SemaphoreType.DMA((3,)),
        ],
        compiler_params=PARAMS,
        cost_estimate=SHORT,
    )(cut, *flatten(patches[:2]), *map(pinned, (probe, cosine, sine)), *tables)


def flatten(patches):
    return [chunk for patch in patches for chunk in patch]


def chain(cut, patches, early, probe, cosine, sine, observed, tables):
    n = probe.shape[1]
    sections = len(patches)
    chunks = len(patches[0])
    planes_in = [cosine, sine, observed, probe, early]

    def kernel(cut_ref, *refs):
        sources, rest = grouped(refs, sections, chunks)
        *planes, right, left, out, patch, waves, held, probe, sems, early_sem, held_sem = rest
        me = cut_ref[0]
        tables = (right, left)
        targets = [held.at[0], held.at[1], held.at[2], probe]
        copies = [pltpu.make_async_copy(x, y, held_sem.at[i]) for i, (x, y) in enumerate(zip(planes, targets))]
        cosine, sine, observed = [held.at[i] for i in range(3)]

        def wave(s):
            return probe if s == 0 else waves.at[s - 1]

        def first_two():
            for s in range(2):
                run_forward(s, wave(s), patch.at[s], waves.at[s], cosine, sine, tables)

        def back(s, re, im):
            @pl.when(me == s)
            def _():
                out[0], out[1] = conj_times(wave(s)[0], wave(s)[1], re, im)

            if s > 0:

                @pl.when(me < s)
                def _():
                    gr, gi = conj_times(patch[s, 0], patch[s, 1], re, im)
                    a, b = forward(gr, gi, tables)
                    a, b = by_phase(a, b, cosine[...], -sine[...])
                    back(s - 1, *inverse(a, b, tables))

        early_copy = pltpu.make_async_copy(planes[4], waves.at[pl.ds(0, 2)], early_sem)

        @pl.when(me < 2)
        def _():
            early_copy.start()

        fetch_patches(me, sources, patch, sems)
        for copy in copies:
            copy.start()
        for s in range(2):
            wait_slot(patch, s, sems.at[s])
        for copy in (copies[0], copies[1], copies[3]):
            copy.wait()

        @pl.when(me < 2)
        def _():
            early_copy.wait()

        pl.when(me >= 2)(first_two)
        for s in range(2, sections):
            wait_slot(patch, s, sems.at[s])
            if s < sections - 1:
                run_forward(s, wave(s), patch.at[s], waves.at[s], cosine, sine, tables)
        copies[2].wait()
        last = sections - 1
        re, im = times(wave(last)[0], wave(last)[1], patch[last, 0], patch[last, 1])
        a, b = forward(re, im, tables)
        a, b = by_residual(a, b, observed[...])
        back(last, *inverse(a, b, tables))

    return pl.pallas_call(
        kernel,
        out_shape=jax.ShapeDtypeStruct((2, n, n), f32),
        in_specs=[SMEM] + [ANY] * (sections * chunks + len(planes_in)) + [VMEM] * 2,
        out_specs=VMEM,
        scratch_shapes=[
            pltpu.VMEM((sections, 2, n, n), f32),
            pltpu.VMEM((sections - 1, 2, n, n), f32),
            pltpu.VMEM((3, n, n), f32),
            pltpu.VMEM((2, n, n), f32),
            pltpu.SemaphoreType.DMA((sections,)),
            pltpu.SemaphoreType.DMA,
            pltpu.SemaphoreType.DMA((4,)),
        ],
        compiler_params=PARAMS,
        cost_estimate=pl.CostEstimate(flops=10 * 24 * n**3, bytes_accessed=16 * n * n, transcendentals=0),
    )(cut, *flatten(patches), *map(pinned, (cosine, sine, observed, probe)), early, *tables)


def window_start(column, width, columns):
    start = jnp.minimum(column // LANE * LANE, columns - width - LANE)
    return pl.multiple_of(start, LANE), column - start


def packed(row_off, col_off):
    def kernel(row_off, col_off, out):
        out[0] = row_off[0]
        out[1] = col_off[0]

    return pl.pallas_call(
        kernel,
        out_shape=jax.ShapeDtypeStruct((2,), jnp.int32),
        in_specs=[SMEM, SMEM],
        out_specs=SMEM,
        compiler_params=PARAMS,
    )(row_off, col_off)


def cut_window(offsets, strip, width, bounds):
    _, _, rows, columns = strip.shape
    chunks = len(bounds) - 1

    def kernel(offsets, strip, *refs):
        outs, (wide, sem) = refs[:chunks], refs[chunks:]
        row, column = offsets[0], offsets[1]
        start, shift = window_start(column, width, columns)
        run = pl.ds(start, width + LANE)
        copies = [pltpu.make_async_copy(strip.at[0, c, :, run], wide.at[c], sem.at[c]) for c in range(2)]
        for copy in copies:
            copy.start()
        for c in range(2):
            copies[c].wait()
            x = pltpu.roll(wide[c], lax.rem(width + LANE - shift, width + LANE), 1)[:, :width]
            x = pltpu.roll(x, lax.rem(rows - row, rows), 0)
            for j in range(chunks):
                outs[j][c] = x[bounds[j] : bounds[j + 1]]

    return pl.pallas_call(
        kernel,
        out_shape=[jax.ShapeDtypeStruct((2, bounds[j + 1] - bounds[j], width), f32) for j in range(chunks)],
        in_specs=[SMEM, ANY],
        out_specs=[VMEM] * chunks,
        scratch_shapes=[pltpu.VMEM((2, rows, width + LANE), f32), pltpu.SemaphoreType.DMA((2,))],
        compiler_params=PARAMS,
    )(offsets, pinned(strip))


def moved(piece, row, shift, keep):
    rows = piece.shape[0]
    x = jnp.where(keep, pltpu.roll(piece, row, 0), 0.0)
    return pltpu.roll(jnp.concatenate([x, jnp.zeros((rows, LANE), f32)], 1), shift, 1)


def place_own(offsets, piece, columns):
    _, rows, width = piece.shape

    def kernel(offsets, piece, out):
        index = lax.broadcasted_iota(jnp.int32, (rows, width), 0)
        out[...] = jnp.zeros_like(out)
        row = offsets[0]
        start, shift = window_start(offsets[1], width, columns)
        for c in range(2):
            out[0, c, :, pl.ds(start, width + LANE)] = moved(piece[c], row, shift, index >= row)

    return pl.pallas_call(
        kernel,
        out_shape=jax.ShapeDtypeStruct((1, 2, rows, columns), f32),
        in_specs=[SMEM, VMEM],
        out_specs=VMEM,
        compiler_params=PARAMS,
    )(offsets, piece)


def add_came(offsets, came, base):
    _, rows, width = came.shape
    columns = base.shape[3]

    def kernel(offsets, came, base, out, wide, sem):
        row = offsets[0]
        start, shift = window_start(offsets[1], width, columns)
        run = pl.ds(start, width + LANE)
        reads = [pltpu.make_async_copy(base.at[0, c, :, run], wide.at[c], sem.at[c]) for c in range(2)]
        writes = [pltpu.make_async_copy(wide.at[c], out.at[0, c, :, run], sem.at[c]) for c in range(2)]
        for copy in reads:
            copy.start()
        index = lax.broadcasted_iota(jnp.int32, (rows, width), 0)
        for c in range(2):
            x = moved(came[c], row, shift, index < row)
            reads[c].wait()
            wide[c] = wide[c] + x
            writes[c].start()
        for copy in writes:
            copy.wait()

    return pl.pallas_call(
        kernel,
        out_shape=jax.ShapeDtypeStruct(base.shape, f32),
        in_specs=[SMEM, VMEM, ANY],
        out_specs=ANY,
        input_output_aliases={2: 0},
        scratch_shapes=[pltpu.VMEM((2, rows, width + LANE), f32), pltpu.SemaphoreType.DMA((2,))],
        compiler_params=PARAMS,
    )(offsets, came, pinned(base))


def shifted(value, by):
    devices = lax.axis_size("tile")
    pairs = [(i, i + by) for i in range(devices) if 0 <= i + by < devices]
    return lax.ppermute(value, "tile", pairs)


def swapped(value, bit):
    devices = lax.axis_size("cuts")
    return lax.ppermute(value, "cuts", [(i, i ^ bit) for i in range(devices)])


def after(*values):
    return lax.optimization_barrier(values)


def merged(first, second, top, row, rows):
    index = lax.broadcasted_iota(jnp.int32, first.shape, 1) + top
    return jnp.where(index < rows - row, first, second)


BOUNDS = (0, 128, 256)


def per_device(transmission, probe, prop_phase, row_off, col_off, measured):
    rows, columns = transmission.shape[2:]
    width = probe.shape[1]
    cut = lax.axis_index("cuts").astype(jnp.int32).reshape(1)
    offsets = packed(row_off, col_off)
    came_offsets = shifted(offsets, 1)
    below = [shifted(band, -1) for band in cut_window(came_offsets, transmission, width, BOUNDS)]
    own = cut_window(offsets, transmission, width, BOUNDS)
    cosine, sine, observed = prepare(prop_phase, measured)
    tables = [jnp.asarray(t) for t in dft_tables(width)]

    chunks, across = [], []
    for j, (first, second) in enumerate(zip(own, below)):
        if chunks:
            first, second, chunks[-1], cosine = after(first, second, chunks[-1], cosine)
        chunks.append(merged(first, second, BOUNDS[j], row_off[0], rows))
        chunk = chunks[-1]
        across.append(swapped(chunk, 2))
    across[0], *later = after(across[0], *chunks)
    beside = [swapped(chunk, 1) for chunk in later]
    early = early_waves(cut, [chunks, beside], probe, cosine, sine, tables)
    *across, early = after(*across, early)
    opposite = [swapped(chunk, 1) for chunk in across]
    piece = chain(cut, [chunks, beside, across, opposite], early, probe, cosine, sine, observed, tables)

    came = shifted(piece, 1)
    return add_came(came_offsets, came, place_own(offsets, piece, columns))


def solution(mesh):
    placed = (P("cuts", None, "tile", None), P(), P(), P("tile"), P("tile"), P("tile", None, None))
    return jax.shard_map(
        per_device,
        mesh=mesh,
        in_specs=placed,
        out_specs=P("cuts", None, "tile", None),
        check_vma=False,
    )
```

time: 158 us -> 66.2 us (0.42)
  local copies, waits for them, and re-layouts: 90.7 us -> 0.72 us
  waiting for transfers between devices: 34.4 us -> 20.2 us
  Pallas kernels: 17.5 us -> 26 us
  starting transfers between devices: 12 us -> 16.5 us
    sin x3 -> x0, local copies, waits for them, and re-layouts: 29.7 us -> none  [per_device(): cosine, sine = (jnp.cos(phase), jnp.sin(phase))]
    cos x2 -> x0, local copies, waits for them, and re-layouts: 27.9 us -> none  [per_device(): cosine, sine = (jnp.cos(phase), jnp.sin(phase))]
    another operation x1 -> x0, local copies, waits for them, and re-layouts: 18 us -> none  [by_parity(): return x.reshape(n // 2, 2, n // 2, 2).transpose(1, 0, 3, 2).reshape(n, n)]
    pallas_call x3 -> x7, Pallas kernels: 4.92 us -> 16.7 us  [the longest x1 4.51 us: early_waves(): pl.pallas_call(kernel, out_shape=jax.ShapeDtypeStruct((2, 2, n, n), f32),...]
    transpose x1 -> x0, local copies, waits for them, and re-layouts: 9.79 us -> none  [by_parity(): return x.reshape(n // 2, 2, n // 2, 2).transpose(1, 0, 3, 2).reshape(n, n)]
    ppermute x3 -> x4, waiting for transfers between devices: 24.1 us -> 14.7 us  [shifted(): return lax.ppermute(value, 'tile', pairs)]
    ppermute x3 -> x6, waiting for transfers between devices: 10.4 us -> 5.48 us  [swapped(): return lax.ppermute(value, 'cuts', [(i, i ^ bit) for i in range(devices)])]
    unnamed x13 -> x12, local copies, waits for them, and re-layouts: 4.16 us -> 0.72 us
  transfers between devices with their start and end apart: 6 -> 10, of which waited for: 4 -> 9; matrix products, arithmetic and copies ran while one was open for 56% -> 1% of each run, Pallas kernels for 1% -> 17%
where the time goes in v2:
time: 66.2 us; the launch traced here: 65.7 us
  Pallas kernels  26 us (39%)
  waiting for transfers between devices  20.2 us (31%)
  starting transfers between devices  16.5 us (25%)
  between operations  1.44 us (2%)
  other arithmetic  0.9 us (1%)
  local copies, waits for them, and re-layouts  0.72 us (1%)
    ppermute x4, waiting for transfers between devices, shifted(): return lax.ppermute(value, 'tile', pairs)  14.7 us
    ppermute x4, starting transfers between devices, shifted(): return lax.ppermute(value, 'tile', pairs)  12.4 us
    pallas_call x1, Pallas kernels, chain(): pl.pallas_call(kernel, out_shape=jax.ShapeDtypeStruct((2, n, n), f32), in...  9.31 us
    ppermute x6, waiting for transfers between devices, swapped(): return lax.ppermute(value, 'cuts', [(i, i ^ bit) for i in range(devices)])  5.48 us
    pallas_call x1, Pallas kernels, early_waves(): pl.pallas_call(kernel, out_shape=jax.ShapeDtypeStruct((2, 2, n, n), f32),...  4.51 us
    pallas_call x2, Pallas kernels, cut_window(): pl.pallas_call(kernel, out_shape=[jax.ShapeDtypeStruct((2, bounds[j + 1]...  4.12 us
    ppermute x6, starting transfers between devices, swapped(): return lax.ppermute(value, 'cuts', [(i, i ^ bit) for i in range(devices)])  4.07 us
    pallas_call x1, Pallas kernels, add_came(): pl.pallas_call(kernel, out_shape=jax.ShapeDtypeStruct(base.shape, f32), i...  2.63 us
  transfers between devices with their start and end apart: 10, of which 9 were waited for; matrix products, arithmetic and copies ran while one was open for 1% of the time, Pallas kernels for 17%

profile of v2, /device:TPU:0, one launch (start us, length us, event | category | flops | bytes accessed | tf_op | source)
XLA Modules:
  0.0 65.7 jit_solution(7049249479489471224)
XLA Ops:
  1.3 0.6 shard_map.82.offsets
  1.9 0.0 copy-start.2
  1.9 5.0 %collective-permute-start = (s32[2]{0:T(128)S(1)}, s32[2]{0:T(128)S(1)}, u32[]{:S(2)}, u32[]{:S(2)}) collective-permute-start(s32[2]{0:T(128)S(1)} %shard_map.82.offsets), channel_id=1, source_target_pairs={{0,4},{4,8},{8,12},{12,16},{16,20},{20,24},{24,28},{1,5},{5,9},{9,... | collective-permute-start | bytes 32 | tf_op jit(solution)/shard_map/ppermute | solution.py:455
  6.9 1.3 %collective-permute-done.offsets = s32[2]{0:T(128)S(1)} collective-permute-done((s32[2]{0:T(128)S(1)}, s32[2]{0:T(128)S(1)}, u32[]{:S(2)}, u32[]{:S(2)}) %collective-permute-start) | collective-permute-done | bytes 40 | tf_op jit(solution)/shard_map/ppermute | solution.py:455
  8.2 2.1 %shard_map.84 = (f32[2,128,256]{2,1,0:T(8,128)S(1)}, f32[2,128,256]{2,1,0:T(8,128)S(1)}) custom-call(s32[2]{0:T(128)S(1)} %collective-permute-done.offsets, f32[1,2,256,1024]{3,2,1,0:T(8,128)} %strip.3), custom_call_target="tpu_custom_call" | custom-call | tf_op jit(solution)/shard_map/pallas_call | solution.py:384
  10.3 1.3 %collective-permute-start.2 = (f32[2,128,256]{2,1,0:T(8,128)S(1)}, f32[2,128,256]{2,1,0:T(8,128)S(1)}, u32[]{:S(2)}, u32[]{:S(2)}) collective-permute-start(f32[2,128,256]{2,1,0:T(8,128)S(1)} %get-tuple-element.25), channel_id=1, source_target_pairs={{4,0},{8,4},{12,8},{16,12},{20,16},{24,20},{28,24},{5,1},{9,5},{13... | collective-permute-start | bytes 786440 | tf_op jit(solution)/shard_map/ppermute | solution.py:455
  11.6 2.1 %shard_map.83 = (f32[2,128,256]{2,1,0:T(8,128)S(1)}, f32[2,128,256]{2,1,0:T(8,128)S(1)}) custom-call(s32[2]{0:T(128)S(1)} %shard_map.82.offsets, f32[1,2,256,1024]{3,2,1,0:T(8,128)} %strip.3), custom_call_target="tpu_custom_call" | custom-call | tf_op jit(solution)/shard_map/pallas_call | solution.py:384
  13.6 0.0 copy-start
  13.7 0.0 copy-start.1
  13.7 1.6 %collective-permute-start.1 = (f32[2,128,256]{2,1,0:T(8,128)S(1)}, f32[2,128,256]{2,1,0:T(8,128)S(1)}, u32[]{:S(2)}, u32[]{:S(2)}) collective-permute-start(f32[2,128,256]{2,1,0:T(8,128)S(1)} %get-tuple-element.23), channel_id=1, source_target_pairs={{4,0},{8,4},{12,8},{16,12},{20,16},{24,20},{28,24},{5,1},{9,5},{13... | collective-permute-start | bytes 786440 | tf_op jit(solution)/shard_map/ppermute | solution.py:455
  15.3 5.6 %collective-permute-done.2 = f32[2,128,256]{2,1,0:T(8,128)S(1)} collective-permute-done((f32[2,128,256]{2,1,0:T(8,128)S(1)}, f32[2,128,256]{2,1,0:T(8,128)S(1)}, u32[]{:S(2)}, u32[]{:S(2)}) %collective-permute-start.2) | collective-permute-done | bytes 262176 | tf_op jit(solution)/shard_map/ppermute | solution.py:455
  20.8 0.1 broadcast_select_fusion.1.refs_0_
  20.9 1.6 %collective-permute-start.3 = (f32[2,128,256]{2,1,0:T(8,128)S(1)}, f32[2,128,256]{2,1,0:T(8,128)S(1)}, u32[]{:S(2)}, u32[]{:S(2)}) collective-permute-start(f32[2,128,256]{2,1,0:T(8,128)S(1)} %broadcast_select_fusion.1.refs_0_), channel_id=1, source_target_pairs={{0,2},{1,3},{2,0},{3,1},{4,6},{5,7},{6,4},{7,5},{8,10},{9,11},{10,... | collective-permute-start | bytes 786440 | tf_op jit(solution)/shard_map/ppermute | solution.py:460
  22.5 2.4 %shard_map.85 = (f32[256,256]{1,0:T(8,128)}, f32[256,256]{1,0:T(8,128)}, f32[256,256]{1,0:T(8,128)}) custom-call(f32[256,256]{1,0:T(8,128)S(1)} %copy-done.2, f32[1,256,256]{2,1,0:T(8,128)S(1)} %copy-done.3), custom_call_target="tpu_custom_call" | custom-call | flops 603979776 | bytes 1966080 | tf_op jit(solution)/shard_map/pallas_call | solution.py:174
  24.9 0.3 collective-permute-done.1
  25.2 0.8 %broadcast_select_fusion.refs_1_ = f32[2,128,256]{2,1,0:T(8,128)} fusion(f32[2,128,256]{2,1,0:T(8,128)S(1)} %get-tuple-element.28, f32[2,128,256]{2,1,0:T(8,128)S(1)} %collective-permute-done.1, pred[128]{0:T(512)(128)(4,1)S(1)} %add_compare_fusion), kind=kLoop, calls=%fused_computation | loop fusion | flops 65536 | bytes 786560 | tf_op jit(solution)/shard_map/jit(_where)/select_n | solution.py:469
  26.0 1.4 %collective-permute-done.3.refs_4_ = f32[2,128,256]{2,1,0:T(8,128)S(1)} collective-permute-done((f32[2,128,256]{2,1,0:T(8,128)S(1)}, f32[2,128,256]{2,1,0:T(8,128)S(1)}, u32[]{:S(2)}, u32[]{:S(2)}) %collective-permute-start.3) | collective-permute-done | bytes 262176 | tf_op jit(solution)/shard_map/ppermute | solution.py:460
  27.4 0.7 %copy-done.4 = f32[2,128,256]{2,1,0:T(8,128)} copy-done((f32[2,128,256]{2,1,0:T(8,128)}, f32[2,128,256]{2,1,0:T(8,128)S(1)}, u32[]{:S(2)}) %copy-start.4) | copy-done | bytes 262168
  28.0 0.5 collective-permute-start.5
  28.6 1.5 %collective-permute-start.6 = (f32[2,128,256]{2,1,0:T(8,128)}, f32[2,128,256]{2,1,0:T(8,128)}, u32[]{:S(2)}, u32[]{:S(2)}) collective-permute-start(f32[2,128,256]{2,1,0:T(8,128)} %broadcast_select_fusion.refs_1_), channel_id=1, source_target_pairs={{0,2},{1,3},{2,0},{3,1},{4,6},{5,7},{6,4},{7,5},{8,10},{9,11},{10,... | collective-permute-start | bytes 786440 | tf_op jit(solution)/shard_map/ppermute | solution.py:460
  30.0 0.0 collective-permute-done.4.refs_2_
  30.1 0.2 collective-permute-done.5.refs_3_
  30.3 4.5 %shard_map.86.refs_12_ = f32[2,2,256,256]{3,2,1,0:T(8,128)S(1)} custom-call(s32[1]{0:T(128)} %bitcast.cut_ref, f32[2,128,256]{2,1,0:T(8,128)S(1)} %broadcast_select_fusion.1.refs_0_, f32[2,128,256]{2,1,0:T(8,128)} %broadcast_select_fusion.refs_1_, f32[2,128,256]{2,1,0:T(8,128)} %collective-permute-done.4.refs_2_, ...), custom_call_target="tpu_custom_call" | custom-call | flops 65536 | bytes 4096 | tf_op jit(solution)/shard_map/pallas_call | solution.py:240
  34.8 2.3 %collective-permute-done.6.refs_5_ = f32[2,128,256]{2,1,0:T(8,128)} collective-permute-done((f32[2,128,256]{2,1,0:T(8,128)}, f32[2,128,256]{2,1,0:T(8,128)}, u32[]{:S(2)}, u32[]{:S(2)}) %collective-permute-start.6) | collective-permute-done | bytes 262176 | tf_op jit(solution)/shard_map/ppermute | solution.py:460
  37.1 0.5 collective-permute-start.8
  37.6 1.4 %collective-permute-done.7.refs_6_ = f32[2,128,256]{2,1,0:T(8,128)S(1)} collective-permute-done((f32[2,128,256]{2,1,0:T(8,128)S(1)}, f32[2,128,256]{2,1,0:T(8,128)S(1)}, u32[]{:S(2)}, u32[]{:S(2)}) %collective-permute-start.7) | collective-permute-done | bytes 262176 | tf_op jit(solution)/shard_map/ppermute | solution.py:460
  39.0 0.2 collective-permute-done.8.refs_7_
  39.2 9.3 %shard_map.87.piece = f32[2,256,256]{2,1,0:T(8,128)S(1)} custom-call(s32[1]{0:T(128)} %bitcast.cut_ref, f32[2,128,256]{2,1,0:T(8,128)S(1)} %broadcast_select_fusion.1.refs_0_, f32[2,128,256]{2,1,0:T(8,128)} %broadcast_select_fusion.refs_1_, f32[2,128,256]{2,1,0:T(8,128)} %collective-permute-done.4.refs_2_, f32[2,128,256]{2,1,0:T(8,128)} %collective-permute-done.5.refs_3_, ...), custom_call_target="tpu_custom_call" | custom-call | flops 4026531840 | bytes 1048576 | tf_op jit(solution)/shard_map/pallas_call | solution.py:327
  48.5 4.6 %collective-permute-start.9 = (f32[2,256,256]{2,1,0:T(8,128)S(1)}, f32[2,256,256]{2,1,0:T(8,128)S(1)}, u32[]{:S(2)}, u32[]{:S(2)}) collective-permute-start(f32[2,256,256]{2,1,0:T(8,128)S(1)} %shard_map.87.piece), channel_id=1, source_target_pairs={{0,4},{4,8},{8,12},{12,16},{16,20},{20,24},{24,28},{1,5},{5,9},{9,... | collective-permute-start | bytes 1572872 | tf_op jit(solution)/shard_map/ppermute | solution.py:455
  53.1 2.4 %shard_map.88.base = f32[1,2,256,1024]{3,2,1,0:T(8,128)} custom-call(s32[2]{0:T(128)S(1)} %shard_map.82.offsets, f32[2,256,256]{2,1,0:T(8,128)S(1)} %shard_map.87.piece), custom_call_target="tpu_custom_call" | custom-call | tf_op jit(solution)/shard_map/pallas_call | solution.py:411
  55.5 7.6 %collective-permute-done.9.came = f32[2,256,256]{2,1,0:T(8,128)S(1)} collective-permute-done((f32[2,256,256]{2,1,0:T(8,128)S(1)}, f32[2,256,256]{2,1,0:T(8,128)S(1)}, u32[]{:S(2)}, u32[]{:S(2)}) %collective-permute-start.9) | collective-permute-done | bytes 524320 | tf_op jit(solution)/shard_map/ppermute | solution.py:455
  63.0 2.6 %shard_map.89 = f32[1,2,256,1024]{3,2,1,0:T(8,128)} custom-call(s32[2]{0:T(128)S(1)} %collective-permute-done.offsets, f32[2,256,256]{2,1,0:T(8,128)S(1)} %collective-permute-done.9.came, f32[1,2,256,1024]{3,2,1,0:T(8,128)} %shard_map.88.base), custom_call_target="tpu_custom_call", output_to_operand_aliasing={{}: (2, {})} | custom-call | tf_op jit(solution)/shard_map/pallas_call | solution.py:441
  (12 shorter events, 0.0 us)
Async XLA Ops:
  1.9 20.6 %copy-start.2 = (f32[256,256]{1,0:T(8,128)S(1)}, f32[256,256]{1,0:T(8,128)}, u32[]{:S(2)}) copy-start(f32[256,256]{1,0:T(8,128)} %phase.1) | copy-start | bytes 786436
  1.9 20.6 %copy-start.3 = (f32[1,256,256]{2,1,0:T(8,128)S(1)}, f32[1,256,256]{2,1,0:T(8,128)}, u32[]{:S(2)}) copy-start(f32[1,256,256]{2,1,0:T(8,128)} %refs_0_.1) | copy-start | bytes 786436
  1.9 6.3 %collective-permute-start = (s32[2]{0:T(128)S(1)}, s32[2]{0:T(128)S(1)}, u32[]{:S(2)}, u32[]{:S(2)}) collective-permute-start(s32[2]{0:T(128)S(1)} %shard_map.82.offsets), channel_id=1, source_target_pairs={{0,4},{4,8},{8,12},{12,16},{16,20},{20,24},{24,28},{1,5},{5,9},{9,... | collective-permute-start | bytes 32 | tf_op jit(solution)/shard_map/ppermute | solution.py:455
  10.3 10.5 %collective-permute-start.2 = (f32[2,128,256]{2,1,0:T(8,128)S(1)}, f32[2,128,256]{2,1,0:T(8,128)S(1)}, u32[]{:S(2)}, u32[]{:S(2)}) collective-permute-start(f32[2,128,256]{2,1,0:T(8,128)S(1)} %get-tuple-element.25), channel_id=1, source_target_pairs={{4,0},{8,4},{12,8},{16,12},{20,16},{24,20},{28,24},{5,1},{9,5},{13... | collective-permute-start | bytes 786440 | tf_op jit(solution)/shard_map/ppermute | solution.py:455
  13.6 16.7 %copy-start = (bf16[4,256,768]{2,1,0:T(8,128)(2,1)S(1)}, bf16[4,256,768]{2,1,0:T(8,128)(2,1)}, u32[]{:S(2)}) copy-start(bf16[4,256,768]{2,1,0:T(8,128)(2,1)} %constant.14.clone.refs_8_.refs_14_) | copy-start | bytes 4718596
  13.7 16.6 %copy-start.1 = (bf16[4,768,256]{2,1,0:T(8,128)(2,1)S(1)}, bf16[4,768,256]{2,1,0:T(8,128)(2,1)}, u32[]{:S(2)}) copy-start(bf16[4,768,256]{2,1,0:T(8,128)(2,1)} %constant.13.clone.refs_7_.refs_13_) | copy-start | bytes 4718596
  13.7 11.5 %collective-permute-start.1 = (f32[2,128,256]{2,1,0:T(8,128)S(1)}, f32[2,128,256]{2,1,0:T(8,128)S(1)}, u32[]{:S(2)}, u32[]{:S(2)}) collective-permute-start(f32[2,128,256]{2,1,0:T(8,128)S(1)} %get-tuple-element.23), channel_id=1, source_target_pairs={{4,0},{8,4},{12,8},{16,12},{20,16},{24,20},{28,24},{5,1},{9,5},{13... | collective-permute-start | bytes 786440 | tf_op jit(solution)/shard_map/ppermute | solution.py:455
  20.9 6.4 %collective-permute-start.3 = (f32[2,128,256]{2,1,0:T(8,128)S(1)}, f32[2,128,256]{2,1,0:T(8,128)S(1)}, u32[]{:S(2)}, u32[]{:S(2)}) collective-permute-start(f32[2,128,256]{2,1,0:T(8,128)S(1)} %broadcast_select_fusion.1.refs_0_), channel_id=1, source_target_pairs={{0,2},{1,3},{2,0},{3,1},{4,6},{5,7},{6,4},{7,5},{8,10},{9,11},{10,... | collective-permute-start | bytes 786440 | tf_op jit(solution)/shard_map/ppermute | solution.py:460
  27.4 0.7 %copy-start.4 = (f32[2,128,256]{2,1,0:T(8,128)}, f32[2,128,256]{2,1,0:T(8,128)S(1)}, u32[]{:S(2)}) copy-start(f32[2,128,256]{2,1,0:T(8,128)S(1)} %collective-permute-done.3.refs_4_) | copy-start | bytes 786436
  28.0 2.0 %collective-permute-start.4 = (f32[2,128,256]{2,1,0:T(8,128)S(1)}, f32[2,128,256]{2,1,0:T(8,128)}, u32[]{:S(2)}, u32[]{:S(2)}) collective-permute-start(f32[2,128,256]{2,1,0:T(8,128)S(1)} %broadcast_select_fusion.1.refs_0_), channel_id=1, source_target_pairs={{0,1},{1,0},{2,3},{3,2},{4,5},{5,4},{6,7},{7,6},{8,9},{9,8},{10,11... | collective-permute-start | bytes 786440 | tf_op jit(solution)/shard_map/ppermute | solution.py:460
  28.0 2.2 %collective-permute-start.5 = (f32[2,128,256]{2,1,0:T(8,128)}, f32[2,128,256]{2,1,0:T(8,128)}, u32[]{:S(2)}, u32[]{:S(2)}) collective-permute-start(f32[2,128,256]{2,1,0:T(8,128)} %broadcast_select_fusion.refs_1_), channel_id=1, source_target_pairs={{0,1},{1,0},{2,3},{3,2},{4,5},{5,4},{6,7},{7,6},{8,9},{9,8},{10,11... | collective-permute-start | bytes 786440 | tf_op jit(solution)/shard_map/ppermute | solution.py:460
  28.6 8.5 %collective-permute-start.6 = (f32[2,128,256]{2,1,0:T(8,128)}, f32[2,128,256]{2,1,0:T(8,128)}, u32[]{:S(2)}, u32[]{:S(2)}) collective-permute-start(f32[2,128,256]{2,1,0:T(8,128)} %broadcast_select_fusion.refs_1_), channel_id=1, source_target_pairs={{0,2},{1,3},{2,0},{3,1},{4,6},{5,7},{6,4},{7,5},{8,10},{9,11},{10,... | collective-permute-start | bytes 786440 | tf_op jit(solution)/shard_map/ppermute | solution.py:460
  30.3 6.8 %copy-start.5 = (f32[2,128,256]{2,1,0:T(8,128)S(1)}, f32[2,128,256]{2,1,0:T(8,128)}, u32[]{:S(2)}) copy-start(f32[2,128,256]{2,1,0:T(8,128)} %copy-done.4) | copy-start | bytes 786436
  37.1 1.9 %collective-permute-start.7 = (f32[2,128,256]{2,1,0:T(8,128)S(1)}, f32[2,128,256]{2,1,0:T(8,128)S(1)}, u32[]{:S(2)}, u32[]{:S(2)}) collective-permute-start(f32[2,128,256]{2,1,0:T(8,128)S(1)} %copy-done.5), channel_id=1, source_target_pairs={{0,1},{1,0},{2,3},{3,2},{4,5},{5,4},{6,7},{7,6},{8,9},{9,8},{10,11... | collective-permute-start | bytes 786440 | tf_op jit(solution)/shard_map/ppermute | solution.py:460
  37.1 2.1 %collective-permute-start.8 = (f32[2,128,256]{2,1,0:T(8,128)}, f32[2,128,256]{2,1,0:T(8,128)S(1)}, u32[]{:S(2)}, u32[]{:S(2)}) collective-permute-start(f32[2,128,256]{2,1,0:T(8,128)} %collective-permute-done.6.refs_5_), channel_id=1, source_target_pairs={{0,1},{1,0},{2,3},{3,2},{4,5},{5,4},{6,7},{7,6},{8,9},{9,8},{10,11... | collective-permute-start | bytes 786440 | tf_op jit(solution)/shard_map/ppermute | solution.py:460
  48.5 14.5 %collective-permute-start.9 = (f32[2,256,256]{2,1,0:T(8,128)S(1)}, f32[2,256,256]{2,1,0:T(8,128)S(1)}, u32[]{:S(2)}, u32[]{:S(2)}) collective-permute-start(f32[2,256,256]{2,1,0:T(8,128)S(1)} %shard_map.87.piece), channel_id=1, source_target_pairs={{0,4},{4,8},{8,12},{12,16},{16,20},{20,24},{24,28},{1,5},{5,9},{9,... | collective-permute-start | bytes 1572872 | tf_op jit(solution)/shard_map/ppermute | solution.py:455

commit v3 on v2

--- a/solution.py
+++ b/solution.py
@@ -203,9 +203,9 @@
     pltpu.make_async_copy(patch.at[slot], patch.at[slot], sem).wait()
 
 
-def fetch_patches(me, sources, patch, sems):
-    for i, chunks in enumerate(sources):
-        start_chunks(chunks, patch, me ^ i, sems.at[me ^ i])
+def fetch_patches(me, sources, patch, sems, which):
+    for i in which:
+        start_chunks(sources[i], patch, me ^ i, sems.at[me ^ i])
 
 
 def grouped(refs, patches, chunks):
@@ -225,7 +225,7 @@
 
         @pl.when(me < 2)
         def _():
-            fetch_patches(me, sources, patch, sems)
+            fetch_patches(me, sources, patch, sems, (0, 1))
             for copy in copies:
                 copy.start()
             before = first
@@ -266,7 +266,7 @@
 
     def kernel(cut_ref, *refs):
         sources, rest = grouped(refs, sections, chunks)
-        *planes, right, left, out, patch, waves, held, probe, sems, early_sem, held_sem = rest
+        *planes, right, left, out_re, out_im, patch, waves, held, probe, sems, early_sem, held_sem = rest
         me = cut_ref[0]
         tables = (right, left)
         targets = [held.at[0], held.at[1], held.at[2], probe]
@@ -283,7 +283,7 @@
         def back(s, re, im):
             @pl.when(me == s)
             def _():
-                out[0], out[1] = conj_times(wave(s)[0], wave(s)[1], re, im)
+                out_re[...], out_im[...] = conj_times(wave(s)[0], wave(s)[1], re, im)
 
             if s > 0:
 
@@ -296,28 +296,41 @@
 
         early_copy = pltpu.make_async_copy(planes[4], waves.at[pl.ds(0, 2)], early_sem)
 
+        fetch_patches(me, sources, patch, sems, (2, 3))
+
         @pl.when(me < 2)
         def _():
             early_copy.start()
 
-        fetch_patches(me, sources, patch, sems)
         for copy in copies:
             copy.start()
-        for s in range(2):
-            wait_slot(patch, s, sems.at[s])
-        for copy in (copies[0], copies[1], copies[3]):
+        fetch_patches(me, sources, patch, sems, (0, 1))
+        for copy in copies[:2]:
             copy.wait()
 
         @pl.when(me < 2)
         def _():
             early_copy.wait()
 
-        pl.when(me >= 2)(first_two)
+        @pl.when(me >= 2)
+        def _():
+            copies[3].wait()
+            for s in range(2):
+                wait_slot(patch, s, sems.at[s])
+            first_two()
+
         for s in range(2, sections):
             wait_slot(patch, s, sems.at[s])
             if s < sections - 1:
                 run_forward(s, wave(s), patch.at[s], waves.at[s], cosine, sine, tables)
         copies[2].wait()
+
+        @pl.when(me < 2)
+        def _():
+            copies[3].wait()
+            for s in range(2):
+                wait_slot(patch, s, sems.at[s])
+
         last = sections - 1
         re, im = times(wave(last)[0], wave(last)[1], patch[last, 0], patch[last, 1])
         a, b = forward(re, im, tables)
@@ -326,9 +339,9 @@
 
     return pl.pallas_call(
         kernel,
-        out_shape=jax.ShapeDtypeStruct((2, n, n), f32),
+        out_shape=[jax.ShapeDtypeStruct((n, n), f32)] * 2,
         in_specs=[SMEM] + [ANY] * (sections * chunks + len(planes_in)) + [VMEM] * 2,
-        out_specs=VMEM,
+        out_specs=[VMEM] * 2,
         scratch_shapes=[
             pltpu.VMEM((sections, 2, n, n), f32),
             pltpu.VMEM((sections - 1, 2, n, n), f32),
@@ -397,56 +410,50 @@
     return pltpu.roll(jnp.concatenate([x, jnp.zeros((rows, LANE), f32)], 1), shift, 1)
 
 
-def place_own(offsets, piece, columns):
-    _, rows, width = piece.shape
-
-    def kernel(offsets, piece, out):
+def place_own(offsets, came_offsets, planes, columns):
+    rows, width = planes[0].shape
+
+    def kernel(offsets, came_offsets, re, im, out, *runs):
         index = lax.broadcasted_iota(jnp.int32, (rows, width), 0)
         out[...] = jnp.zeros_like(out)
         row = offsets[0]
         start, shift = window_start(offsets[1], width, columns)
-        for c in range(2):
-            out[0, c, :, pl.ds(start, width + LANE)] = moved(piece[c], row, shift, index >= row)
-
-    return pl.pallas_call(
-        kernel,
-        out_shape=jax.ShapeDtypeStruct((1, 2, rows, columns), f32),
-        in_specs=[SMEM, VMEM],
-        out_specs=VMEM,
-        compiler_params=PARAMS,
-    )(offsets, piece)
-
-
-def add_came(offsets, came, base):
-    _, rows, width = came.shape
+        came_start, _ = window_start(came_offsets[1], width, columns)
+        for c, plane in enumerate((re, im)):
+            out[0, c, :, pl.ds(start, width + LANE)] = moved(plane[...], row, shift, index >= row)
+            runs[c][...] = out[0, c, :, pl.ds(came_start, width + LANE)]
+
+    return pl.pallas_call(
+        kernel,
+        out_shape=[jax.ShapeDtypeStruct((1, 2, rows, columns), f32)] + [pltpu.VMEM((rows, width + LANE), f32)] * 2,
+        in_specs=[SMEM, SMEM, VMEM, VMEM],
+        out_specs=[VMEM] * 3,
+        compiler_params=PARAMS,
+    )(offsets, came_offsets, *planes)
+
+
+def add_came(offsets, came, run, base, c):
+    rows, width = came.shape
     columns = base.shape[3]
 
-    def kernel(offsets, came, base, out, wide, sem):
+    def kernel(offsets, came, run, base, out, wide, sem):
         row = offsets[0]
         start, shift = window_start(offsets[1], width, columns)
-        run = pl.ds(start, width + LANE)
-        reads = [pltpu.make_async_copy(base.at[0, c, :, run], wide.at[c], sem.at[c]) for c in range(2)]
-        writes = [pltpu.make_async_copy(wide.at[c], out.at[0, c, :, run], sem.at[c]) for c in range(2)]
-        for copy in reads:
-            copy.start()
         index = lax.broadcasted_iota(jnp.int32, (rows, width), 0)
-        for c in range(2):
-            x = moved(came[c], row, shift, index < row)
-            reads[c].wait()
-            wide[c] = wide[c] + x
-            writes[c].start()
-        for copy in writes:
-            copy.wait()
+        wide[...] = run[...] + moved(came[...], row, shift, index < row)
+        write = pltpu.make_async_copy(wide, out.at[0, c, :, pl.ds(start, width + LANE)], sem)
+        write.start()
+        write.wait()
 
     return pl.pallas_call(
         kernel,
         out_shape=jax.ShapeDtypeStruct(base.shape, f32),
-        in_specs=[SMEM, VMEM, ANY],
+        in_specs=[SMEM, VMEM, VMEM, ANY],
         out_specs=ANY,
-        input_output_aliases={2: 0},
-        scratch_shapes=[pltpu.VMEM((2, rows, width + LANE), f32), pltpu.SemaphoreType.DMA((2,))],
-        compiler_params=PARAMS,
-    )(offsets, came, pinned(base))
+        input_output_aliases={3: 0},
+        scratch_shapes=[pltpu.VMEM((rows, width + LANE), f32), pltpu.SemaphoreType.DMA],
+        compiler_params=PARAMS,
+    )(offsets, came, run, pinned(base))
 
 
 def shifted(value, by):
@@ -478,27 +485,32 @@
     cut = lax.axis_index("cuts").astype(jnp.int32).reshape(1)
     offsets = packed(row_off, col_off)
     came_offsets = shifted(offsets, 1)
-    below = [shifted(band, -1) for band in cut_window(came_offsets, transmission, width, BOUNDS)]
+    cosine, sine, observed = prepare(prop_phase, measured)
+    bands = list(cut_window(came_offsets, transmission, width, BOUNDS))
+    below = [shifted(band, -1) for band in bands]
     own = cut_window(offsets, transmission, width, BOUNDS)
-    cosine, sine, observed = prepare(prop_phase, measured)
     tables = [jnp.asarray(t) for t in dft_tables(width)]
 
     chunks, across = [], []
+    below[0], cosine, sine, observed = after(below[0], cosine, sine, observed)
     for j, (first, second) in enumerate(zip(own, below)):
         if chunks:
-            first, second, chunks[-1], cosine = after(first, second, chunks[-1], cosine)
+            first, second, chunks[-1] = after(first, second, chunks[-1])
         chunks.append(merged(first, second, BOUNDS[j], row_off[0], rows))
         chunk = chunks[-1]
         across.append(swapped(chunk, 2))
-    across[0], *later = after(across[0], *chunks)
-    beside = [swapped(chunk, 1) for chunk in later]
+    beside = [swapped(chunk, 1) for chunk in chunks]
+    across[0], beside[0] = after(across[0], beside[0])
     early = early_waves(cut, [chunks, beside], probe, cosine, sine, tables)
-    *across, early = after(*across, early)
+    across[1], early = after(across[1], early)
     opposite = [swapped(chunk, 1) for chunk in across]
-    piece = chain(cut, [chunks, beside, across, opposite], early, probe, cosine, sine, observed, tables)
-
-    came = shifted(piece, 1)
-    return add_came(came_offsets, came, place_own(offsets, piece, columns))
+    planes = chain(cut, [chunks, beside, across, opposite], early, probe, cosine, sine, observed, tables)
+
+    came = [shifted(plane, 1) for plane in planes]
+    gradient, *runs = place_own(offsets, came_offsets, planes, columns)
+    for c in range(2):
+        gradient = add_came(came_offsets, came[c], runs[c], gradient, c)
+    return gradient
 
 
 def solution(mesh):

time: 66.2 us -> 62.5 us (0.944)
  waiting for transfers between devices: 20.2 us -> 13.8 us
  starting transfers between devices: 16.5 us -> 19 us
  local copies, waits for them, and re-layouts: 0.72 us -> 0.02 us
    ppermute x4 -> x5, waiting for transfers between devices: 14.7 us -> 9.51 us  [shifted(): return lax.ppermute(value, 'tile', pairs)]
    ppermute x4 -> x5, starting transfers between devices: 12.4 us -> 15.4 us  [shifted(): return lax.ppermute(value, 'tile', pairs)]
    ppermute x6, waiting for transfers between devices: 5.48 us -> 4.28 us  [swapped(): return lax.ppermute(value, 'cuts', [(i, i ^ bit) for i in range(devices)])]
    unnamed x12 -> x8, local copies, waits for them, and re-layouts: 0.72 us -> 0.02 us
    pallas_call x1 -> x2, Pallas kernels: 2.63 us -> 3.18 us  [add_came(): pl.pallas_call(kernel, out_shape=jax.ShapeDtypeStruct(base.shape, f32), i...]
  transfers between devices with their start and end apart: 10 -> 11, of which waited for: 9 -> 8; matrix products, arithmetic and copies ran while one was open for 1% -> 1% of each run, Pallas kernels for 17% -> 22%
where the time goes in v3:
time: 62.5 us; the launch traced here: 61.6 us
  Pallas kernels  26.4 us (42%)
  starting transfers between devices  19 us (30%)
  waiting for transfers between devices  13.8 us (22%)
  between operations  1.53 us (2%)
  other arithmetic  0.9 us (1%)
    ppermute x5, starting transfers between devices, shifted(): return lax.ppermute(value, 'tile', pairs)  15.4 us
    ppermute x5, waiting for transfers between devices, shifted(): return lax.ppermute(value, 'tile', pairs)  9.51 us
    pallas_call x1, Pallas kernels, chain(): pl.pallas_call(kernel, out_shape=[jax.ShapeDtypeStruct((n, n), f32)] * 2,...  8.83 us
    pallas_call x1, Pallas kernels, early_waves(): pl.pallas_call(kernel, out_shape=jax.ShapeDtypeStruct((2, 2, n, n), f32),...  4.47 us
    pallas_call x2, Pallas kernels, cut_window(): pl.pallas_call(kernel, out_shape=[jax.ShapeDtypeStruct((2, bounds[j + 1]...  4.4 us
    ppermute x6, waiting for transfers between devices, swapped(): return lax.ppermute(value, 'cuts', [(i, i ^ bit) for i in range(devices)])  4.28 us
    ppermute x6, starting transfers between devices, swapped(): return lax.ppermute(value, 'cuts', [(i, i ^ bit) for i in range(devices)])  3.56 us
    pallas_call x2, Pallas kernels, add_came(): pl.pallas_call(kernel, out_shape=jax.ShapeDtypeStruct(base.shape, f32), i...  3.18 us
  transfers between devices with their start and end apart: 11, of which 8 were waited for; matrix products, arithmetic and copies ran while one was open for 1% of the time, Pallas kernels for 22%

profile of v3, /device:TPU:0, one launch (start us, length us, event | category | flops | bytes accessed | tf_op | source)
XLA Modules:
  0.0 61.6 jit_solution(2252943512516758474)
XLA Ops:
  1.4 0.6 shard_map.82.offsets
  2.0 4.9 %collective-permute-start = (s32[2]{0:T(128)S(1)}, s32[2]{0:T(128)S(1)}, u32[]{:S(2)}, u32[]{:S(2)}) collective-permute-start(s32[2]{0:T(128)S(1)} %shard_map.82.offsets), channel_id=1, source_target_pairs={{0,4},{4,8},{8,12},{12,16},{16,20},{20,24},{24,28},{1,5},{5,9},{9,... | collective-permute-start | bytes 32 | tf_op jit(solution)/shard_map/ppermute | solution.py:462
  6.8 1.3 %collective-permute-done.offsets.came_offsets = s32[2]{0:T(128)S(1)} collective-permute-done((s32[2]{0:T(128)S(1)}, s32[2]{0:T(128)S(1)}, u32[]{:S(2)}, u32[]{:S(2)}) %collective-permute-start) | collective-permute-done | bytes 40 | tf_op jit(solution)/shard_map/ppermute | solution.py:462
  8.1 2.1 %shard_map.84 = (f32[2,128,256]{2,1,0:T(8,128)S(1)}, f32[2,128,256]{2,1,0:T(8,128)S(1)}) custom-call(s32[2]{0:T(128)S(1)} %collective-permute-done.offsets.came_offsets, f32[1,2,256,1024]{3,2,1,0:T(8,128)} %strip.3), custom_call_target="tpu_custom_call" | custom-call | tf_op jit(solution)/shard_map/pallas_call | solution.py:397
  10.2 1.3 %collective-permute-start.2 = (f32[2,128,256]{2,1,0:T(8,128)S(1)}, f32[2,128,256]{2,1,0:T(8,128)S(1)}, u32[]{:S(2)}, u32[]{:S(2)}) collective-permute-start(f32[2,128,256]{2,1,0:T(8,128)S(1)} %get-tuple-element.31), channel_id=1, source_target_pairs={{4,0},{8,4},{12,8},{16,12},{20,16},{24,20},{28,24},{5,1},{9,5},{13... | collective-permute-start | bytes 786440 | tf_op jit(solution)/shard_map/ppermute | solution.py:462
  11.5 1.3 %collective-permute-start.1 = (f32[2,128,256]{2,1,0:T(8,128)S(1)}, f32[2,128,256]{2,1,0:T(8,128)S(1)}, u32[]{:S(2)}, u32[]{:S(2)}) collective-permute-start(f32[2,128,256]{2,1,0:T(8,128)S(1)} %get-tuple-element.29), channel_id=1, source_target_pairs={{4,0},{8,4},{12,8},{16,12},{20,16},{24,20},{28,24},{5,1},{9,5},{13... | collective-permute-start | bytes 786440 | tf_op jit(solution)/shard_map/ppermute | solution.py:462
  12.8 2.4 %shard_map.85 = (f32[256,256]{1,0:T(8,128)}, f32[256,256]{1,0:T(8,128)}, f32[256,256]{1,0:T(8,128)}) custom-call(f32[256,256]{1,0:T(8,128)S(1)} %copy-done.2, f32[1,256,256]{2,1,0:T(8,128)S(1)} %copy-done.3), custom_call_target="tpu_custom_call" | custom-call | flops 603979776 | bytes 1966080 | tf_op jit(solution)/shard_map/pallas_call | solution.py:174
  15.3 0.0 copy-start
  15.3 0.0 copy-start.1
  15.3 2.3 %shard_map.83 = (f32[2,128,256]{2,1,0:T(8,128)S(1)}, f32[2,128,256]{2,1,0:T(8,128)S(1)}) custom-call(s32[2]{0:T(128)S(1)} %shard_map.82.offsets, f32[1,2,256,1024]{3,2,1,0:T(8,128)} %strip.3), custom_call_target="tpu_custom_call" | custom-call | tf_op jit(solution)/shard_map/pallas_call | solution.py:397
  17.7 3.9 %collective-permute-done.2 = f32[2,128,256]{2,1,0:T(8,128)S(1)} collective-permute-done((f32[2,128,256]{2,1,0:T(8,128)S(1)}, f32[2,128,256]{2,1,0:T(8,128)S(1)}, u32[]{:S(2)}, u32[]{:S(2)}) %collective-permute-start.2) | collective-permute-done | bytes 262176 | tf_op jit(solution)/shard_map/ppermute | solution.py:462
  21.6 0.1 broadcast_select_fusion.1.refs_0_
  21.6 1.6 %collective-permute-start.3 = (f32[2,128,256]{2,1,0:T(8,128)S(1)}, f32[2,128,256]{2,1,0:T(8,128)}, u32[]{:S(2)}, u32[]{:S(2)}) collective-permute-start(f32[2,128,256]{2,1,0:T(8,128)S(1)} %broadcast_select_fusion.1.refs_0_), channel_id=1, source_target_pairs={{0,2},{1,3},{2,0},{3,1},{4,6},{5,7},{6,4},{7,5},{8,10},{9,11},{10,... | collective-permute-start | bytes 786440 | tf_op jit(solution)/shard_map/ppermute | solution.py:467
  23.2 1.9 %collective-permute-done.1 = f32[2,128,256]{2,1,0:T(8,128)S(1)} collective-permute-done((f32[2,128,256]{2,1,0:T(8,128)S(1)}, f32[2,128,256]{2,1,0:T(8,128)S(1)}, u32[]{:S(2)}, u32[]{:S(2)}) %collective-permute-start.1) | collective-permute-done | bytes 262176 | tf_op jit(solution)/shard_map/ppermute | solution.py:462
  25.1 0.0 collective-permute-start.4
  25.1 0.8 %broadcast_select_fusion.refs_1_ = f32[2,128,256]{2,1,0:T(8,128)} fusion(f32[2,128,256]{2,1,0:T(8,128)S(1)} %get-tuple-element.37, f32[2,128,256]{2,1,0:T(8,128)S(1)} %collective-permute-done.1, pred[128]{0:T(512)(128)(4,1)S(1)} %add_compare_fusion), kind=kLoop, calls=%fused_computation | loop fusion | flops 65536 | bytes 786560 | tf_op jit(solution)/shard_map/jit(_where)/select_n | solution.py:476
  25.9 0.5 collective-permute-start.5
  26.4 1.5 %collective-permute-start.6 = (f32[2,128,256]{2,1,0:T(8,128)}, f32[2,128,256]{2,1,0:T(8,128)}, u32[]{:S(2)}, u32[]{:S(2)}) collective-permute-start(f32[2,128,256]{2,1,0:T(8,128)} %broadcast_select_fusion.refs_1_), channel_id=1, source_target_pairs={{0,2},{1,3},{2,0},{3,1},{4,6},{5,7},{6,4},{7,5},{8,10},{9,11},{10,... | collective-permute-start | bytes 786440 | tf_op jit(solution)/shard_map/ppermute | solution.py:467
  27.9 0.0 collective-permute-done.4.refs_2_
  27.9 0.3 collective-permute-done.3.refs_4_
  28.2 0.0 collective-permute-start.7
  28.2 4.5 %shard_map.86.refs_12_ = f32[2,2,256,256]{3,2,1,0:T(8,128)S(1)} custom-call(s32[1]{0:T(128)} %bitcast.cut_ref, f32[2,128,256]{2,1,0:T(8,128)S(1)} %broadcast_select_fusion.1.refs_0_, f32[2,128,256]{2,1,0:T(8,128)} %broadcast_select_fusion.refs_1_, f32[2,128,256]{2,1,0:T(8,128)} %collective-permute-done.4.refs_2_, ...), custom_call_target="tpu_custom_call" | custom-call | flops 65536 | bytes 4096 | tf_op jit(solution)/shard_map/pallas_call | solution.py:240
  32.7 2.2 %collective-permute-done.6.refs_5_ = f32[2,128,256]{2,1,0:T(8,128)} collective-permute-done((f32[2,128,256]{2,1,0:T(8,128)}, f32[2,128,256]{2,1,0:T(8,128)}, u32[]{:S(2)}, u32[]{:S(2)}) %collective-permute-start.6) | collective-permute-done | bytes 262176 | tf_op jit(solution)/shard_map/ppermute | solution.py:467
  34.9 1.7 %collective-permute-done.8.refs_7_ = f32[2,128,256]{2,1,0:T(8,128)S(1)} collective-permute-done((f32[2,128,256]{2,1,0:T(8,128)}, f32[2,128,256]{2,1,0:T(8,128)S(1)}, u32[]{:S(2)}, u32[]{:S(2)}) %collective-permute-start.8) | collective-permute-done | bytes 262176 | tf_op jit(solution)/shard_map/ppermute | solution.py:467
  36.7 8.8 %shard_map.87 = (f32[256,256]{1,0:T(8,128)S(1)}, f32[256,256]{1,0:T(8,128)S(1)}) custom-call(s32[1]{0:T(128)} %bitcast.cut_ref, f32[2,128,256]{2,1,0:T(8,128)S(1)} %broadcast_select_fusion.1.refs_0_, f32[2,128,256]{2,1,0:T(8,128)} %broadcast_select_fusion.refs_1_, f32[2,128,256]{2,1,0:T(8,128)} %collective-permute-done.4.refs_2_, ...), custom_call_target="tpu_custom_call" | custom-call | flops 4026531840 | bytes 1048576 | tf_op jit(solution)/shard_map/pallas_call | solution.py:340
  45.5 4.5 %collective-permute-start.10 = (f32[256,256]{1,0:T(8,128)S(1)}, f32[256,256]{1,0:T(8,128)S(1)}, u32[]{:S(2)}, u32[]{:S(2)}) collective-permute-start(f32[256,256]{1,0:T(8,128)S(1)} %get-tuple-element.47.re), channel_id=1, source_target_pairs={{0,4},{4,8},{8,12},{12,16},{16,20},{20,24},{24,28},{1,5},{5,9},{9,... | collective-permute-start | bytes 786440 | tf_op jit(solution)/shard_map/ppermute | solution.py:462
  50.1 3.4 %collective-permute-start.9 = (f32[256,256]{1,0:T(8,128)S(1)}, f32[256,256]{1,0:T(8,128)S(1)}, u32[]{:S(2)}, u32[]{:S(2)}) collective-permute-start(f32[256,256]{1,0:T(8,128)S(1)} %get-tuple-element.46.im), channel_id=1, source_target_pairs={{0,4},{4,8},{8,12},{12,16},{16,20},{20,24},{24,28},{1,5},{5,9},{9,... | collective-permute-start | bytes 786440 | tf_op jit(solution)/shard_map/ppermute | solution.py:462
  53.5 2.5 %shard_map.88 = (f32[1,2,256,1024]{3,2,1,0:T(8,128)}, f32[256,384]{1,0:T(8,128)S(1)}, f32[256,384]{1,0:T(8,128)S(1)}) custom-call(s32[2]{0:T(128)S(1)} %shard_map.82.offsets, s32[2]{0:T(128)S(1)} %collective-permute-done.offsets.came_offsets, f32[256,256]{1,0:T(8,128)S(1)} %get-tuple-element.47.re, f32[256,256]{1,0:T(8,128)S(1)} %get-tuple-element.46.im), custom_call_target="tpu_custom_call" | custom-call | tf_op jit(solution)/shard_map/pallas_call | solution.py:426
  56.0 0.8 %collective-permute-done.10.came = f32[256,256]{1,0:T(8,128)S(1)} collective-permute-done((f32[256,256]{1,0:T(8,128)S(1)}, f32[256,256]{1,0:T(8,128)S(1)}, u32[]{:S(2)}, u32[]{:S(2)}) %collective-permute-start.10) | collective-permute-done | bytes 262176 | tf_op jit(solution)/shard_map/ppermute | solution.py:462
  56.8 1.6 %shard_map.89.base = f32[1,2,256,1024]{3,2,1,0:T(8,128)} custom-call(s32[2]{0:T(128)S(1)} %collective-permute-done.offsets.came_offsets, f32[256,256]{1,0:T(8,128)S(1)} %collective-permute-done.10.came, f32[256,384]{1,0:T(8,128)S(1)} %get-tuple-element.49.run, f32[1,2,256,1024]{3,2,1,0:T(8,128)} %get-tuple-element.50.base), custom_call_target="tpu_custom_call", output_to_operand_aliasing={{}: (3, {})} | custom-call | tf_op jit(solution)/shard_map/pallas_call | solution.py:448
  58.4 1.6 %collective-permute-done.9.came = f32[256,256]{1,0:T(8,128)S(1)} collective-permute-done((f32[256,256]{1,0:T(8,128)S(1)}, f32[256,256]{1,0:T(8,128)S(1)}, u32[]{:S(2)}, u32[]{:S(2)}) %collective-permute-start.9) | collective-permute-done | bytes 262176 | tf_op jit(solution)/shard_map/ppermute | solution.py:462
  60.1 1.6 %shard_map.90 = f32[1,2,256,1024]{3,2,1,0:T(8,128)} custom-call(s32[2]{0:T(128)S(1)} %collective-permute-done.offsets.came_offsets, f32[256,256]{1,0:T(8,128)S(1)} %collective-permute-done.9.came, f32[256,384]{1,0:T(8,128)S(1)} %get-tuple-element.48.run, f32[1,2,256,1024]{3,2,1,0:T(8,128)} %shard_map.89.base), custom_call_target="tpu_custom_call", output_to_operand_aliasing={{}: (3, {})} | custom-call | tf_op jit(solution)/shard_map/pallas_call | solution.py:448
  (11 shorter events, 0.0 us)
Async XLA Ops:
  0.0 12.8 %copy-start.3 = (f32[1,256,256]{2,1,0:T(8,128)S(1)}, f32[1,256,256]{2,1,0:T(8,128)}, u32[]{:S(2)}) copy-start(f32[1,256,256]{2,1,0:T(8,128)} %refs_0_.1) | copy-start | bytes 786436
  0.0 12.8 %copy-start.2 = (f32[256,256]{1,0:T(8,128)S(1)}, f32[256,256]{1,0:T(8,128)}, u32[]{:S(2)}) copy-start(f32[256,256]{1,0:T(8,128)} %phase.1) | copy-start | bytes 786436
  2.0 6.2 %collective-permute-start = (s32[2]{0:T(128)S(1)}, s32[2]{0:T(128)S(1)}, u32[]{:S(2)}, u32[]{:S(2)}) collective-permute-start(s32[2]{0:T(128)S(1)} %shard_map.82.offsets), channel_id=1, source_target_pairs={{0,4},{4,8},{8,12},{12,16},{16,20},{20,24},{24,28},{1,5},{5,9},{9,... | collective-permute-start | bytes 32 | tf_op jit(solution)/shard_map/ppermute | solution.py:462
  10.2 11.4 %collective-permute-start.2 = (f32[2,128,256]{2,1,0:T(8,128)S(1)}, f32[2,128,256]{2,1,0:T(8,128)S(1)}, u32[]{:S(2)}, u32[]{:S(2)}) collective-permute-start(f32[2,128,256]{2,1,0:T(8,128)S(1)} %get-tuple-element.31), channel_id=1, source_target_pairs={{4,0},{8,4},{12,8},{16,12},{20,16},{24,20},{28,24},{5,1},{9,5},{13... | collective-permute-start | bytes 786440 | tf_op jit(solution)/shard_map/ppermute | solution.py:462
  11.5 13.6 %collective-permute-start.1 = (f32[2,128,256]{2,1,0:T(8,128)S(1)}, f32[2,128,256]{2,1,0:T(8,128)S(1)}, u32[]{:S(2)}, u32[]{:S(2)}) collective-permute-start(f32[2,128,256]{2,1,0:T(8,128)S(1)} %get-tuple-element.29), channel_id=1, source_target_pairs={{4,0},{8,4},{12,8},{16,12},{20,16},{24,20},{28,24},{5,1},{9,5},{13... | collective-permute-start | bytes 786440 | tf_op jit(solution)/shard_map/ppermute | solution.py:462
  15.3 12.9 %copy-start = (bf16[4,256,768]{2,1,0:T(8,128)(2,1)S(1)}, bf16[4,256,768]{2,1,0:T(8,128)(2,1)}, u32[]{:S(2)}) copy-start(bf16[4,256,768]{2,1,0:T(8,128)(2,1)} %constant.14.clone.refs_8_.refs_14_) | copy-start | bytes 4718596
  15.3 12.9 %copy-start.1 = (bf16[4,768,256]{2,1,0:T(8,128)(2,1)S(1)}, bf16[4,768,256]{2,1,0:T(8,128)(2,1)}, u32[]{:S(2)}) copy-start(bf16[4,768,256]{2,1,0:T(8,128)(2,1)} %constant.13.clone.refs_7_.refs_13_) | copy-start | bytes 4718596
  21.6 6.5 %collective-permute-start.3 = (f32[2,128,256]{2,1,0:T(8,128)S(1)}, f32[2,128,256]{2,1,0:T(8,128)}, u32[]{:S(2)}, u32[]{:S(2)}) collective-permute-start(f32[2,128,256]{2,1,0:T(8,128)S(1)} %broadcast_select_fusion.1.refs_0_), channel_id=1, source_target_pairs={{0,2},{1,3},{2,0},{3,1},{4,6},{5,7},{6,4},{7,5},{8,10},{9,11},{10,... | collective-permute-start | bytes 786440 | tf_op jit(solution)/shard_map/ppermute | solution.py:467
  25.1 2.8 %collective-permute-start.4 = (f32[2,128,256]{2,1,0:T(8,128)S(1)}, f32[2,128,256]{2,1,0:T(8,128)}, u32[]{:S(2)}, u32[]{:S(2)}) collective-permute-start(f32[2,128,256]{2,1,0:T(8,128)S(1)} %broadcast_select_fusion.1.refs_0_), channel_id=1, source_target_pairs={{0,1},{1,0},{2,3},{3,2},{4,5},{5,4},{6,7},{7,6},{8,9},{9,8},{10,11... | collective-permute-start | bytes 786440 | tf_op jit(solution)/shard_map/ppermute | solution.py:467
  25.9 2.3 %collective-permute-start.5 = (f32[2,128,256]{2,1,0:T(8,128)}, f32[2,128,256]{2,1,0:T(8,128)}, u32[]{:S(2)}, u32[]{:S(2)}) collective-permute-start(f32[2,128,256]{2,1,0:T(8,128)} %broadcast_select_fusion.refs_1_), channel_id=1, source_target_pairs={{0,1},{1,0},{2,3},{3,2},{4,5},{5,4},{6,7},{7,6},{8,9},{9,8},{10,11... | collective-permute-start | bytes 786440 | tf_op jit(solution)/shard_map/ppermute | solution.py:467
  26.4 8.5 %collective-permute-start.6 = (f32[2,128,256]{2,1,0:T(8,128)}, f32[2,128,256]{2,1,0:T(8,128)}, u32[]{:S(2)}, u32[]{:S(2)}) collective-permute-start(f32[2,128,256]{2,1,0:T(8,128)} %broadcast_select_fusion.refs_1_), channel_id=1, source_target_pairs={{0,2},{1,3},{2,0},{3,1},{4,6},{5,7},{6,4},{7,5},{8,10},{9,11},{10,... | collective-permute-start | bytes 786440 | tf_op jit(solution)/shard_map/ppermute | solution.py:467
  28.2 6.8 %collective-permute-start.7 = (f32[2,128,256]{2,1,0:T(8,128)}, f32[2,128,256]{2,1,0:T(8,128)S(1)}, u32[]{:S(2)}, u32[]{:S(2)}) collective-permute-start(f32[2,128,256]{2,1,0:T(8,128)} %collective-permute-done.3.refs_4_), channel_id=1, source_target_pairs={{0,1},{1,0},{2,3},{3,2},{4,5},{5,4},{6,7},{7,6},{8,9},{9,8},{10,11... | collective-permute-start | bytes 786440 | tf_op jit(solution)/shard_map/ppermute | solution.py:467
  34.9 1.7 %collective-permute-start.8 = (f32[2,128,256]{2,1,0:T(8,128)}, f32[2,128,256]{2,1,0:T(8,128)S(1)}, u32[]{:S(2)}, u32[]{:S(2)}) collective-permute-start(f32[2,128,256]{2,1,0:T(8,128)} %collective-permute-done.6.refs_5_), channel_id=1, source_target_pairs={{0,1},{1,0},{2,3},{3,2},{4,5},{5,4},{6,7},{7,6},{8,9},{9,8},{10,11... | collective-permute-start | bytes 786440 | tf_op jit(solution)/shard_map/ppermute | solution.py:467
  45.5 11.3 %collective-permute-start.10 = (f32[256,256]{1,0:T(8,128)S(1)}, f32[256,256]{1,0:T(8,128)S(1)}, u32[]{:S(2)}, u32[]{:S(2)}) collective-permute-start(f32[256,256]{1,0:T(8,128)S(1)} %get-tuple-element.47.re), channel_id=1, source_target_pairs={{0,4},{4,8},{8,12},{12,16},{16,20},{20,24},{24,28},{1,5},{5,9},{9,... | collective-permute-start | bytes 786440 | tf_op jit(solution)/shard_map/ppermute | solution.py:462
  50.1 10.0 %collective-permute-start.9 = (f32[256,256]{1,0:T(8,128)S(1)}, f32[256,256]{1,0:T(8,128)S(1)}, u32[]{:S(2)}, u32[]{:S(2)}) collective-permute-start(f32[256,256]{1,0:T(8,128)S(1)} %get-tuple-element.46.im), channel_id=1, source_target_pairs={{0,4},{4,8},{8,12},{12,16},{16,20},{20,24},{24,28},{1,5},{5,9},{9,... | collective-permute-start | bytes 786440 | tf_op jit(solution)/shard_map/ppermute | solution.py:462

commit v4 on v3

--- a/solution.py
+++ b/solution.py
@@ -17,23 +17,30 @@
 
 
 def dft_tables(n):
-    half = n // 2
-    k = np.arange(half)[:, None]
-    m = np.arange(half)[None, :]
-
-    def real_form(odd):
-        angle = -2 * np.pi * ((k * (2 * m + odd)) % n) / n
+    def real_form(radix, first):
+        k = np.arange(n // radix)[:, None]
+        m = np.arange(n // radix)[None, :]
+        angle = -2 * np.pi * ((k * (radix * m + first)) % n) / n
         c, s = np.cos(angle) / np.sqrt(n), np.sin(angle) / np.sqrt(n)
         return np.block([[c, s], [-s, c]])
 
-    def parts(matrix, axis):
+    def parts(matrix):
         high = matrix.astype(np.float32).astype(jnp.bfloat16)
         low = (matrix - high.astype(np.float64)).astype(np.float32).astype(jnp.bfloat16)
-        return np.concatenate([high, high, low], axis=axis)
-
-    even, odd = real_form(0), real_form(1)
-    right = np.stack([parts(m, 0) for m in (even, odd, even.T, odd.T)])
-    left = np.stack([parts(m, 1) for m in (even.T, odd.T, even, odd)])
+        return high, low
+
+    def for_right(matrix):
+        high, low = parts(matrix)
+        return np.concatenate([high, high, low], axis=0)
+
+    def for_left(matrix):
+        high, low = parts(matrix)
+        return np.block([[high, high], [low, np.zeros_like(low)]])
+
+    halves = [real_form(2, first) for first in range(2)]
+    quarters = [real_form(4, first) for first in range(4)]
+    right = np.stack([for_right(m) for m in halves + [m.T for m in halves]])
+    left = np.stack([for_left(m) for m in [m.T for m in quarters] + quarters])
     return right, left
 
 
@@ -41,40 +48,20 @@
     return pltpu.with_memory_space_constraint(x, pltpu.HBM)
 
 
-def split(x, axis):
+def split(x):
     high = x.astype(bf16)
-    low = (x - high.astype(f32)).astype(bf16)
-    return jnp.concatenate([high, low, high], axis=axis)
+    return high, (x - high.astype(f32)).astype(bf16)
 
 
 def right_dot(x, table):
-    return jnp.dot(split(x, 1), table, preferred_element_type=f32)
+    high, low = split(x)
+    return jnp.dot(jnp.concatenate([high, low, high], 1), table, preferred_element_type=f32)
 
 
 def left_dot(table, x):
-    return jnp.dot(table, split(x, 0), preferred_element_type=f32)
-
-
-def to_rows(a, b):
-    h = a.shape[0] // 2
-
-    def one(r):
-        re = jnp.concatenate([a[r : r + h, :h], b[r : r + h, :h]], 1)
-        im = jnp.concatenate([a[r : r + h, h:], b[r : r + h, h:]], 1)
-        return jnp.concatenate([re, im], 0)
-
-    return one(0), one(h)
-
-
-def to_columns(a, b):
-    h = a.shape[0] // 2
-
-    def one(c):
-        top = jnp.concatenate([a[:h, c : c + h], a[h:, c : c + h]], 1)
-        bottom = jnp.concatenate([b[:h, c : c + h], b[h:, c : c + h]], 1)
-        return jnp.concatenate([top, bottom], 0)
-
-    return one(0), one(h)
+    both = jnp.dot(table, jnp.concatenate(split(x), 0), preferred_element_type=f32)
+    h = both.shape[0] // 2
+    return both[:h] + both[h:]
 
 
 def columns_of(re, im):
@@ -96,14 +83,25 @@
 def forward(re, im, tables):
     right, left = tables
     a, b = columns_of(re, im)
-    a, b = to_rows(right_dot(a + b, right[0]), right_dot(a - b, right[1]))
-    return left_dot(left[0], a + b), left_dot(left[1], a - b)
-
-
-def inverse(a, b, tables):
+    re, im = planes_of(right_dot(a + b, right[0]), right_dot(a - b, right[1]))
+    q = re.shape[0] // 4
+    (r0, r1, r2, r3), (i0, i1, i2, i3) = [[x[j * q : (j + 1) * q] for j in range(4)] for x in (re, im)]
+    pr, pi, ur, ui = r0 + r2, i0 + i2, r0 - r2, i0 - i2
+    qr, qi, vr, vi = r1 + r3, i1 + i3, r1 - r3, i1 - i3
+    mixed = ((pr + qr, pi + qi), (ur + vi, ui - vr), (pr - qr, pi - qi), (ur - vi, ui + vr))
+    return [left_dot(left[j], jnp.concatenate(x, 0)) for j, x in enumerate(mixed)]
+
+
+def inverse(spectrum, tables):
     right, left = tables
-    p, q = left_dot(left[2], a), left_dot(left[3], b)
-    a, b = to_columns(p + q, p - q)
+    q = spectrum[0].shape[0] // 2
+    parts = [left_dot(left[4 + j], x) for j, x in enumerate(spectrum)]
+    (r0, i0), (r1, i1), (r2, i2), (r3, i3) = [(x[:q], x[q:]) for x in parts]
+    ar, ai, br, bi = r0 + r2, i0 + i2, r0 - r2, i0 - i2
+    cr, ci, dr, di = r1 + r3, i1 + i3, r1 - r3, i1 - i3
+    re = jnp.concatenate([ar + cr, br - di, ar - cr, br + di], 0)
+    im = jnp.concatenate([ai + ci, bi + dr, ai - ci, bi - dr], 0)
+    a, b = columns_of(re, im)
     p, q = right_dot(a, right[2]), right_dot(b, right[3])
     return planes_of(p + q, p - q)
 
@@ -116,22 +114,21 @@
     return ar * br + ai * bi, ar * bi - ai * br
 
 
-def by_phase(a, b, cosine, sine):
-    h = a.shape[0] // 2
+def by_phase(spectrum, cosine, sine):
+    q = spectrum[0].shape[0] // 2
     out = []
-    for i, x in enumerate((a, b)):
-        at = slice(i * h, (i + 1) * h)
-        re, im = times(x[:h], x[h:], cosine[at], sine[at])
-        out.append(jnp.concatenate([re, im], 0))
+    for i, x in enumerate(spectrum):
+        at = slice(i * q, (i + 1) * q)
+        out.append(jnp.concatenate(times(x[:q], x[q:], cosine[at], sine[at]), 0))
     return out
 
 
-def by_residual(a, b, observed):
-    h = a.shape[0] // 2
+def by_residual(spectrum, observed):
+    q = spectrum[0].shape[0] // 2
     out = []
-    for i, x in enumerate((a, b)):
-        re, im = x[:h], x[h:]
-        residual = re * re + im * im - observed[i * h : (i + 1) * h]
+    for i, x in enumerate(spectrum):
+        re, im = x[:q], x[q:]
+        residual = re * re + im * im - observed[i * q : (i + 1) * q]
         out.append(jnp.concatenate([residual * re, residual * im], 0))
     return out
 
@@ -143,9 +140,8 @@
         observed, outs, (held, sem) = refs[: len(patterns)], refs[len(patterns) : -2], refs[-2:]
         row = lax.broadcasted_iota(jnp.int32, (n, n), 0)
         column = lax.broadcasted_iota(jnp.int32, (n, n), 1)
-        half = n // 2
-        from_row = jnp.where(row < half, 2 * row, 2 * (row - half) + 1)
-        from_column = jnp.where(column < half, 2 * column, 2 * (column - half) + 1)
+        from_row = row % (n // 4) * 4 + row // (n // 4)
+        from_column = column % (n // 2) * 2 + column // (n // 2)
         left = jnp.where(column == from_row, 1.0, 0.0).astype(bf16)
         right = jnp.where(row == from_column, 1.0, 0.0).astype(bf16)
 
@@ -184,9 +180,8 @@
 
 def run_forward(s, before, patch, after, cosine, sine, tables):
     re, im = times(before[0], before[1], patch[0], patch[1])
-    a, b = forward(re, im, tables)
-    a, b = by_phase(a, b, cosine[...], sine[...])
-    re, im = inverse(a, b, tables)
+    spectrum = by_phase(forward(re, im, tables), cosine[...], sine[...])
+    re, im = inverse(spectrum, tables)
     after[0] = re
     after[1] = im
 
@@ -290,9 +285,8 @@
                 @pl.when(me < s)
                 def _():
                     gr, gi = conj_times(patch[s, 0], patch[s, 1], re, im)
-                    a, b = forward(gr, gi, tables)
-                    a, b = by_phase(a, b, cosine[...], -sine[...])
-                    back(s - 1, *inverse(a, b, tables))
+                    spectrum = by_phase(forward(gr, gi, tables), cosine[...], -sine[...])
+                    back(s - 1, *inverse(spectrum, tables))
 
         early_copy = pltpu.make_async_copy(planes[4], waves.at[pl.ds(0, 2)], early_sem)
 
@@ -333,9 +327,8 @@
 
         last = sections - 1
         re, im = times(wave(last)[0], wave(last)[1], patch[last, 0], patch[last, 1])
-        a, b = forward(re, im, tables)
-        a, b = by_residual(a, b, observed[...])
-        back(last, *inverse(a, b, tables))
+        spectrum = by_residual(forward(re, im, tables), observed[...])
+        back(last, *inverse(spectrum, tables))
 
     return pl.pallas_call(
         kernel,
@@ -375,21 +368,32 @@
     )(row_off, col_off)
 
 
+def staged(strip):
+    def kernel(strip, out, sem):
+        copy = pltpu.make_async_copy(strip, out, sem)
+        copy.start()
+        copy.wait()
+
+    return pl.pallas_call(
+        kernel,
+        out_shape=pltpu.VMEM(strip.shape, f32),
+        in_specs=[ANY],
+        out_specs=VMEM,
+        scratch_shapes=[pltpu.SemaphoreType.DMA],
+        compiler_params=PARAMS,
+    )(pinned(strip))
+
+
 def cut_window(offsets, strip, width, bounds):
     _, _, rows, columns = strip.shape
     chunks = len(bounds) - 1
 
-    def kernel(offsets, strip, *refs):
-        outs, (wide, sem) = refs[:chunks], refs[chunks:]
+    def kernel(offsets, strip, *outs):
         row, column = offsets[0], offsets[1]
         start, shift = window_start(column, width, columns)
-        run = pl.ds(start, width + LANE)
-        copies = [pltpu.make_async_copy(strip.at[0, c, :, run], wide.at[c], sem.at[c]) for c in range(2)]
-        for copy in copies:
-            copy.start()
         for c in range(2):
-            copies[c].wait()
-            x = pltpu.roll(wide[c], lax.rem(width + LANE - shift, width + LANE), 1)[:, :width]
+            x = strip[0, c, :, pl.ds(start, width + LANE)]
+            x = pltpu.roll(x, lax.rem(width + LANE - shift, width + LANE), 1)[:, :width]
             x = pltpu.roll(x, lax.rem(rows - row, rows), 0)
             for j in range(chunks):
                 outs[j][c] = x[bounds[j] : bounds[j + 1]]
@@ -397,11 +401,10 @@
     return pl.pallas_call(
         kernel,
         out_shape=[jax.ShapeDtypeStruct((2, bounds[j + 1] - bounds[j], width), f32) for j in range(chunks)],
-        in_specs=[SMEM, ANY],
+        in_specs=[SMEM, VMEM],
         out_specs=[VMEM] * chunks,
-        scratch_shapes=[pltpu.VMEM((2, rows, width + LANE), f32), pltpu.SemaphoreType.DMA((2,))],
-        compiler_params=PARAMS,
-    )(offsets, pinned(strip))
+        compiler_params=PARAMS,
+    )(offsets, strip)
 
 
 def moved(piece, row, shift, keep):
@@ -484,11 +487,12 @@
     width = probe.shape[1]
     cut = lax.axis_index("cuts").astype(jnp.int32).reshape(1)
     offsets = packed(row_off, col_off)
+    strip = staged(transmission)
     came_offsets = shifted(offsets, 1)
     cosine, sine, observed = prepare(prop_phase, measured)
-    bands = list(cut_window(came_offsets, transmission, width, BOUNDS))
+    bands = list(cut_window(came_offsets, strip, width, BOUNDS))
     below = [shifted(band, -1) for band in bands]
-    own = cut_window(offsets, transmission, width, BOUNDS)
+    own = cut_window(offsets, strip, width, BOUNDS)
     tables = [jnp.asarray(t) for t in dft_tables(width)]
 
     chunks, across = [], []

time: 62.5 us -> 59.9 us (0.958)
  Pallas kernels: 26.4 us -> 24.1 us
  waiting for transfers between devices: 13.8 us -> 15.3 us
  other arithmetic: 0.9 us -> 0.2 us
  starting transfers between devices: 19 us -> 18.3 us
    pallas_call x2, Pallas kernels: 4.4 us -> 1.85 us  [cut_window(): pl.pallas_call(kernel, out_shape=[jax.ShapeDtypeStruct((2, bounds[j + 1]...]
    pallas_call x0 -> x1, Pallas kernels: none -> 1.6 us  [staged(): pl.pallas_call(kernel, out_shape=pltpu.VMEM(strip.shape, f32), in_specs=[...]
    ppermute x5, waiting for transfers between devices: 9.51 us -> 10.7 us  [shifted(): return lax.ppermute(value, 'tile', pairs)]
    pallas_call x1, Pallas kernels: 8.83 us -> 7.94 us  [chain(): pl.pallas_call(kernel, out_shape=[jax.ShapeDtypeStruct((n, n), f32)] * 2,...]
    ppermute x5, starting transfers between devices: 15.4 us -> 14.7 us  [shifted(): return lax.ppermute(value, 'tile', pairs)]
    select_n x2, other arithmetic: 0.88 us -> 0.18 us  [merged(): return jnp.where(index < rows - row, first, second)]
  transfers between devices with their start and end apart: 11 -> 11, of which waited for: 8 -> 7; matrix products, arithmetic and copies ran while one was open for 1% -> 0% of each run, Pallas kernels for 22% -> 22%
where the time goes in v4:
time: 59.9 us; the launch traced here: 59.5 us
  Pallas kernels  24.1 us (40%)
  starting transfers between devices  18.3 us (31%)
  waiting for transfers between devices  15.3 us (26%)
  between operations  1.5 us (3%)
    ppermute x5, starting transfers between devices, shifted(): return lax.ppermute(value, 'tile', pairs)  14.7 us
    ppermute x5, waiting for transfers between devices, shifted(): return lax.ppermute(value, 'tile', pairs)  10.7 us
    pallas_call x1, Pallas kernels, chain(): pl.pallas_call(kernel, out_shape=[jax.ShapeDtypeStruct((n, n), f32)] * 2,...  7.94 us
    ppermute x6, waiting for transfers between devices, swapped(): return lax.ppermute(value, 'cuts', [(i, i ^ bit) for i in range(devices)])  4.59 us
    pallas_call x1, Pallas kernels, early_waves(): pl.pallas_call(kernel, out_shape=jax.ShapeDtypeStruct((2, 2, n, n), f32),...  4.03 us
    ppermute x6, starting transfers between devices, swapped(): return lax.ppermute(value, 'cuts', [(i, i ^ bit) for i in range(devices)])  3.63 us
    pallas_call x2, Pallas kernels, add_came(): pl.pallas_call(kernel, out_shape=jax.ShapeDtypeStruct(base.shape, f32), i...  3.18 us
    pallas_call x1, Pallas kernels, place_own(): pl.pallas_call(kernel, out_shape=[jax.ShapeDtypeStruct((1, 2, rows, colum...  2.49 us
  transfers between devices with their start and end apart: 11, of which 7 were waited for; matrix products, arithmetic and copies ran while one was open for 0% of the time, Pallas kernels for 22%

profile of v4, /device:TPU:0, one launch (start us, length us, event | category | flops | bytes accessed | tf_op | source)
XLA Modules:
  0.0 59.5 jit_solution(14720941727892812245)
XLA Ops:
  1.3 0.6 shard_map.82.offsets
  1.9 4.9 %collective-permute-start = (s32[2]{0:T(128)S(1)}, s32[2]{0:T(128)S(1)}, u32[]{:S(2)}, u32[]{:S(2)}) collective-permute-start(s32[2]{0:T(128)S(1)} %shard_map.82.offsets), channel_id=1, source_target_pairs={{0,4},{4,8},{8,12},{12,16},{16,20},{20,24},{24,28},{1,5},{5,9},{9,... | collective-permute-start | bytes 32 | tf_op jit(solution)/shard_map/ppermute | solution.py:465
  6.8 1.6 %shard_map.83.strip = f32[1,2,256,1024]{3,2,1,0:T(8,128)S(1)} custom-call(f32[1,2,256,1024]{3,2,1,0:T(8,128)} %strip.1), custom_call_target="tpu_custom_call" | custom-call | tf_op jit(solution)/shard_map/pallas_call | solution.py:377
  8.4 0.0 copy-start.2
  8.4 0.0 copy-start.3
  8.4 0.0 collective-permute-done.offsets.came_offsets
  8.4 0.9 %shard_map.85 = (f32[2,128,256]{2,1,0:T(8,128)S(1)}, f32[2,128,256]{2,1,0:T(8,128)S(1)}) custom-call(s32[2]{0:T(128)S(1)} %collective-permute-done.offsets.came_offsets, f32[1,2,256,1024]{3,2,1,0:T(8,128)S(1)} %shard_map.83.strip), custom_call_target="tpu_custom_call" | custom-call | tf_op jit(solution)/shard_map/pallas_call | solution.py:401
  9.4 1.3 %collective-permute-start.2 = (f32[2,128,256]{2,1,0:T(8,128)S(1)}, f32[2,128,256]{2,1,0:T(8,128)S(1)}, u32[]{:S(2)}, u32[]{:S(2)}) collective-permute-start(f32[2,128,256]{2,1,0:T(8,128)S(1)} %get-tuple-element.31), channel_id=1, source_target_pairs={{4,0},{8,4},{12,8},{16,12},{20,16},{24,20},{28,24},{5,1},{9,5},{13... | collective-permute-start | bytes 786440 | tf_op jit(solution)/shard_map/ppermute | solution.py:465
  10.7 1.3 %collective-permute-start.1 = (f32[2,128,256]{2,1,0:T(8,128)S(1)}, f32[2,128,256]{2,1,0:T(8,128)S(1)}, u32[]{:S(2)}, u32[]{:S(2)}) collective-permute-start(f32[2,128,256]{2,1,0:T(8,128)S(1)} %get-tuple-element.29), channel_id=1, source_target_pairs={{4,0},{8,4},{12,8},{16,12},{20,16},{24,20},{28,24},{5,1},{9,5},{13... | collective-permute-start | bytes 786440 | tf_op jit(solution)/shard_map/ppermute | solution.py:465
  12.0 2.4 %shard_map.86 = (f32[256,256]{1,0:T(8,128)}, f32[256,256]{1,0:T(8,128)}, f32[256,256]{1,0:T(8,128)}) custom-call(f32[256,256]{1,0:T(8,128)S(1)} %copy-done.2, f32[1,256,256]{2,1,0:T(8,128)S(1)} %copy-done.3), custom_call_target="tpu_custom_call" | custom-call | flops 603979776 | bytes 1966080 | tf_op jit(solution)/shard_map/pallas_call | solution.py:170
  14.4 0.0 copy-start
  14.5 0.0 copy-start.1
  14.5 0.9 %shard_map.84 = (f32[2,128,256]{2,1,0:T(8,128)S(1)}, f32[2,128,256]{2,1,0:T(8,128)S(1)}) custom-call(s32[2]{0:T(128)S(1)} %shard_map.82.offsets, f32[1,2,256,1024]{3,2,1,0:T(8,128)S(1)} %shard_map.83.strip), custom_call_target="tpu_custom_call" | custom-call | tf_op jit(solution)/shard_map/pallas_call | solution.py:401
  15.4 5.1 %collective-permute-done.2 = f32[2,128,256]{2,1,0:T(8,128)S(1)} collective-permute-done((f32[2,128,256]{2,1,0:T(8,128)S(1)}, f32[2,128,256]{2,1,0:T(8,128)S(1)}, u32[]{:S(2)}, u32[]{:S(2)}) %collective-permute-start.2) | collective-permute-done | bytes 262176 | tf_op jit(solution)/shard_map/ppermute | solution.py:465
  20.5 0.1 broadcast_select_fusion.1.refs_0_
  20.6 1.6 %collective-permute-start.3 = (f32[2,128,256]{2,1,0:T(8,128)S(1)}, f32[2,128,256]{2,1,0:T(8,128)}, u32[]{:S(2)}, u32[]{:S(2)}) collective-permute-start(f32[2,128,256]{2,1,0:T(8,128)S(1)} %broadcast_select_fusion.1.refs_0_), channel_id=1, source_target_pairs={{0,2},{1,3},{2,0},{3,1},{4,6},{5,7},{6,4},{7,5},{8,10},{9,11},{10,... | collective-permute-start | bytes 786440 | tf_op jit(solution)/shard_map/ppermute | solution.py:470
  22.1 2.5 %collective-permute-done.1 = f32[2,128,256]{2,1,0:T(8,128)S(1)} collective-permute-done((f32[2,128,256]{2,1,0:T(8,128)S(1)}, f32[2,128,256]{2,1,0:T(8,128)S(1)}, u32[]{:S(2)}, u32[]{:S(2)}) %collective-permute-start.1) | collective-permute-done | bytes 262176 | tf_op jit(solution)/shard_map/ppermute | solution.py:465
  24.6 0.1 broadcast_select_fusion.refs_1_
  24.7 0.6 collective-permute-start.5
  25.3 1.5 %collective-permute-start.6 = (f32[2,128,256]{2,1,0:T(8,128)S(1)}, f32[2,128,256]{2,1,0:T(8,128)}, u32[]{:S(2)}, u32[]{:S(2)}) collective-permute-start(f32[2,128,256]{2,1,0:T(8,128)S(1)} %broadcast_select_fusion.refs_1_), channel_id=1, source_target_pairs={{0,2},{1,3},{2,0},{3,1},{4,6},{5,7},{6,4},{7,5},{8,10},{9,11},{10,... | collective-permute-start | bytes 786440 | tf_op jit(solution)/shard_map/ppermute | solution.py:470
  26.8 0.3 collective-permute-done.3.refs_4_
  27.1 4.0 %shard_map.87.refs_12_ = f32[2,2,256,256]{3,2,1,0:T(8,128)S(1)} custom-call(s32[1]{0:T(128)} %bitcast.cut_ref, f32[2,128,256]{2,1,0:T(8,128)S(1)} %broadcast_select_fusion.1.refs_0_, f32[2,128,256]{2,1,0:T(8,128)S(1)} %broadcast_select_fusion.refs_1_, f32[2,128,256]{2,1,0:T(8,128)S(1)} %collective-permute-done.4.refs_2_, ...), custom_call_target="tpu_custom_call" | custom-call | flops 65536 | bytes 4096 | tf_op jit(solution)/shard_map/pallas_call | solution.py:235
  31.2 2.5 %collective-permute-done.6.refs_5_ = f32[2,128,256]{2,1,0:T(8,128)} collective-permute-done((f32[2,128,256]{2,1,0:T(8,128)S(1)}, f32[2,128,256]{2,1,0:T(8,128)}, u32[]{:S(2)}, u32[]{:S(2)}) %collective-permute-start.6) | collective-permute-done | bytes 262176 | tf_op jit(solution)/shard_map/ppermute | solution.py:470
  33.7 1.7 %collective-permute-done.8.refs_7_ = f32[2,128,256]{2,1,0:T(8,128)S(1)} collective-permute-done((f32[2,128,256]{2,1,0:T(8,128)}, f32[2,128,256]{2,1,0:T(8,128)S(1)}, u32[]{:S(2)}, u32[]{:S(2)}) %collective-permute-start.8) | collective-permute-done | bytes 262176 | tf_op jit(solution)/shard_map/ppermute | solution.py:470
  35.5 7.9 %shard_map.88 = (f32[256,256]{1,0:T(8,128)S(1)}, f32[256,256]{1,0:T(8,128)S(1)}) custom-call(s32[1]{0:T(128)} %bitcast.cut_ref, f32[2,128,256]{2,1,0:T(8,128)S(1)} %broadcast_select_fusion.1.refs_0_, f32[2,128,256]{2,1,0:T(8,128)S(1)} %broadcast_select_fusion.refs_1_, f32[2,128,256]{2,1,0:T(8,128)S(1)} %collective-permute-done.4.refs_2_, ...), custom_call_target="tpu_custom_call" | custom-call | flops 4026531840 | bytes 1048576 | tf_op jit(solution)/shard_map/pallas_call | solution.py:333
  43.4 4.3 %collective-permute-start.10 = (f32[256,256]{1,0:T(8,128)S(1)}, f32[256,256]{1,0:T(8,128)S(1)}, u32[]{:S(2)}, u32[]{:S(2)}) collective-permute-start(f32[256,256]{1,0:T(8,128)S(1)} %get-tuple-element.47.re), channel_id=1, source_target_pairs={{0,4},{4,8},{8,12},{12,16},{16,20},{20,24},{24,28},{1,5},{5,9},{9,... | collective-permute-start | bytes 786440 | tf_op jit(solution)/shard_map/ppermute | solution.py:465
  47.7 2.9 %collective-permute-start.9 = (f32[256,256]{1,0:T(8,128)S(1)}, f32[256,256]{1,0:T(8,128)S(1)}, u32[]{:S(2)}, u32[]{:S(2)}) collective-permute-start(f32[256,256]{1,0:T(8,128)S(1)} %get-tuple-element.46.im), channel_id=1, source_target_pairs={{0,4},{4,8},{8,12},{12,16},{16,20},{20,24},{24,28},{1,5},{5,9},{9,... | collective-permute-start | bytes 786440 | tf_op jit(solution)/shard_map/ppermute | solution.py:465
  50.7 2.5 %shard_map.89 = (f32[1,2,256,1024]{3,2,1,0:T(8,128)}, f32[256,384]{1,0:T(8,128)S(1)}, f32[256,384]{1,0:T(8,128)S(1)}) custom-call(s32[2]{0:T(128)S(1)} %shard_map.82.offsets, s32[2]{0:T(128)S(1)} %collective-permute-done.offsets.came_offsets, f32[256,256]{1,0:T(8,128)S(1)} %get-tuple-element.47.re, f32[256,256]{1,0:T(8,128)S(1)} %get-tuple-element.46.im), custom_call_target="tpu_custom_call" | custom-call | tf_op jit(solution)/shard_map/pallas_call | solution.py:429
  53.2 1.3 %collective-permute-done.10.came = f32[256,256]{1,0:T(8,128)S(1)} collective-permute-done((f32[256,256]{1,0:T(8,128)S(1)}, f32[256,256]{1,0:T(8,128)S(1)}, u32[]{:S(2)}, u32[]{:S(2)}) %collective-permute-start.10) | collective-permute-done | bytes 262176 | tf_op jit(solution)/shard_map/ppermute | solution.py:465
  54.5 1.6 %shard_map.90.base = f32[1,2,256,1024]{3,2,1,0:T(8,128)} custom-call(s32[2]{0:T(128)S(1)} %collective-permute-done.offsets.came_offsets, f32[256,256]{1,0:T(8,128)S(1)} %collective-permute-done.10.came, f32[256,384]{1,0:T(8,128)S(1)} %get-tuple-element.49.run, f32[1,2,256,1024]{3,2,1,0:T(8,128)} %get-tuple-element.50.base), custom_call_target="tpu_custom_call", output_to_operand_aliasing={{}: (3, {})} | custom-call | tf_op jit(solution)/shard_map/pallas_call | solution.py:451
  56.1 1.8 %collective-permute-done.9.came = f32[256,256]{1,0:T(8,128)S(1)} collective-permute-done((f32[256,256]{1,0:T(8,128)S(1)}, f32[256,256]{1,0:T(8,128)S(1)}, u32[]{:S(2)}, u32[]{:S(2)}) %collective-permute-start.9) | collective-permute-done | bytes 262176 | tf_op jit(solution)/shard_map/ppermute | solution.py:465
  57.9 1.6 %shard_map.91 = f32[1,2,256,1024]{3,2,1,0:T(8,128)} custom-call(s32[2]{0:T(128)S(1)} %collective-permute-done.offsets.came_offsets, f32[256,256]{1,0:T(8,128)S(1)} %collective-permute-done.9.came, f32[256,384]{1,0:T(8,128)S(1)} %get-tuple-element.48.run, f32[1,2,256,1024]{3,2,1,0:T(8,128)} %shard_map.90.base), custom_call_target="tpu_custom_call", output_to_operand_aliasing={{}: (3, {})} | custom-call | tf_op jit(solution)/shard_map/pallas_call | solution.py:451
  (12 shorter events, 0.0 us)
Async XLA Ops:
  1.9 6.5 %collective-permute-start = (s32[2]{0:T(128)S(1)}, s32[2]{0:T(128)S(1)}, u32[]{:S(2)}, u32[]{:S(2)}) collective-permute-start(s32[2]{0:T(128)S(1)} %shard_map.82.offsets), channel_id=1, source_target_pairs={{0,4},{4,8},{8,12},{12,16},{16,20},{20,24},{24,28},{1,5},{5,9},{9,... | collective-permute-start | bytes 32 | tf_op jit(solution)/shard_map/ppermute | solution.py:465
  8.4 3.6 %copy-start.2 = (f32[256,256]{1,0:T(8,128)S(1)}, f32[256,256]{1,0:T(8,128)}, u32[]{:S(2)}) copy-start(f32[256,256]{1,0:T(8,128)} %phase.1) | copy-start | bytes 786436
  8.4 3.6 %copy-start.3 = (f32[1,256,256]{2,1,0:T(8,128)S(1)}, f32[1,256,256]{2,1,0:T(8,128)}, u32[]{:S(2)}) copy-start(f32[1,256,256]{2,1,0:T(8,128)} %refs_0_.1) | copy-start | bytes 786436
  9.4 11.1 %collective-permute-start.2 = (f32[2,128,256]{2,1,0:T(8,128)S(1)}, f32[2,128,256]{2,1,0:T(8,128)S(1)}, u32[]{:S(2)}, u32[]{:S(2)}) collective-permute-start(f32[2,128,256]{2,1,0:T(8,128)S(1)} %get-tuple-element.31), channel_id=1, source_target_pairs={{4,0},{8,4},{12,8},{16,12},{20,16},{24,20},{28,24},{5,1},{9,5},{13... | collective-permute-start | bytes 786440 | tf_op jit(solution)/shard_map/ppermute | solution.py:465
  10.7 13.9 %collective-permute-start.1 = (f32[2,128,256]{2,1,0:T(8,128)S(1)}, f32[2,128,256]{2,1,0:T(8,128)S(1)}, u32[]{:S(2)}, u32[]{:S(2)}) collective-permute-start(f32[2,128,256]{2,1,0:T(8,128)S(1)} %get-tuple-element.29), channel_id=1, source_target_pairs={{4,0},{8,4},{12,8},{16,12},{20,16},{24,20},{28,24},{5,1},{9,5},{13... | collective-permute-start | bytes 786440 | tf_op jit(solution)/shard_map/ppermute | solution.py:465
  14.4 12.7 %copy-start = (bf16[4,768,256]{2,1,0:T(8,128)(2,1)S(1)}, bf16[4,768,256]{2,1,0:T(8,128)(2,1)}, u32[]{:S(2)}) copy-start(bf16[4,768,256]{2,1,0:T(8,128)(2,1)} %constant.13.clone.refs_7_.refs_13_) | copy-start | bytes 4718596
  14.5 12.7 %copy-start.1 = (bf16[8,256,256]{2,1,0:T(8,128)(2,1)S(1)}, bf16[8,256,256]{2,1,0:T(8,128)(2,1)}, u32[]{:S(2)}) copy-start(bf16[8,256,256]{2,1,0:T(8,128)(2,1)} %constant.14.clone.refs_8_.refs_14_) | copy-start | bytes 3145732
  20.6 6.5 %collective-permute-start.3 = (f32[2,128,256]{2,1,0:T(8,128)S(1)}, f32[2,128,256]{2,1,0:T(8,128)}, u32[]{:S(2)}, u32[]{:S(2)}) collective-permute-start(f32[2,128,256]{2,1,0:T(8,128)S(1)} %broadcast_select_fusion.1.refs_0_), channel_id=1, source_target_pairs={{0,2},{1,3},{2,0},{3,1},{4,6},{5,7},{6,4},{7,5},{8,10},{9,11},{10,... | collective-permute-start | bytes 786440 | tf_op jit(solution)/shard_map/ppermute | solution.py:470
  24.6 2.2 %collective-permute-start.4 = (f32[2,128,256]{2,1,0:T(8,128)S(1)}, f32[2,128,256]{2,1,0:T(8,128)S(1)}, u32[]{:S(2)}, u32[]{:S(2)}) collective-permute-start(f32[2,128,256]{2,1,0:T(8,128)S(1)} %broadcast_select_fusion.1.refs_0_), channel_id=1, source_target_pairs={{0,1},{1,0},{2,3},{3,2},{4,5},{5,4},{6,7},{7,6},{8,9},{9,8},{10,11... | collective-permute-start | bytes 786440 | tf_op jit(solution)/shard_map/ppermute | solution.py:470
  24.7 2.4 %collective-permute-start.5 = (f32[2,128,256]{2,1,0:T(8,128)S(1)}, f32[2,128,256]{2,1,0:T(8,128)}, u32[]{:S(2)}, u32[]{:S(2)}) collective-permute-start(f32[2,128,256]{2,1,0:T(8,128)S(1)} %broadcast_select_fusion.refs_1_), channel_id=1, source_target_pairs={{0,1},{1,0},{2,3},{3,2},{4,5},{5,4},{6,7},{7,6},{8,9},{9,8},{10,11... | collective-permute-start | bytes 786440 | tf_op jit(solution)/shard_map/ppermute | solution.py:470
  25.3 8.4 %collective-permute-start.6 = (f32[2,128,256]{2,1,0:T(8,128)S(1)}, f32[2,128,256]{2,1,0:T(8,128)}, u32[]{:S(2)}, u32[]{:S(2)}) collective-permute-start(f32[2,128,256]{2,1,0:T(8,128)S(1)} %broadcast_select_fusion.refs_1_), channel_id=1, source_target_pairs={{0,2},{1,3},{2,0},{3,1},{4,6},{5,7},{6,4},{7,5},{8,10},{9,11},{10,... | collective-permute-start | bytes 786440 | tf_op jit(solution)/shard_map/ppermute | solution.py:470
  27.1 6.6 %collective-permute-start.7 = (f32[2,128,256]{2,1,0:T(8,128)}, f32[2,128,256]{2,1,0:T(8,128)S(1)}, u32[]{:S(2)}, u32[]{:S(2)}) collective-permute-start(f32[2,128,256]{2,1,0:T(8,128)} %collective-permute-done.3.refs_4_), channel_id=1, source_target_pairs={{0,1},{1,0},{2,3},{3,2},{4,5},{5,4},{6,7},{7,6},{8,9},{9,8},{10,11... | collective-permute-start | bytes 786440 | tf_op jit(solution)/shard_map/ppermute | solution.py:470
  33.7 1.7 %collective-permute-start.8 = (f32[2,128,256]{2,1,0:T(8,128)}, f32[2,128,256]{2,1,0:T(8,128)S(1)}, u32[]{:S(2)}, u32[]{:S(2)}) collective-permute-start(f32[2,128,256]{2,1,0:T(8,128)} %collective-permute-done.6.refs_5_), channel_id=1, source_target_pairs={{0,1},{1,0},{2,3},{3,2},{4,5},{5,4},{6,7},{7,6},{8,9},{9,8},{10,11... | collective-permute-start | bytes 786440 | tf_op jit(solution)/shard_map/ppermute | solution.py:470
  43.4 11.1 %collective-permute-start.10 = (f32[256,256]{1,0:T(8,128)S(1)}, f32[256,256]{1,0:T(8,128)S(1)}, u32[]{:S(2)}, u32[]{:S(2)}) collective-permute-start(f32[256,256]{1,0:T(8,128)S(1)} %get-tuple-element.47.re), channel_id=1, source_target_pairs={{0,4},{4,8},{8,12},{12,16},{16,20},{20,24},{24,28},{1,5},{5,9},{9,... | collective-permute-start | bytes 786440 | tf_op jit(solution)/shard_map/ppermute | solution.py:465
  47.7 10.2 %collective-permute-start.9 = (f32[256,256]{1,0:T(8,128)S(1)}, f32[256,256]{1,0:T(8,128)S(1)}, u32[]{:S(2)}, u32[]{:S(2)}) collective-permute-start(f32[256,256]{1,0:T(8,128)S(1)} %get-tuple-element.46.im), channel_id=1, source_target_pairs={{0,4},{4,8},{8,12},{12,16},{16,20},{20,24},{24,28},{1,5},{5,9},{9,... | collective-permute-start | bytes 786440 | tf_op jit(solution)/shard_map/ppermute | solution.py:465

commit v5 on v4

--- a/solution.py
+++ b/solution.py
@@ -178,9 +178,12 @@
     )(prop_phase, *patterns)
 
 
-def run_forward(s, before, patch, after, cosine, sine, tables):
+def run_forward(s, before, patch, after, cosine, sine, tables, ready=None):
     re, im = times(before[0], before[1], patch[0], patch[1])
-    spectrum = by_phase(forward(re, im, tables), cosine[...], sine[...])
+    spectrum = forward(re, im, tables)
+    if ready is not None:
+        ready()
+    spectrum = by_phase(spectrum, cosine[...], sine[...])
     re, im = inverse(spectrum, tables)
     after[0] = re
     after[1] = im
@@ -271,10 +274,6 @@
         def wave(s):
             return probe if s == 0 else waves.at[s - 1]
 
-        def first_two():
-            for s in range(2):
-                run_forward(s, wave(s), patch.at[s], waves.at[s], cosine, sine, tables)
-
         def back(s, re, im):
             @pl.when(me == s)
             def _():
@@ -288,40 +287,55 @@
                     spectrum = by_phase(forward(gr, gi, tables), cosine[...], -sine[...])
                     back(s - 1, *inverse(spectrum, tables))
 
-        early_copy = pltpu.make_async_copy(planes[4], waves.at[pl.ds(0, 2)], early_sem)
-
-        fetch_patches(me, sources, patch, sems, (2, 3))
+        early_copies = [pltpu.make_async_copy(planes[4].at[s], waves.at[s], early_sem.at[s]) for s in range(2)]
+        for odd in range(2):
+
+            @pl.when(me % 2 == odd)
+            def _(odd=odd):
+                fetch_patches(me, sources, patch, sems, (2 + odd,))
 
         @pl.when(me < 2)
         def _():
-            early_copy.start()
-
-        for copy in copies:
-            copy.start()
+            early_copies[1].start()
+
+        for i in (3, 0, 1, 2):
+            copies[i].start()
+        for odd in range(2):
+
+            @pl.when(me % 2 == odd)
+            def _(odd=odd):
+                fetch_patches(me, sources, patch, sems, (3 - odd,))
+
         fetch_patches(me, sources, patch, sems, (0, 1))
-        for copy in copies[:2]:
-            copy.wait()
+
+        def wait_phase():
+            for copy in copies[:2]:
+                copy.wait()
 
         @pl.when(me < 2)
         def _():
-            early_copy.wait()
+            early_copies[0].start()
+            early_copies[1].wait()
 
         @pl.when(me >= 2)
         def _():
             copies[3].wait()
             for s in range(2):
                 wait_slot(patch, s, sems.at[s])
-            first_two()
+                ready = wait_phase if s == 0 else None
+                run_forward(s, wave(s), patch.at[s], waves.at[s], cosine, sine, tables, ready)
 
         for s in range(2, sections):
             wait_slot(patch, s, sems.at[s])
             if s < sections - 1:
-                run_forward(s, wave(s), patch.at[s], waves.at[s], cosine, sine, tables)
+                ready = (lambda: pl.when(me < 2)(wait_phase)) if s == 2 else None
+                run_forward(s, wave(s), patch.at[s], waves.at[s], cosine, sine, tables, ready)
         copies[2].wait()
 
         @pl.when(me < 2)
         def _():
             copies[3].wait()
+            early_copies[0].wait()
             for s in range(2):
                 wait_slot(patch, s, sems.at[s])
 
@@ -341,7 +355,7 @@
             pltpu.VMEM((3, n, n), f32),
             pltpu.VMEM((2, n, n), f32),
             pltpu.SemaphoreType.DMA((sections,)),
-            pltpu.SemaphoreType.DMA,
+            pltpu.SemaphoreType.DMA((2,)),
             pltpu.SemaphoreType.DMA((4,)),
         ],
         compiler_params=PARAMS,
@@ -352,20 +366,6 @@
 def window_start(column, width, columns):
     start = jnp.minimum(column // LANE * LANE, columns - width - LANE)
     return pl.multiple_of(start, LANE), column - start
-
-
-def packed(row_off, col_off):
-    def kernel(row_off, col_off, out):
-        out[0] = row_off[0]
-        out[1] = col_off[0]
-
-    return pl.pallas_call(
-        kernel,
-        out_shape=jax.ShapeDtypeStruct((2,), jnp.int32),
-        in_specs=[SMEM, SMEM],
-        out_specs=SMEM,
-        compiler_params=PARAMS,
-    )(row_off, col_off)
 
 
 def staged(strip):
@@ -479,14 +479,14 @@
     return jnp.where(index < rows - row, first, second)
 
 
-BOUNDS = (0, 128, 256)
+BOUNDS = (0, 144, 256)
 
 
 def per_device(transmission, probe, prop_phase, row_off, col_off, measured):
     rows, columns = transmission.shape[2:]
     width = probe.shape[1]
     cut = lax.axis_index("cuts").astype(jnp.int32).reshape(1)
-    offsets = packed(row_off, col_off)
+    offsets = jnp.concatenate([row_off, col_off])
     strip = staged(transmission)
     came_offsets = shifted(offsets, 1)
     cosine, sine, observed = prepare(prop_phase, measured)

time: 59.9 us -> 58.7 us (0.980)
  waiting for transfers between devices: 15.3 us -> 14.4 us
    ppermute x6, waiting for transfers between devices: 4.59 us -> 3.68 us  [swapped(): return lax.ppermute(value, 'cuts', [(i, i ^ bit) for i in range(devices)])]
  transfers between devices with their start and end apart: 11 -> 11, of which waited for: 7 -> 7; matrix products, arithmetic and copies ran while one was open for 0% -> 0% of each run, Pallas kernels for 22% -> 23%
where the time goes in v5:
time: 58.7 us; the launch traced here: 58.1 us
  Pallas kernels  23.6 us (40%)
  starting transfers between devices  18.3 us (31%)
  waiting for transfers between devices  14.4 us (25%)
  between operations  1.5 us (3%)
    ppermute x5, starting transfers between devices, shifted(): return lax.ppermute(value, 'tile', pairs)  14.7 us
    ppermute x5, waiting for transfers between devices, shifted(): return lax.ppermute(value, 'tile', pairs)  10.7 us
    pallas_call x1, Pallas kernels, chain(): pl.pallas_call(kernel, out_shape=[jax.ShapeDtypeStruct((n, n), f32)] * 2,...  7.89 us
    pallas_call x1, Pallas kernels, early_waves(): pl.pallas_call(kernel, out_shape=jax.ShapeDtypeStruct((2, 2, n, n), f32),...  4.19 us
    ppermute x6, waiting for transfers between devices, swapped(): return lax.ppermute(value, 'cuts', [(i, i ^ bit) for i in range(devices)])  3.68 us
    ppermute x6, starting transfers between devices, swapped(): return lax.ppermute(value, 'cuts', [(i, i ^ bit) for i in range(devices)])  3.63 us
    pallas_call x2, Pallas kernels, add_came(): pl.pallas_call(kernel, out_shape=jax.ShapeDtypeStruct(base.shape, f32), i...  3.18 us
    pallas_call x1, Pallas kernels, place_own(): pl.pallas_call(kernel, out_shape=[jax.ShapeDtypeStruct((1, 2, rows, colum...  2.49 us
  transfers between devices with their start and end apart: 11, of which 7 were waited for; matrix products, arithmetic and copies ran while one was open for 0% of the time, Pallas kernels for 23%

profile of v5, /device:TPU:0, one launch (start us, length us, event | category | flops | bytes accessed | tf_op | source)
XLA Modules:
  0.0 58.1 jit_solution(3323169052108153887)
XLA Ops:
  1.3 0.1 pad_add_fusion.offsets
  1.4 4.9 %collective-permute-start = (s32[2]{0:T(128)S(1)}, s32[2]{0:T(128)S(1)}, u32[]{:S(2)}, u32[]{:S(2)}) collective-permute-start(s32[2]{0:T(128)S(1)} %pad_add_fusion.offsets), channel_id=1, source_target_pairs={{0,4},{4,8},{8,12},{12,16},{16,20},{20,24},{24,28},{1,5},{5,9},{9,... | collective-permute-start | bytes 32 | tf_op jit(solution)/shard_map/ppermute | solution.py:465
  6.2 1.6 %shard_map.82.strip = f32[1,2,256,1024]{3,2,1,0:T(8,128)S(1)} custom-call(f32[1,2,256,1024]{3,2,1,0:T(8,128)} %strip.1), custom_call_target="tpu_custom_call" | custom-call | tf_op jit(solution)/shard_map/pallas_call | solution.py:377
  7.8 0.0 copy-start.2
  7.9 0.0 copy-start.3
  7.9 0.0 collective-permute-done.offsets.came_offsets
  7.9 0.9 %shard_map.84 = (f32[2,144,256]{2,1,0:T(8,128)S(1)}, f32[2,112,256]{2,1,0:T(8,128)S(1)}) custom-call(s32[2]{0:T(128)S(1)} %collective-permute-done.offsets.came_offsets, f32[1,2,256,1024]{3,2,1,0:T(8,128)S(1)} %shard_map.82.strip), custom_call_target="tpu_custom_call" | custom-call | tf_op jit(solution)/shard_map/pallas_call | solution.py:401
  8.8 1.3 %collective-permute-start.2 = (f32[2,144,256]{2,1,0:T(8,128)S(1)}, f32[2,144,256]{2,1,0:T(8,128)S(1)}, u32[]{:S(2)}, u32[]{:S(2)}) collective-permute-start(f32[2,144,256]{2,1,0:T(8,128)S(1)} %get-tuple-element.31), channel_id=1, source_target_pairs={{4,0},{8,4},{12,8},{16,12},{20,16},{24,20},{28,24},{5,1},{9,5},{13... | collective-permute-start | bytes 884744 | tf_op jit(solution)/shard_map/ppermute | solution.py:465
  10.1 0.9 %shard_map.83 = (f32[2,144,256]{2,1,0:T(8,128)S(1)}, f32[2,112,256]{2,1,0:T(8,128)S(1)}) custom-call(s32[2]{0:T(128)S(1)} %pad_add_fusion.offsets, f32[1,2,256,1024]{3,2,1,0:T(8,128)S(1)} %shard_map.82.strip), custom_call_target="tpu_custom_call" | custom-call | tf_op jit(solution)/shard_map/pallas_call | solution.py:401
  11.1 0.0 copy-start
  11.1 0.0 copy-start.1
  11.1 2.4 %shard_map.85 = (f32[256,256]{1,0:T(8,128)}, f32[256,256]{1,0:T(8,128)}, f32[256,256]{1,0:T(8,128)}) custom-call(f32[256,256]{1,0:T(8,128)S(1)} %copy-done.2, f32[1,256,256]{2,1,0:T(8,128)S(1)} %copy-done.3), custom_call_target="tpu_custom_call" | custom-call | flops 603979776 | bytes 1966080 | tf_op jit(solution)/shard_map/pallas_call | solution.py:170
  13.5 1.3 %collective-permute-start.1 = (f32[2,112,256]{2,1,0:T(8,128)S(1)}, f32[2,112,256]{2,1,0:T(8,128)S(1)}, u32[]{:S(2)}, u32[]{:S(2)}) collective-permute-start(f32[2,112,256]{2,1,0:T(8,128)S(1)} %get-tuple-element.29), channel_id=1, source_target_pairs={{4,0},{8,4},{12,8},{16,12},{20,16},{24,20},{28,24},{5,1},{9,5},{13... | collective-permute-start | bytes 688136 | tf_op jit(solution)/shard_map/ppermute | solution.py:465
  14.8 5.2 %collective-permute-done.2 = f32[2,144,256]{2,1,0:T(8,128)S(1)} collective-permute-done((f32[2,144,256]{2,1,0:T(8,128)S(1)}, f32[2,144,256]{2,1,0:T(8,128)S(1)}, u32[]{:S(2)}, u32[]{:S(2)}) %collective-permute-start.2) | collective-permute-done | bytes 294944 | tf_op jit(solution)/shard_map/ppermute | solution.py:465
  20.1 0.1 broadcast_select_fusion.refs_0_
  20.2 1.6 %collective-permute-start.3 = (f32[2,144,256]{2,1,0:T(8,128)S(1)}, f32[2,144,256]{2,1,0:T(8,128)}, u32[]{:S(2)}, u32[]{:S(2)}) collective-permute-start(f32[2,144,256]{2,1,0:T(8,128)S(1)} %broadcast_select_fusion.refs_0_), channel_id=1, source_target_pairs={{0,2},{1,3},{2,0},{3,1},{4,6},{5,7},{6,4},{7,5},{8,10},{9,11},{10,... | collective-permute-start | bytes 884744 | tf_op jit(solution)/shard_map/ppermute | solution.py:470
  21.7 2.4 %collective-permute-done.1 = f32[2,112,256]{2,1,0:T(8,128)S(1)} collective-permute-done((f32[2,112,256]{2,1,0:T(8,128)S(1)}, f32[2,112,256]{2,1,0:T(8,128)S(1)}, u32[]{:S(2)}, u32[]{:S(2)}) %collective-permute-start.1) | collective-permute-done | bytes 229408 | tf_op jit(solution)/shard_map/ppermute | solution.py:465
  24.1 0.1 broadcast_select_fusion.1.refs_1_
  24.2 0.6 collective-permute-start.5
  24.8 1.5 %collective-permute-start.6 = (f32[2,112,256]{2,1,0:T(8,128)S(1)}, f32[2,112,256]{2,1,0:T(8,128)}, u32[]{:S(2)}, u32[]{:S(2)}) collective-permute-start(f32[2,112,256]{2,1,0:T(8,128)S(1)} %broadcast_select_fusion.1.refs_1_), channel_id=1, source_target_pairs={{0,2},{1,3},{2,0},{3,1},{4,6},{5,7},{6,4},{7,5},{8,10},{9,11},{10,... | collective-permute-start | bytes 688136 | tf_op jit(solution)/shard_map/ppermute | solution.py:470
  26.3 0.8 %collective-permute-done.3.refs_4_ = f32[2,144,256]{2,1,0:T(8,128)} collective-permute-done((f32[2,144,256]{2,1,0:T(8,128)S(1)}, f32[2,144,256]{2,1,0:T(8,128)}, u32[]{:S(2)}, u32[]{:S(2)}) %collective-permute-start.3) | collective-permute-done | bytes 294944 | tf_op jit(solution)/shard_map/ppermute | solution.py:470
  27.1 4.2 %shard_map.86.refs_12_ = f32[2,2,256,256]{3,2,1,0:T(8,128)S(1)} custom-call(s32[1]{0:T(128)} %bitcast.cut_ref, f32[2,144,256]{2,1,0:T(8,128)S(1)} %broadcast_select_fusion.refs_0_, f32[2,112,256]{2,1,0:T(8,128)S(1)} %broadcast_select_fusion.1.refs_1_, f32[2,144,256]{2,1,0:T(8,128)S(1)} %collective-permute-done.4.refs_2_, ...), custom_call_target="tpu_custom_call" | custom-call | flops 65536 | bytes 4096 | tf_op jit(solution)/shard_map/pallas_call | solution.py:238
  31.3 1.2 %collective-permute-done.6.refs_5_ = f32[2,112,256]{2,1,0:T(8,128)} collective-permute-done((f32[2,112,256]{2,1,0:T(8,128)S(1)}, f32[2,112,256]{2,1,0:T(8,128)}, u32[]{:S(2)}, u32[]{:S(2)}) %collective-permute-start.6) | collective-permute-done | bytes 229408 | tf_op jit(solution)/shard_map/ppermute | solution.py:470
  32.5 1.7 %collective-permute-done.8.refs_7_ = f32[2,112,256]{2,1,0:T(8,128)S(1)} collective-permute-done((f32[2,112,256]{2,1,0:T(8,128)}, f32[2,112,256]{2,1,0:T(8,128)S(1)}, u32[]{:S(2)}, u32[]{:S(2)}) %collective-permute-start.8) | collective-permute-done | bytes 229408 | tf_op jit(solution)/shard_map/ppermute | solution.py:470
  34.2 7.9 %shard_map.87 = (f32[256,256]{1,0:T(8,128)S(1)}, f32[256,256]{1,0:T(8,128)S(1)}) custom-call(s32[1]{0:T(128)} %bitcast.cut_ref, f32[2,144,256]{2,1,0:T(8,128)S(1)} %broadcast_select_fusion.refs_0_, f32[2,112,256]{2,1,0:T(8,128)S(1)} %broadcast_select_fusion.1.refs_1_, f32[2,144,256]{2,1,0:T(8,128)S(1)} %collective-permute-done.4.refs_2_, ...), custom_call_target="tpu_custom_call" | custom-call | flops 4026531840 | bytes 1048576 | tf_op jit(solution)/shard_map/pallas_call | solution.py:347
  42.1 4.3 %collective-permute-start.10 = (f32[256,256]{1,0:T(8,128)S(1)}, f32[256,256]{1,0:T(8,128)S(1)}, u32[]{:S(2)}, u32[]{:S(2)}) collective-permute-start(f32[256,256]{1,0:T(8,128)S(1)} %get-tuple-element.47.re), channel_id=1, source_target_pairs={{0,4},{4,8},{8,12},{12,16},{16,20},{20,24},{24,28},{1,5},{5,9},{9,... | collective-permute-start | bytes 786440 | tf_op jit(solution)/shard_map/ppermute | solution.py:465
  46.4 2.9 %collective-permute-start.9 = (f32[256,256]{1,0:T(8,128)S(1)}, f32[256,256]{1,0:T(8,128)S(1)}, u32[]{:S(2)}, u32[]{:S(2)}) collective-permute-start(f32[256,256]{1,0:T(8,128)S(1)} %get-tuple-element.46.im), channel_id=1, source_target_pairs={{0,4},{4,8},{8,12},{12,16},{16,20},{20,24},{24,28},{1,5},{5,9},{9,... | collective-permute-start | bytes 786440 | tf_op jit(solution)/shard_map/ppermute | solution.py:465
  49.3 2.5 %shard_map.88 = (f32[1,2,256,1024]{3,2,1,0:T(8,128)}, f32[256,384]{1,0:T(8,128)S(1)}, f32[256,384]{1,0:T(8,128)S(1)}) custom-call(s32[2]{0:T(128)S(1)} %pad_add_fusion.offsets, s32[2]{0:T(128)S(1)} %collective-permute-done.offsets.came_offsets, f32[256,256]{1,0:T(8,128)S(1)} %get-tuple-element.47.re, f32[256,256]{1,0:T(8,128)S(1)} %get-tuple-element.46.im), custom_call_target="tpu_custom_call" | custom-call | tf_op jit(solution)/shard_map/pallas_call | solution.py:429
  51.8 1.3 %collective-permute-done.10.came = f32[256,256]{1,0:T(8,128)S(1)} collective-permute-done((f32[256,256]{1,0:T(8,128)S(1)}, f32[256,256]{1,0:T(8,128)S(1)}, u32[]{:S(2)}, u32[]{:S(2)}) %collective-permute-start.10) | collective-permute-done | bytes 262176 | tf_op jit(solution)/shard_map/ppermute | solution.py:465
  53.1 1.6 %shard_map.89.base = f32[1,2,256,1024]{3,2,1,0:T(8,128)} custom-call(s32[2]{0:T(128)S(1)} %collective-permute-done.offsets.came_offsets, f32[256,256]{1,0:T(8,128)S(1)} %collective-permute-done.10.came, f32[256,384]{1,0:T(8,128)S(1)} %get-tuple-element.49.run, f32[1,2,256,1024]{3,2,1,0:T(8,128)} %get-tuple-element.50.base), custom_call_target="tpu_custom_call", output_to_operand_aliasing={{}: (3, {})} | custom-call | tf_op jit(solution)/shard_map/pallas_call | solution.py:451
  54.7 1.8 %collective-permute-done.9.came = f32[256,256]{1,0:T(8,128)S(1)} collective-permute-done((f32[256,256]{1,0:T(8,128)S(1)}, f32[256,256]{1,0:T(8,128)S(1)}, u32[]{:S(2)}, u32[]{:S(2)}) %collective-permute-start.9) | collective-permute-done | bytes 262176 | tf_op jit(solution)/shard_map/ppermute | solution.py:465
  56.5 1.6 %shard_map.90 = f32[1,2,256,1024]{3,2,1,0:T(8,128)} custom-call(s32[2]{0:T(128)S(1)} %collective-permute-done.offsets.came_offsets, f32[256,256]{1,0:T(8,128)S(1)} %collective-permute-done.9.came, f32[256,384]{1,0:T(8,128)S(1)} %get-tuple-element.48.run, f32[1,2,256,1024]{3,2,1,0:T(8,128)} %shard_map.89.base), custom_call_target="tpu_custom_call", output_to_operand_aliasing={{}: (3, {})} | custom-call | tf_op jit(solution)/shard_map/pallas_call | solution.py:451
  (12 shorter events, 0.0 us)
Async XLA Ops:
  1.4 6.5 %collective-permute-start = (s32[2]{0:T(128)S(1)}, s32[2]{0:T(128)S(1)}, u32[]{:S(2)}, u32[]{:S(2)}) collective-permute-start(s32[2]{0:T(128)S(1)} %pad_add_fusion.offsets), channel_id=1, source_target_pairs={{0,4},{4,8},{8,12},{12,16},{16,20},{20,24},{24,28},{1,5},{5,9},{9,... | collective-permute-start | bytes 32 | tf_op jit(solution)/shard_map/ppermute | solution.py:465
  7.8 3.2 %copy-start.2 = (f32[256,256]{1,0:T(8,128)S(1)}, f32[256,256]{1,0:T(8,128)}, u32[]{:S(2)}) copy-start(f32[256,256]{1,0:T(8,128)} %phase.1) | copy-start | bytes 786436
  7.9 3.2 %copy-start.3 = (f32[1,256,256]{2,1,0:T(8,128)S(1)}, f32[1,256,256]{2,1,0:T(8,128)}, u32[]{:S(2)}) copy-start(f32[1,256,256]{2,1,0:T(8,128)} %refs_0_.1) | copy-start | bytes 786436
  8.8 11.3 %collective-permute-start.2 = (f32[2,144,256]{2,1,0:T(8,128)S(1)}, f32[2,144,256]{2,1,0:T(8,128)S(1)}, u32[]{:S(2)}, u32[]{:S(2)}) collective-permute-start(f32[2,144,256]{2,1,0:T(8,128)S(1)} %get-tuple-element.31), channel_id=1, source_target_pairs={{4,0},{8,4},{12,8},{16,12},{20,16},{24,20},{28,24},{5,1},{9,5},{13... | collective-permute-start | bytes 884744 | tf_op jit(solution)/shard_map/ppermute | solution.py:465
  11.1 16.0 %copy-start = (bf16[4,768,256]{2,1,0:T(8,128)(2,1)S(1)}, bf16[4,768,256]{2,1,0:T(8,128)(2,1)}, u32[]{:S(2)}) copy-start(bf16[4,768,256]{2,1,0:T(8,128)(2,1)} %constant.13.clone.refs_7_.refs_13_) | copy-start | bytes 4718596
  11.1 16.0 %copy-start.1 = (bf16[8,256,256]{2,1,0:T(8,128)(2,1)S(1)}, bf16[8,256,256]{2,1,0:T(8,128)(2,1)}, u32[]{:S(2)}) copy-start(bf16[8,256,256]{2,1,0:T(8,128)(2,1)} %constant.14.clone.refs_8_.refs_14_) | copy-start | bytes 3145732
  13.5 10.6 %collective-permute-start.1 = (f32[2,112,256]{2,1,0:T(8,128)S(1)}, f32[2,112,256]{2,1,0:T(8,128)S(1)}, u32[]{:S(2)}, u32[]{:S(2)}) collective-permute-start(f32[2,112,256]{2,1,0:T(8,128)S(1)} %get-tuple-element.29), channel_id=1, source_target_pairs={{4,0},{8,4},{12,8},{16,12},{20,16},{24,20},{28,24},{5,1},{9,5},{13... | collective-permute-start | bytes 688136 | tf_op jit(solution)/shard_map/ppermute | solution.py:465
  20.2 6.9 %collective-permute-start.3 = (f32[2,144,256]{2,1,0:T(8,128)S(1)}, f32[2,144,256]{2,1,0:T(8,128)}, u32[]{:S(2)}, u32[]{:S(2)}) collective-permute-start(f32[2,144,256]{2,1,0:T(8,128)S(1)} %broadcast_select_fusion.refs_0_), channel_id=1, source_target_pairs={{0,2},{1,3},{2,0},{3,1},{4,6},{5,7},{6,4},{7,5},{8,10},{9,11},{10,... | collective-permute-start | bytes 884744 | tf_op jit(solution)/shard_map/ppermute | solution.py:470
  24.1 2.2 %collective-permute-start.4 = (f32[2,144,256]{2,1,0:T(8,128)S(1)}, f32[2,144,256]{2,1,0:T(8,128)S(1)}, u32[]{:S(2)}, u32[]{:S(2)}) collective-permute-start(f32[2,144,256]{2,1,0:T(8,128)S(1)} %broadcast_select_fusion.refs_0_), channel_id=1, source_target_pairs={{0,1},{1,0},{2,3},{3,2},{4,5},{5,4},{6,7},{7,6},{8,9},{9,8},{10,11... | collective-permute-start | bytes 884744 | tf_op jit(solution)/shard_map/ppermute | solution.py:470
  24.2 2.9 %collective-permute-start.5 = (f32[2,112,256]{2,1,0:T(8,128)S(1)}, f32[2,112,256]{2,1,0:T(8,128)}, u32[]{:S(2)}, u32[]{:S(2)}) collective-permute-start(f32[2,112,256]{2,1,0:T(8,128)S(1)} %broadcast_select_fusion.1.refs_1_), channel_id=1, source_target_pairs={{0,1},{1,0},{2,3},{3,2},{4,5},{5,4},{6,7},{7,6},{8,9},{9,8},{10,11... | collective-permute-start | bytes 688136 | tf_op jit(solution)/shard_map/ppermute | solution.py:470
  24.8 7.7 %collective-permute-start.6 = (f32[2,112,256]{2,1,0:T(8,128)S(1)}, f32[2,112,256]{2,1,0:T(8,128)}, u32[]{:S(2)}, u32[]{:S(2)}) collective-permute-start(f32[2,112,256]{2,1,0:T(8,128)S(1)} %broadcast_select_fusion.1.refs_1_), channel_id=1, source_target_pairs={{0,2},{1,3},{2,0},{3,1},{4,6},{5,7},{6,4},{7,5},{8,10},{9,11},{10,... | collective-permute-start | bytes 688136 | tf_op jit(solution)/shard_map/ppermute | solution.py:470
  27.1 7.1 %collective-permute-start.7 = (f32[2,144,256]{2,1,0:T(8,128)}, f32[2,144,256]{2,1,0:T(8,128)}, u32[]{:S(2)}, u32[]{:S(2)}) collective-permute-start(f32[2,144,256]{2,1,0:T(8,128)} %collective-permute-done.3.refs_4_), channel_id=1, source_target_pairs={{0,1},{1,0},{2,3},{3,2},{4,5},{5,4},{6,7},{7,6},{8,9},{9,8},{10,11... | collective-permute-start | bytes 884744 | tf_op jit(solution)/shard_map/ppermute | solution.py:470
  32.5 1.7 %collective-permute-start.8 = (f32[2,112,256]{2,1,0:T(8,128)}, f32[2,112,256]{2,1,0:T(8,128)S(1)}, u32[]{:S(2)}, u32[]{:S(2)}) collective-permute-start(f32[2,112,256]{2,1,0:T(8,128)} %collective-permute-done.6.refs_5_), channel_id=1, source_target_pairs={{0,1},{1,0},{2,3},{3,2},{4,5},{5,4},{6,7},{7,6},{8,9},{9,8},{10,11... | collective-permute-start | bytes 688136 | tf_op jit(solution)/shard_map/ppermute | solution.py:470
  42.1 11.1 %collective-permute-start.10 = (f32[256,256]{1,0:T(8,128)S(1)}, f32[256,256]{1,0:T(8,128)S(1)}, u32[]{:S(2)}, u32[]{:S(2)}) collective-permute-start(f32[256,256]{1,0:T(8,128)S(1)} %get-tuple-element.47.re), channel_id=1, source_target_pairs={{0,4},{4,8},{8,12},{12,16},{16,20},{20,24},{24,28},{1,5},{5,9},{9,... | collective-permute-start | bytes 786440 | tf_op jit(solution)/shard_map/ppermute | solution.py:465
  46.4 10.1 %collective-permute-start.9 = (f32[256,256]{1,0:T(8,128)S(1)}, f32[256,256]{1,0:T(8,128)S(1)}, u32[]{:S(2)}, u32[]{:S(2)}) collective-permute-start(f32[256,256]{1,0:T(8,128)S(1)} %get-tuple-element.46.im), channel_id=1, source_target_pairs={{0,4},{4,8},{8,12},{12,16},{16,20},{20,24},{24,28},{1,5},{5,9},{9,... | collective-permute-start | bytes 786440 | tf_op jit(solution)/shard_map/ppermute | solution.py:465

commit v6 on v5

--- a/solution.py
+++ b/solution.py
@@ -11,7 +11,6 @@
 VMEM = pl.BlockSpec(memory_space=pltpu.VMEM)
 SMEM = pl.BlockSpec(memory_space=pltpu.SMEM)
 ANY = pl.BlockSpec(memory_space=pl.ANY)
-HBM = pl.BlockSpec(memory_space=pltpu.HBM)
 SHORT = pl.CostEstimate(flops=1 << 16, bytes_accessed=1 << 12, transcendentals=0)
 PARAMS = pltpu.CompilerParams(vmem_limit_bytes=12 << 20)
 
@@ -114,12 +113,12 @@
     return ar * br + ai * bi, ar * bi - ai * br
 
 
-def by_phase(spectrum, cosine, sine):
+def by_phase(spectrum, cosine, sine, product=times):
     q = spectrum[0].shape[0] // 2
     out = []
     for i, x in enumerate(spectrum):
         at = slice(i * q, (i + 1) * q)
-        out.append(jnp.concatenate(times(x[:q], x[q:], cosine[at], sine[at]), 0))
+        out.append(jnp.concatenate(product(cosine[at], sine[at], x[:q], x[q:]), 0))
     return out
 
 
@@ -284,7 +283,7 @@
                 @pl.when(me < s)
                 def _():
                     gr, gi = conj_times(patch[s, 0], patch[s, 1], re, im)
-                    spectrum = by_phase(forward(gr, gi, tables), cosine[...], -sine[...])
+                    spectrum = by_phase(forward(gr, gi, tables), cosine[...], sine[...], conj_times)
                     back(s - 1, *inverse(spectrum, tables))
 
         early_copies = [pltpu.make_async_copy(planes[4].at[s], waves.at[s], early_sem.at[s]) for s in range(2)]
@@ -479,7 +478,7 @@
     return jnp.where(index < rows - row, first, second)
 
 
-BOUNDS = (0, 144, 256)
+BOUNDS = (0, 152, 256)
 
 
 def per_device(transmission, probe, prop_phase, row_off, col_off, measured):

time: 58.7 us -> 58.5 us (level)
    ppermute x5, starting transfers between devices: 14.7 us -> 14.1 us  [shifted(): return lax.ppermute(value, 'tile', pairs)]
  transfers between devices with their start and end apart: 11 -> 11, of which waited for: 7 -> 6; matrix products, arithmetic and copies ran while one was open for 0% -> 0% of each run, Pallas kernels for 23% -> 23%
where the time goes in v6:
time: 58.5 us; the launch traced here: 58.2 us
  Pallas kernels  23.6 us (40%)
  starting transfers between devices  18.3 us (31%)
  waiting for transfers between devices  14.4 us (25%)
  between operations  1.5 us (3%)
    ppermute x5, starting transfers between devices, shifted(): return lax.ppermute(value, 'tile', pairs)  14.1 us
    ppermute x5, waiting for transfers between devices, shifted(): return lax.ppermute(value, 'tile', pairs)  11.1 us
    pallas_call x1, Pallas kernels, chain(): pl.pallas_call(kernel, out_shape=[jax.ShapeDtypeStruct((n, n), f32)] * 2,...  7.91 us
    pallas_call x1, Pallas kernels, early_waves(): pl.pallas_call(kernel, out_shape=jax.ShapeDtypeStruct((2, 2, n, n), f32),...  4.2 us
    ppermute x6, starting transfers between devices, swapped(): return lax.ppermute(value, 'cuts', [(i, i ^ bit) for i in range(devices)])  4.19 us
    ppermute x6, waiting for transfers between devices, swapped(): return lax.ppermute(value, 'cuts', [(i, i ^ bit) for i in range(devices)])  3.35 us
    pallas_call x2, Pallas kernels, add_came(): pl.pallas_call(kernel, out_shape=jax.ShapeDtypeStruct(base.shape, f32), i...  3.18 us
    pallas_call x1, Pallas kernels, place_own(): pl.pallas_call(kernel, out_shape=[jax.ShapeDtypeStruct((1, 2, rows, colum...  2.49 us
  transfers between devices with their start and end apart: 11, of which 6 were waited for; matrix products, arithmetic and copies ran while one was open for 0% of the time, Pallas kernels for 23%

profile of v6, /device:TPU:0, one launch (start us, length us, event | category | flops | bytes accessed | tf_op | source)
XLA Modules:
  0.0 58.2 jit_solution(81131311041494641)
XLA Ops:
  1.3 0.1 pad_add_fusion.offsets
  1.4 4.9 %collective-permute-start = (s32[2]{0:T(128)S(1)}, s32[2]{0:T(128)S(1)}, u32[]{:S(2)}, u32[]{:S(2)}) collective-permute-start(s32[2]{0:T(128)S(1)} %pad_add_fusion.offsets), channel_id=1, source_target_pairs={{0,4},{4,8},{8,12},{12,16},{16,20},{20,24},{24,28},{1,5},{5,9},{9,... | collective-permute-start | bytes 32 | tf_op jit(solution)/shard_map/ppermute | solution.py:464
  6.2 1.6 %shard_map.82.strip = f32[1,2,256,1024]{3,2,1,0:T(8,128)S(1)} custom-call(f32[1,2,256,1024]{3,2,1,0:T(8,128)} %strip.1), custom_call_target="tpu_custom_call" | custom-call | tf_op jit(solution)/shard_map/pallas_call | solution.py:376
  7.8 0.0 copy-start.2
  7.9 0.0 copy-start.3
  7.9 0.9 %shard_map.84 = (f32[2,152,256]{2,1,0:T(8,128)S(1)}, f32[2,104,256]{2,1,0:T(8,128)S(1)}) custom-call(s32[2]{0:T(128)S(1)} %collective-permute-done.offsets.came_offsets, f32[1,2,256,1024]{3,2,1,0:T(8,128)S(1)} %shard_map.82.strip), custom_call_target="tpu_custom_call" | custom-call | tf_op jit(solution)/shard_map/pallas_call | solution.py:400
  8.8 1.3 %collective-permute-start.2 = (f32[2,152,256]{2,1,0:T(8,128)S(1)}, f32[2,152,256]{2,1,0:T(8,128)S(1)}, u32[]{:S(2)}, u32[]{:S(2)}) collective-permute-start(f32[2,152,256]{2,1,0:T(8,128)S(1)} %get-tuple-element.31), channel_id=1, source_target_pairs={{4,0},{8,4},{12,8},{16,12},{20,16},{24,20},{28,24},{5,1},{9,5},{13... | collective-permute-start | bytes 933896 | tf_op jit(solution)/shard_map/ppermute | solution.py:464
  10.1 0.9 %shard_map.83 = (f32[2,152,256]{2,1,0:T(8,128)S(1)}, f32[2,104,256]{2,1,0:T(8,128)S(1)}) custom-call(s32[2]{0:T(128)S(1)} %pad_add_fusion.offsets, f32[1,2,256,1024]{3,2,1,0:T(8,128)S(1)} %shard_map.82.strip), custom_call_target="tpu_custom_call" | custom-call | tf_op jit(solution)/shard_map/pallas_call | solution.py:400
  11.1 0.0 copy-start
  11.1 0.0 copy-start.1
  11.1 2.4 %shard_map.85 = (f32[256,256]{1,0:T(8,128)}, f32[256,256]{1,0:T(8,128)}, f32[256,256]{1,0:T(8,128)}) custom-call(f32[256,256]{1,0:T(8,128)S(1)} %copy-done.2, f32[1,256,256]{2,1,0:T(8,128)S(1)} %copy-done.3), custom_call_target="tpu_custom_call" | custom-call | flops 603979776 | bytes 1966080 | tf_op jit(solution)/shard_map/pallas_call | solution.py:169
  13.5 1.3 %collective-permute-start.1 = (f32[2,104,256]{2,1,0:T(8,128)S(1)}, f32[2,104,256]{2,1,0:T(8,128)S(1)}, u32[]{:S(2)}, u32[]{:S(2)}) collective-permute-start(f32[2,104,256]{2,1,0:T(8,128)S(1)} %get-tuple-element.29), channel_id=1, source_target_pairs={{4,0},{8,4},{12,8},{16,12},{20,16},{24,20},{28,24},{5,1},{9,5},{13... | collective-permute-start | bytes 638984 | tf_op jit(solution)/shard_map/ppermute | solution.py:464
  14.8 5.9 %collective-permute-done.2 = f32[2,152,256]{2,1,0:T(8,128)S(1)} collective-permute-done((f32[2,152,256]{2,1,0:T(8,128)S(1)}, f32[2,152,256]{2,1,0:T(8,128)S(1)}, u32[]{:S(2)}, u32[]{:S(2)}) %collective-permute-start.2) | collective-permute-done | bytes 311328 | tf_op jit(solution)/shard_map/ppermute | solution.py:464
  20.8 0.1 broadcast_select_fusion.refs_0_
  20.9 1.6 %collective-permute-start.3 = (f32[2,152,256]{2,1,0:T(8,128)S(1)}, f32[2,152,256]{2,1,0:T(8,128)}, u32[]{:S(2)}, u32[]{:S(2)}) collective-permute-start(f32[2,152,256]{2,1,0:T(8,128)S(1)} %broadcast_select_fusion.refs_0_), channel_id=1, source_target_pairs={{0,2},{1,3},{2,0},{3,1},{4,6},{5,7},{6,4},{7,5},{8,10},{9,11},{10,... | collective-permute-start | bytes 933896 | tf_op jit(solution)/shard_map/ppermute | solution.py:469
  22.4 1.7 %collective-permute-done.1 = f32[2,104,256]{2,1,0:T(8,128)S(1)} collective-permute-done((f32[2,104,256]{2,1,0:T(8,128)S(1)}, f32[2,104,256]{2,1,0:T(8,128)S(1)}, u32[]{:S(2)}, u32[]{:S(2)}) %collective-permute-start.1) | collective-permute-done | bytes 213024 | tf_op jit(solution)/shard_map/ppermute | solution.py:464
  24.1 0.1 broadcast_select_fusion.1.refs_1_
  24.2 0.6 collective-permute-start.5
  24.8 1.5 %collective-permute-start.6 = (f32[2,104,256]{2,1,0:T(8,128)S(1)}, f32[2,104,256]{2,1,0:T(8,128)}, u32[]{:S(2)}, u32[]{:S(2)}) collective-permute-start(f32[2,104,256]{2,1,0:T(8,128)S(1)} %broadcast_select_fusion.1.refs_1_), channel_id=1, source_target_pairs={{0,2},{1,3},{2,0},{3,1},{4,6},{5,7},{6,4},{7,5},{8,10},{9,11},{10,... | collective-permute-start | bytes 638984 | tf_op jit(solution)/shard_map/ppermute | solution.py:469
  26.3 2.0 %collective-permute-done.3.refs_4_ = f32[2,152,256]{2,1,0:T(8,128)} collective-permute-done((f32[2,152,256]{2,1,0:T(8,128)S(1)}, f32[2,152,256]{2,1,0:T(8,128)}, u32[]{:S(2)}, u32[]{:S(2)}) %collective-permute-start.3) | collective-permute-done | bytes 311328 | tf_op jit(solution)/shard_map/ppermute | solution.py:469
  28.3 0.0 collective-permute-start.7
  28.3 4.2 %shard_map.86.refs_12_ = f32[2,2,256,256]{3,2,1,0:T(8,128)S(1)} custom-call(s32[1]{0:T(128)} %bitcast.cut_ref, f32[2,152,256]{2,1,0:T(8,128)S(1)} %broadcast_select_fusion.refs_0_, f32[2,104,256]{2,1,0:T(8,128)S(1)} %broadcast_select_fusion.1.refs_1_, f32[2,152,256]{2,1,0:T(8,128)S(1)} %collective-permute-done.4.refs_2_, ...), custom_call_target="tpu_custom_call" | custom-call | flops 65536 | bytes 4096 | tf_op jit(solution)/shard_map/pallas_call | solution.py:237
  32.5 0.6 collective-permute-start.8
  33.1 1.3 %collective-permute-done.8.refs_7_ = f32[2,104,256]{2,1,0:T(8,128)S(1)} collective-permute-done((f32[2,104,256]{2,1,0:T(8,128)}, f32[2,104,256]{2,1,0:T(8,128)S(1)}, u32[]{:S(2)}, u32[]{:S(2)}) %collective-permute-start.8) | collective-permute-done | bytes 213024 | tf_op jit(solution)/shard_map/ppermute | solution.py:469
  34.4 7.9 %shard_map.87 = (f32[256,256]{1,0:T(8,128)S(1)}, f32[256,256]{1,0:T(8,128)S(1)}) custom-call(s32[1]{0:T(128)} %bitcast.cut_ref, f32[2,152,256]{2,1,0:T(8,128)S(1)} %broadcast_select_fusion.refs_0_, f32[2,104,256]{2,1,0:T(8,128)S(1)} %broadcast_select_fusion.1.refs_1_, f32[2,152,256]{2,1,0:T(8,128)S(1)} %collective-permute-done.4.refs_2_, ...), custom_call_target="tpu_custom_call" | custom-call | flops 4026531840 | bytes 1048576 | tf_op jit(solution)/shard_map/pallas_call | solution.py:346
  42.3 3.9 %collective-permute-start.10 = (f32[256,256]{1,0:T(8,128)S(1)}, f32[256,256]{1,0:T(8,128)S(1)}, u32[]{:S(2)}, u32[]{:S(2)}) collective-permute-start(f32[256,256]{1,0:T(8,128)S(1)} %get-tuple-element.47.re), channel_id=1, source_target_pairs={{0,4},{4,8},{8,12},{12,16},{16,20},{20,24},{24,28},{1,5},{5,9},{9,... | collective-permute-start | bytes 786440 | tf_op jit(solution)/shard_map/ppermute | solution.py:464
  46.3 2.7 %collective-permute-start.9 = (f32[256,256]{1,0:T(8,128)S(1)}, f32[256,256]{1,0:T(8,128)S(1)}, u32[]{:S(2)}, u32[]{:S(2)}) collective-permute-start(f32[256,256]{1,0:T(8,128)S(1)} %get-tuple-element.46.im), channel_id=1, source_target_pairs={{0,4},{4,8},{8,12},{12,16},{16,20},{20,24},{24,28},{1,5},{5,9},{9,... | collective-permute-start | bytes 786440 | tf_op jit(solution)/shard_map/ppermute | solution.py:464
  49.0 2.5 %shard_map.88 = (f32[1,2,256,1024]{3,2,1,0:T(8,128)}, f32[256,384]{1,0:T(8,128)S(1)}, f32[256,384]{1,0:T(8,128)S(1)}) custom-call(s32[2]{0:T(128)S(1)} %pad_add_fusion.offsets, s32[2]{0:T(128)S(1)} %collective-permute-done.offsets.came_offsets, f32[256,256]{1,0:T(8,128)S(1)} %get-tuple-element.47.re, f32[256,256]{1,0:T(8,128)S(1)} %get-tuple-element.46.im), custom_call_target="tpu_custom_call" | custom-call | tf_op jit(solution)/shard_map/pallas_call | solution.py:428
  51.5 1.5 %collective-permute-done.10.came = f32[256,256]{1,0:T(8,128)S(1)} collective-permute-done((f32[256,256]{1,0:T(8,128)S(1)}, f32[256,256]{1,0:T(8,128)S(1)}, u32[]{:S(2)}, u32[]{:S(2)}) %collective-permute-start.10) | collective-permute-done | bytes 262176 | tf_op jit(solution)/shard_map/ppermute | solution.py:464
  53.0 1.6 %shard_map.89.base = f32[1,2,256,1024]{3,2,1,0:T(8,128)} custom-call(s32[2]{0:T(128)S(1)} %collective-permute-done.offsets.came_offsets, f32[256,256]{1,0:T(8,128)S(1)} %collective-permute-done.10.came, f32[256,384]{1,0:T(8,128)S(1)} %get-tuple-element.49.run, f32[1,2,256,1024]{3,2,1,0:T(8,128)} %get-tuple-element.50.base), custom_call_target="tpu_custom_call", output_to_operand_aliasing={{}: (3, {})} | custom-call | tf_op jit(solution)/shard_map/pallas_call | solution.py:450
  54.6 2.0 %collective-permute-done.9.came = f32[256,256]{1,0:T(8,128)S(1)} collective-permute-done((f32[256,256]{1,0:T(8,128)S(1)}, f32[256,256]{1,0:T(8,128)S(1)}, u32[]{:S(2)}, u32[]{:S(2)}) %collective-permute-start.9) | collective-permute-done | bytes 262176 | tf_op jit(solution)/shard_map/ppermute | solution.py:464
  56.6 1.6 %shard_map.90 = f32[1,2,256,1024]{3,2,1,0:T(8,128)} custom-call(s32[2]{0:T(128)S(1)} %collective-permute-done.offsets.came_offsets, f32[256,256]{1,0:T(8,128)S(1)} %collective-permute-done.9.came, f32[256,384]{1,0:T(8,128)S(1)} %get-tuple-element.48.run, f32[1,2,256,1024]{3,2,1,0:T(8,128)} %shard_map.89.base), custom_call_target="tpu_custom_call", output_to_operand_aliasing={{}: (3, {})} | custom-call | tf_op jit(solution)/shard_map/pallas_call | solution.py:450
  (12 shorter events, 0.0 us)
Async XLA Ops:
  1.4 6.5 %collective-permute-start = (s32[2]{0:T(128)S(1)}, s32[2]{0:T(128)S(1)}, u32[]{:S(2)}, u32[]{:S(2)}) collective-permute-start(s32[2]{0:T(128)S(1)} %pad_add_fusion.offsets), channel_id=1, source_target_pairs={{0,4},{4,8},{8,12},{12,16},{16,20},{20,24},{24,28},{1,5},{5,9},{9,... | collective-permute-start | bytes 32 | tf_op jit(solution)/shard_map/ppermute | solution.py:464
  7.8 3.2 %copy-start.2 = (f32[256,256]{1,0:T(8,128)S(1)}, f32[256,256]{1,0:T(8,128)}, u32[]{:S(2)}) copy-start(f32[256,256]{1,0:T(8,128)} %phase.1) | copy-start | bytes 786436
  7.9 3.2 %copy-start.3 = (f32[1,256,256]{2,1,0:T(8,128)S(1)}, f32[1,256,256]{2,1,0:T(8,128)}, u32[]{:S(2)}) copy-start(f32[1,256,256]{2,1,0:T(8,128)} %refs_0_.1) | copy-start | bytes 786436
  8.8 12.0 %collective-permute-start.2 = (f32[2,152,256]{2,1,0:T(8,128)S(1)}, f32[2,152,256]{2,1,0:T(8,128)S(1)}, u32[]{:S(2)}, u32[]{:S(2)}) collective-permute-start(f32[2,152,256]{2,1,0:T(8,128)S(1)} %get-tuple-element.31), channel_id=1, source_target_pairs={{4,0},{8,4},{12,8},{16,12},{20,16},{24,20},{28,24},{5,1},{9,5},{13... | collective-permute-start | bytes 933896 | tf_op jit(solution)/shard_map/ppermute | solution.py:464
  11.1 17.3 %copy-start = (bf16[4,768,256]{2,1,0:T(8,128)(2,1)S(1)}, bf16[4,768,256]{2,1,0:T(8,128)(2,1)}, u32[]{:S(2)}) copy-start(bf16[4,768,256]{2,1,0:T(8,128)(2,1)} %constant.13.clone.refs_7_.refs_13_) | copy-start | bytes 4718596
  11.1 17.2 %copy-start.1 = (bf16[8,256,256]{2,1,0:T(8,128)(2,1)S(1)}, bf16[8,256,256]{2,1,0:T(8,128)(2,1)}, u32[]{:S(2)}) copy-start(bf16[8,256,256]{2,1,0:T(8,128)(2,1)} %constant.14.clone.refs_8_.refs_14_) | copy-start | bytes 3145732
  13.5 10.5 %collective-permute-start.1 = (f32[2,104,256]{2,1,0:T(8,128)S(1)}, f32[2,104,256]{2,1,0:T(8,128)S(1)}, u32[]{:S(2)}, u32[]{:S(2)}) collective-permute-start(f32[2,104,256]{2,1,0:T(8,128)S(1)} %get-tuple-element.29), channel_id=1, source_target_pairs={{4,0},{8,4},{12,8},{16,12},{20,16},{24,20},{28,24},{5,1},{9,5},{13... | collective-permute-start | bytes 638984 | tf_op jit(solution)/shard_map/ppermute | solution.py:464
  20.9 7.4 %collective-permute-start.3 = (f32[2,152,256]{2,1,0:T(8,128)S(1)}, f32[2,152,256]{2,1,0:T(8,128)}, u32[]{:S(2)}, u32[]{:S(2)}) collective-permute-start(f32[2,152,256]{2,1,0:T(8,128)S(1)} %broadcast_select_fusion.refs_0_), channel_id=1, source_target_pairs={{0,2},{1,3},{2,0},{3,1},{4,6},{5,7},{6,4},{7,5},{8,10},{9,11},{10,... | collective-permute-start | bytes 933896 | tf_op jit(solution)/shard_map/ppermute | solution.py:469
  24.1 2.2 %collective-permute-start.4 = (f32[2,152,256]{2,1,0:T(8,128)S(1)}, f32[2,152,256]{2,1,0:T(8,128)S(1)}, u32[]{:S(2)}, u32[]{:S(2)}) collective-permute-start(f32[2,152,256]{2,1,0:T(8,128)S(1)} %broadcast_select_fusion.refs_0_), channel_id=1, source_target_pairs={{0,1},{1,0},{2,3},{3,2},{4,5},{5,4},{6,7},{7,6},{8,9},{9,8},{10,11... | collective-permute-start | bytes 933896 | tf_op jit(solution)/shard_map/ppermute | solution.py:469
  24.2 4.1 %collective-permute-start.5 = (f32[2,104,256]{2,1,0:T(8,128)S(1)}, f32[2,104,256]{2,1,0:T(8,128)}, u32[]{:S(2)}, u32[]{:S(2)}) collective-permute-start(f32[2,104,256]{2,1,0:T(8,128)S(1)} %broadcast_select_fusion.1.refs_1_), channel_id=1, source_target_pairs={{0,1},{1,0},{2,3},{3,2},{4,5},{5,4},{6,7},{7,6},{8,9},{9,8},{10,11... | collective-permute-start | bytes 638984 | tf_op jit(solution)/shard_map/ppermute | solution.py:469
  24.8 7.8 %collective-permute-start.6 = (f32[2,104,256]{2,1,0:T(8,128)S(1)}, f32[2,104,256]{2,1,0:T(8,128)}, u32[]{:S(2)}, u32[]{:S(2)}) collective-permute-start(f32[2,104,256]{2,1,0:T(8,128)S(1)} %broadcast_select_fusion.1.refs_1_), channel_id=1, source_target_pairs={{0,2},{1,3},{2,0},{3,1},{4,6},{5,7},{6,4},{7,5},{8,10},{9,11},{10,... | collective-permute-start | bytes 638984 | tf_op jit(solution)/shard_map/ppermute | solution.py:469
  28.3 6.1 %collective-permute-start.7 = (f32[2,152,256]{2,1,0:T(8,128)}, f32[2,152,256]{2,1,0:T(8,128)}, u32[]{:S(2)}, u32[]{:S(2)}) collective-permute-start(f32[2,152,256]{2,1,0:T(8,128)} %collective-permute-done.3.refs_4_), channel_id=1, source_target_pairs={{0,1},{1,0},{2,3},{3,2},{4,5},{5,4},{6,7},{7,6},{8,9},{9,8},{10,11... | collective-permute-start | bytes 933896 | tf_op jit(solution)/shard_map/ppermute | solution.py:469
  32.5 1.9 %collective-permute-start.8 = (f32[2,104,256]{2,1,0:T(8,128)}, f32[2,104,256]{2,1,0:T(8,128)S(1)}, u32[]{:S(2)}, u32[]{:S(2)}) collective-permute-start(f32[2,104,256]{2,1,0:T(8,128)} %collective-permute-done.6.refs_5_), channel_id=1, source_target_pairs={{0,1},{1,0},{2,3},{3,2},{4,5},{5,4},{6,7},{7,6},{8,9},{9,8},{10,11... | collective-permute-start | bytes 638984 | tf_op jit(solution)/shard_map/ppermute | solution.py:469
  42.3 10.7 %collective-permute-start.10 = (f32[256,256]{1,0:T(8,128)S(1)}, f32[256,256]{1,0:T(8,128)S(1)}, u32[]{:S(2)}, u32[]{:S(2)}) collective-permute-start(f32[256,256]{1,0:T(8,128)S(1)} %get-tuple-element.47.re), channel_id=1, source_target_pairs={{0,4},{4,8},{8,12},{12,16},{16,20},{20,24},{24,28},{1,5},{5,9},{9,... | collective-permute-start | bytes 786440 | tf_op jit(solution)/shard_map/ppermute | solution.py:464
  46.3 10.3 %collective-permute-start.9 = (f32[256,256]{1,0:T(8,128)S(1)}, f32[256,256]{1,0:T(8,128)S(1)}, u32[]{:S(2)}, u32[]{:S(2)}) collective-permute-start(f32[256,256]{1,0:T(8,128)S(1)} %get-tuple-element.46.im), channel_id=1, source_target_pairs={{0,4},{4,8},{8,12},{12,16},{16,20},{20,24},{24,28},{1,5},{5,9},{9,... | collective-permute-start | bytes 786440 | tf_op jit(solution)/shard_map/ppermute | solution.py:464

commit v7 on v6

--- a/solution.py
+++ b/solution.py
@@ -407,9 +407,11 @@
 
 
 def moved(piece, row, shift, keep):
-    rows = piece.shape[0]
-    x = jnp.where(keep, pltpu.roll(piece, row, 0), 0.0)
-    return pltpu.roll(jnp.concatenate([x, jnp.zeros((rows, LANE), f32)], 1), shift, 1)
+    return shifted_right(jnp.where(keep, pltpu.roll(piece, row, 0), 0.0), shift)
+
+
+def shifted_right(x, shift):
+    return pltpu.roll(jnp.concatenate([x, jnp.zeros((x.shape[0], LANE), f32)], 1), shift, 1)
 
 
 def place_own(offsets, came_offsets, planes, columns):
@@ -438,14 +440,23 @@
     rows, width = came.shape
     columns = base.shape[3]
 
+    parts = 4
+    step = rows // parts
+
     def kernel(offsets, came, run, base, out, wide, sem):
         row = offsets[0]
         start, shift = window_start(offsets[1], width, columns)
         index = lax.broadcasted_iota(jnp.int32, (rows, width), 0)
-        wide[...] = run[...] + moved(came[...], row, shift, index < row)
-        write = pltpu.make_async_copy(wide, out.at[0, c, :, pl.ds(start, width + LANE)], sem)
-        write.start()
-        write.wait()
+        x = jnp.where(index < row, pltpu.roll(came[...], row, 0), 0.0)
+        writes = []
+        for part in range(parts):
+            at = pl.ds(part * step, step)
+            wide[at] = run[at] + shifted_right(x[part * step : (part + 1) * step], shift)
+            to = out.at[0, c, at, pl.ds(start, width + LANE)]
+            writes.append(pltpu.make_async_copy(wide.at[at], to, sem.at[part]))
+            writes[-1].start()
+        for write in writes:
+            write.wait()
 
     return pl.pallas_call(
         kernel,
@@ -453,7 +464,7 @@
         in_specs=[SMEM, VMEM, VMEM, ANY],
         out_specs=ANY,
         input_output_aliases={3: 0},
-        scratch_shapes=[pltpu.VMEM((rows, width + LANE), f32), pltpu.SemaphoreType.DMA],
+        scratch_shapes=[pltpu.VMEM((rows, width + LANE), f32), pltpu.SemaphoreType.DMA((parts,))],
         compiler_params=PARAMS,
     )(offsets, came, run, pinned(base))
 

time: 58.5 us -> 58.4 us (level)
  no operation moved by 1% of the time
where the time goes in v7:
time: 58.4 us; the launch traced here: 58.1 us
  Pallas kernels  23.4 us (40%)
  starting transfers between devices  18.3 us (31%)
  waiting for transfers between devices  14.6 us (25%)
  between operations  1.5 us (3%)
    ppermute x5, starting transfers between devices, shifted(): return lax.ppermute(value, 'tile', pairs)  14.1 us
    ppermute x5, waiting for transfers between devices, shifted(): return lax.ppermute(value, 'tile', pairs)  11.2 us
    pallas_call x1, Pallas kernels, chain(): pl.pallas_call(kernel, out_shape=[jax.ShapeDtypeStruct((n, n), f32)] * 2,...  7.91 us
    pallas_call x1, Pallas kernels, early_waves(): pl.pallas_call(kernel, out_shape=jax.ShapeDtypeStruct((2, 2, n, n), f32),...  4.2 us
    ppermute x6, starting transfers between devices, swapped(): return lax.ppermute(value, 'cuts', [(i, i ^ bit) for i in range(devices)])  4.19 us
    ppermute x6, waiting for transfers between devices, swapped(): return lax.ppermute(value, 'cuts', [(i, i ^ bit) for i in range(devices)])  3.35 us
    pallas_call x2, Pallas kernels, add_came(): pl.pallas_call(kernel, out_shape=jax.ShapeDtypeStruct(base.shape, f32), i...  2.95 us
    pallas_call x1, Pallas kernels, place_own(): pl.pallas_call(kernel, out_shape=[jax.ShapeDtypeStruct((1, 2, rows, colum...  2.49 us
  transfers between devices with their start and end apart: 11, of which 6 were waited for; matrix products, arithmetic and copies ran while one was open for 0% of the time, Pallas kernels for 23%

profile of v7, /device:TPU:0, one launch (start us, length us, event | category | flops | bytes accessed | tf_op | source)
XLA Modules:
  0.0 58.1 jit_solution(2986989609102831359)
XLA Ops:
  1.3 0.1 pad_add_fusion.offsets
  1.4 4.9 %collective-permute-start = (s32[2]{0:T(128)S(1)}, s32[2]{0:T(128)S(1)}, u32[]{:S(2)}, u32[]{:S(2)}) collective-permute-start(s32[2]{0:T(128)S(1)} %pad_add_fusion.offsets), channel_id=1, source_target_pairs={{0,4},{4,8},{8,12},{12,16},{16,20},{20,24},{24,28},{1,5},{5,9},{9,... | collective-permute-start | bytes 32 | tf_op jit(solution)/shard_map/ppermute | solution.py:475
  6.2 1.6 %shard_map.82.strip = f32[1,2,256,1024]{3,2,1,0:T(8,128)S(1)} custom-call(f32[1,2,256,1024]{3,2,1,0:T(8,128)} %strip.1), custom_call_target="tpu_custom_call" | custom-call | tf_op jit(solution)/shard_map/pallas_call | solution.py:376
  7.8 0.0 copy-start.2
  7.9 0.0 copy-start.3
  7.9 0.9 %shard_map.84 = (f32[2,152,256]{2,1,0:T(8,128)S(1)}, f32[2,104,256]{2,1,0:T(8,128)S(1)}) custom-call(s32[2]{0:T(128)S(1)} %collective-permute-done.offsets.came_offsets, f32[1,2,256,1024]{3,2,1,0:T(8,128)S(1)} %shard_map.82.strip), custom_call_target="tpu_custom_call" | custom-call | tf_op jit(solution)/shard_map/pallas_call | solution.py:400
  8.8 1.3 %collective-permute-start.2 = (f32[2,152,256]{2,1,0:T(8,128)S(1)}, f32[2,152,256]{2,1,0:T(8,128)S(1)}, u32[]{:S(2)}, u32[]{:S(2)}) collective-permute-start(f32[2,152,256]{2,1,0:T(8,128)S(1)} %get-tuple-element.31), channel_id=1, source_target_pairs={{4,0},{8,4},{12,8},{16,12},{20,16},{24,20},{28,24},{5,1},{9,5},{13... | collective-permute-start | bytes 933896 | tf_op jit(solution)/shard_map/ppermute | solution.py:475
  10.1 0.9 %shard_map.83 = (f32[2,152,256]{2,1,0:T(8,128)S(1)}, f32[2,104,256]{2,1,0:T(8,128)S(1)}) custom-call(s32[2]{0:T(128)S(1)} %pad_add_fusion.offsets, f32[1,2,256,1024]{3,2,1,0:T(8,128)S(1)} %shard_map.82.strip), custom_call_target="tpu_custom_call" | custom-call | tf_op jit(solution)/shard_map/pallas_call | solution.py:400
  11.1 0.0 copy-start
  11.1 0.0 copy-start.1
  11.1 2.4 %shard_map.85 = (f32[256,256]{1,0:T(8,128)}, f32[256,256]{1,0:T(8,128)}, f32[256,256]{1,0:T(8,128)}) custom-call(f32[256,256]{1,0:T(8,128)S(1)} %copy-done.2, f32[1,256,256]{2,1,0:T(8,128)S(1)} %copy-done.3), custom_call_target="tpu_custom_call" | custom-call | flops 603979776 | bytes 1966080 | tf_op jit(solution)/shard_map/pallas_call | solution.py:169
  13.5 1.3 %collective-permute-start.1 = (f32[2,104,256]{2,1,0:T(8,128)S(1)}, f32[2,104,256]{2,1,0:T(8,128)S(1)}, u32[]{:S(2)}, u32[]{:S(2)}) collective-permute-start(f32[2,104,256]{2,1,0:T(8,128)S(1)} %get-tuple-element.29), channel_id=1, source_target_pairs={{4,0},{8,4},{12,8},{16,12},{20,16},{24,20},{28,24},{5,1},{9,5},{13... | collective-permute-start | bytes 638984 | tf_op jit(solution)/shard_map/ppermute | solution.py:475
  14.8 5.9 %collective-permute-done.2 = f32[2,152,256]{2,1,0:T(8,128)S(1)} collective-permute-done((f32[2,152,256]{2,1,0:T(8,128)S(1)}, f32[2,152,256]{2,1,0:T(8,128)S(1)}, u32[]{:S(2)}, u32[]{:S(2)}) %collective-permute-start.2) | collective-permute-done | bytes 311328 | tf_op jit(solution)/shard_map/ppermute | solution.py:475
  20.8 0.1 broadcast_select_fusion.refs_0_
  20.9 1.6 %collective-permute-start.3 = (f32[2,152,256]{2,1,0:T(8,128)S(1)}, f32[2,152,256]{2,1,0:T(8,128)}, u32[]{:S(2)}, u32[]{:S(2)}) collective-permute-start(f32[2,152,256]{2,1,0:T(8,128)S(1)} %broadcast_select_fusion.refs_0_), channel_id=1, source_target_pairs={{0,2},{1,3},{2,0},{3,1},{4,6},{5,7},{6,4},{7,5},{8,10},{9,11},{10,... | collective-permute-start | bytes 933896 | tf_op jit(solution)/shard_map/ppermute | solution.py:480
  22.4 1.7 %collective-permute-done.1 = f32[2,104,256]{2,1,0:T(8,128)S(1)} collective-permute-done((f32[2,104,256]{2,1,0:T(8,128)S(1)}, f32[2,104,256]{2,1,0:T(8,128)S(1)}, u32[]{:S(2)}, u32[]{:S(2)}) %collective-permute-start.1) | collective-permute-done | bytes 213024 | tf_op jit(solution)/shard_map/ppermute | solution.py:475
  24.1 0.1 broadcast_select_fusion.1.refs_1_
  24.2 0.6 collective-permute-start.5
  24.8 1.5 %collective-permute-start.6 = (f32[2,104,256]{2,1,0:T(8,128)S(1)}, f32[2,104,256]{2,1,0:T(8,128)}, u32[]{:S(2)}, u32[]{:S(2)}) collective-permute-start(f32[2,104,256]{2,1,0:T(8,128)S(1)} %broadcast_select_fusion.1.refs_1_), channel_id=1, source_target_pairs={{0,2},{1,3},{2,0},{3,1},{4,6},{5,7},{6,4},{7,5},{8,10},{9,11},{10,... | collective-permute-start | bytes 638984 | tf_op jit(solution)/shard_map/ppermute | solution.py:480
  26.3 2.0 %collective-permute-done.3.refs_4_ = f32[2,152,256]{2,1,0:T(8,128)} collective-permute-done((f32[2,152,256]{2,1,0:T(8,128)S(1)}, f32[2,152,256]{2,1,0:T(8,128)}, u32[]{:S(2)}, u32[]{:S(2)}) %collective-permute-start.3) | collective-permute-done | bytes 311328 | tf_op jit(solution)/shard_map/ppermute | solution.py:480
  28.3 0.0 collective-permute-start.7
  28.3 4.2 %shard_map.86.refs_12_ = f32[2,2,256,256]{3,2,1,0:T(8,128)S(1)} custom-call(s32[1]{0:T(128)} %bitcast.cut_ref, f32[2,152,256]{2,1,0:T(8,128)S(1)} %broadcast_select_fusion.refs_0_, f32[2,104,256]{2,1,0:T(8,128)S(1)} %broadcast_select_fusion.1.refs_1_, f32[2,152,256]{2,1,0:T(8,128)S(1)} %collective-permute-done.4.refs_2_, ...), custom_call_target="tpu_custom_call" | custom-call | flops 65536 | bytes 4096 | tf_op jit(solution)/shard_map/pallas_call | solution.py:237
  32.5 0.6 collective-permute-start.8
  33.1 1.3 %collective-permute-done.8.refs_7_ = f32[2,104,256]{2,1,0:T(8,128)S(1)} collective-permute-done((f32[2,104,256]{2,1,0:T(8,128)}, f32[2,104,256]{2,1,0:T(8,128)S(1)}, u32[]{:S(2)}, u32[]{:S(2)}) %collective-permute-start.8) | collective-permute-done | bytes 213024 | tf_op jit(solution)/shard_map/ppermute | solution.py:480
  34.4 7.9 %shard_map.87 = (f32[256,256]{1,0:T(8,128)S(1)}, f32[256,256]{1,0:T(8,128)S(1)}) custom-call(s32[1]{0:T(128)} %bitcast.cut_ref, f32[2,152,256]{2,1,0:T(8,128)S(1)} %broadcast_select_fusion.refs_0_, f32[2,104,256]{2,1,0:T(8,128)S(1)} %broadcast_select_fusion.1.refs_1_, f32[2,152,256]{2,1,0:T(8,128)S(1)} %collective-permute-done.4.refs_2_, ...), custom_call_target="tpu_custom_call" | custom-call | flops 4026531840 | bytes 1048576 | tf_op jit(solution)/shard_map/pallas_call | solution.py:346
  42.3 3.9 %collective-permute-start.10 = (f32[256,256]{1,0:T(8,128)S(1)}, f32[256,256]{1,0:T(8,128)S(1)}, u32[]{:S(2)}, u32[]{:S(2)}) collective-permute-start(f32[256,256]{1,0:T(8,128)S(1)} %get-tuple-element.47.re), channel_id=1, source_target_pairs={{0,4},{4,8},{8,12},{12,16},{16,20},{20,24},{24,28},{1,5},{5,9},{9,... | collective-permute-start | bytes 786440 | tf_op jit(solution)/shard_map/ppermute | solution.py:475
  46.3 2.7 %collective-permute-start.9 = (f32[256,256]{1,0:T(8,128)S(1)}, f32[256,256]{1,0:T(8,128)S(1)}, u32[]{:S(2)}, u32[]{:S(2)}) collective-permute-start(f32[256,256]{1,0:T(8,128)S(1)} %get-tuple-element.46.im), channel_id=1, source_target_pairs={{0,4},{4,8},{8,12},{12,16},{16,20},{20,24},{24,28},{1,5},{5,9},{9,... | collective-permute-start | bytes 786440 | tf_op jit(solution)/shard_map/ppermute | solution.py:475
  49.0 2.5 %shard_map.88 = (f32[1,2,256,1024]{3,2,1,0:T(8,128)}, f32[256,384]{1,0:T(8,128)S(1)}, f32[256,384]{1,0:T(8,128)S(1)}) custom-call(s32[2]{0:T(128)S(1)} %pad_add_fusion.offsets, s32[2]{0:T(128)S(1)} %collective-permute-done.offsets.came_offsets, f32[256,256]{1,0:T(8,128)S(1)} %get-tuple-element.47.re, f32[256,256]{1,0:T(8,128)S(1)} %get-tuple-element.46.im), custom_call_target="tpu_custom_call" | custom-call | tf_op jit(solution)/shard_map/pallas_call | solution.py:430
  51.5 1.5 %collective-permute-done.10.came = f32[256,256]{1,0:T(8,128)S(1)} collective-permute-done((f32[256,256]{1,0:T(8,128)S(1)}, f32[256,256]{1,0:T(8,128)S(1)}, u32[]{:S(2)}, u32[]{:S(2)}) %collective-permute-start.10) | collective-permute-done | bytes 262176 | tf_op jit(solution)/shard_map/ppermute | solution.py:475
  53.0 1.5 %shard_map.89.base = f32[1,2,256,1024]{3,2,1,0:T(8,128)} custom-call(s32[2]{0:T(128)S(1)} %collective-permute-done.offsets.came_offsets, f32[256,256]{1,0:T(8,128)S(1)} %collective-permute-done.10.came, f32[256,384]{1,0:T(8,128)S(1)} %get-tuple-element.49.run, f32[1,2,256,1024]{3,2,1,0:T(8,128)} %get-tuple-element.50.base), custom_call_target="tpu_custom_call", output_to_operand_aliasing={{}: (3, {})} | custom-call | tf_op jit(solution)/shard_map/pallas_call | solution.py:461
  54.5 2.1 %collective-permute-done.9.came = f32[256,256]{1,0:T(8,128)S(1)} collective-permute-done((f32[256,256]{1,0:T(8,128)S(1)}, f32[256,256]{1,0:T(8,128)S(1)}, u32[]{:S(2)}, u32[]{:S(2)}) %collective-permute-start.9) | collective-permute-done | bytes 262176 | tf_op jit(solution)/shard_map/ppermute | solution.py:475
  56.6 1.5 %shard_map.90 = f32[1,2,256,1024]{3,2,1,0:T(8,128)} custom-call(s32[2]{0:T(128)S(1)} %collective-permute-done.offsets.came_offsets, f32[256,256]{1,0:T(8,128)S(1)} %collective-permute-done.9.came, f32[256,384]{1,0:T(8,128)S(1)} %get-tuple-element.48.run, f32[1,2,256,1024]{3,2,1,0:T(8,128)} %shard_map.89.base), custom_call_target="tpu_custom_call", output_to_operand_aliasing={{}: (3, {})} | custom-call | tf_op jit(solution)/shard_map/pallas_call | solution.py:461
  (12 shorter events, 0.0 us)
Async XLA Ops:
  1.4 6.5 %collective-permute-start = (s32[2]{0:T(128)S(1)}, s32[2]{0:T(128)S(1)}, u32[]{:S(2)}, u32[]{:S(2)}) collective-permute-start(s32[2]{0:T(128)S(1)} %pad_add_fusion.offsets), channel_id=1, source_target_pairs={{0,4},{4,8},{8,12},{12,16},{16,20},{20,24},{24,28},{1,5},{5,9},{9,... | collective-permute-start | bytes 32 | tf_op jit(solution)/shard_map/ppermute | solution.py:475
  7.8 3.2 %copy-start.2 = (f32[256,256]{1,0:T(8,128)S(1)}, f32[256,256]{1,0:T(8,128)}, u32[]{:S(2)}) copy-start(f32[256,256]{1,0:T(8,128)} %phase.1) | copy-start | bytes 786436
  7.9 3.2 %copy-start.3 = (f32[1,256,256]{2,1,0:T(8,128)S(1)}, f32[1,256,256]{2,1,0:T(8,128)}, u32[]{:S(2)}) copy-start(f32[1,256,256]{2,1,0:T(8,128)} %refs_0_.1) | copy-start | bytes 786436
  8.8 12.0 %collective-permute-start.2 = (f32[2,152,256]{2,1,0:T(8,128)S(1)}, f32[2,152,256]{2,1,0:T(8,128)S(1)}, u32[]{:S(2)}, u32[]{:S(2)}) collective-permute-start(f32[2,152,256]{2,1,0:T(8,128)S(1)} %get-tuple-element.31), channel_id=1, source_target_pairs={{4,0},{8,4},{12,8},{16,12},{20,16},{24,20},{28,24},{5,1},{9,5},{13... | collective-permute-start | bytes 933896 | tf_op jit(solution)/shard_map/ppermute | solution.py:475
  11.1 17.3 %copy-start = (bf16[4,768,256]{2,1,0:T(8,128)(2,1)S(1)}, bf16[4,768,256]{2,1,0:T(8,128)(2,1)}, u32[]{:S(2)}) copy-start(bf16[4,768,256]{2,1,0:T(8,128)(2,1)} %constant.13.clone.refs_7_.refs_13_) | copy-start | bytes 4718596
  11.1 17.2 %copy-start.1 = (bf16[8,256,256]{2,1,0:T(8,128)(2,1)S(1)}, bf16[8,256,256]{2,1,0:T(8,128)(2,1)}, u32[]{:S(2)}) copy-start(bf16[8,256,256]{2,1,0:T(8,128)(2,1)} %constant.14.clone.refs_8_.refs_14_) | copy-start | bytes 3145732
  13.5 10.5 %collective-permute-start.1 = (f32[2,104,256]{2,1,0:T(8,128)S(1)}, f32[2,104,256]{2,1,0:T(8,128)S(1)}, u32[]{:S(2)}, u32[]{:S(2)}) collective-permute-start(f32[2,104,256]{2,1,0:T(8,128)S(1)} %get-tuple-element.29), channel_id=1, source_target_pairs={{4,0},{8,4},{12,8},{16,12},{20,16},{24,20},{28,24},{5,1},{9,5},{13... | collective-permute-start | bytes 638984 | tf_op jit(solution)/shard_map/ppermute | solution.py:475
  20.9 7.4 %collective-permute-start.3 = (f32[2,152,256]{2,1,0:T(8,128)S(1)}, f32[2,152,256]{2,1,0:T(8,128)}, u32[]{:S(2)}, u32[]{:S(2)}) collective-permute-start(f32[2,152,256]{2,1,0:T(8,128)S(1)} %broadcast_select_fusion.refs_0_), channel_id=1, source_target_pairs={{0,2},{1,3},{2,0},{3,1},{4,6},{5,7},{6,4},{7,5},{8,10},{9,11},{10,... | collective-permute-start | bytes 933896 | tf_op jit(solution)/shard_map/ppermute | solution.py:480
  24.1 2.2 %collective-permute-start.4 = (f32[2,152,256]{2,1,0:T(8,128)S(1)}, f32[2,152,256]{2,1,0:T(8,128)S(1)}, u32[]{:S(2)}, u32[]{:S(2)}) collective-permute-start(f32[2,152,256]{2,1,0:T(8,128)S(1)} %broadcast_select_fusion.refs_0_), channel_id=1, source_target_pairs={{0,1},{1,0},{2,3},{3,2},{4,5},{5,4},{6,7},{7,6},{8,9},{9,8},{10,11... | collective-permute-start | bytes 933896 | tf_op jit(solution)/shard_map/ppermute | solution.py:480
  24.2 4.1 %collective-permute-start.5 = (f32[2,104,256]{2,1,0:T(8,128)S(1)}, f32[2,104,256]{2,1,0:T(8,128)}, u32[]{:S(2)}, u32[]{:S(2)}) collective-permute-start(f32[2,104,256]{2,1,0:T(8,128)S(1)} %broadcast_select_fusion.1.refs_1_), channel_id=1, source_target_pairs={{0,1},{1,0},{2,3},{3,2},{4,5},{5,4},{6,7},{7,6},{8,9},{9,8},{10,11... | collective-permute-start | bytes 638984 | tf_op jit(solution)/shard_map/ppermute | solution.py:480
  24.8 7.8 %collective-permute-start.6 = (f32[2,104,256]{2,1,0:T(8,128)S(1)}, f32[2,104,256]{2,1,0:T(8,128)}, u32[]{:S(2)}, u32[]{:S(2)}) collective-permute-start(f32[2,104,256]{2,1,0:T(8,128)S(1)} %broadcast_select_fusion.1.refs_1_), channel_id=1, source_target_pairs={{0,2},{1,3},{2,0},{3,1},{4,6},{5,7},{6,4},{7,5},{8,10},{9,11},{10,... | collective-permute-start | bytes 638984 | tf_op jit(solution)/shard_map/ppermute | solution.py:480
  28.3 6.1 %collective-permute-start.7 = (f32[2,152,256]{2,1,0:T(8,128)}, f32[2,152,256]{2,1,0:T(8,128)}, u32[]{:S(2)}, u32[]{:S(2)}) collective-permute-start(f32[2,152,256]{2,1,0:T(8,128)} %collective-permute-done.3.refs_4_), channel_id=1, source_target_pairs={{0,1},{1,0},{2,3},{3,2},{4,5},{5,4},{6,7},{7,6},{8,9},{9,8},{10,11... | collective-permute-start | bytes 933896 | tf_op jit(solution)/shard_map/ppermute | solution.py:480
  32.5 1.9 %collective-permute-start.8 = (f32[2,104,256]{2,1,0:T(8,128)}, f32[2,104,256]{2,1,0:T(8,128)S(1)}, u32[]{:S(2)}, u32[]{:S(2)}) collective-permute-start(f32[2,104,256]{2,1,0:T(8,128)} %collective-permute-done.6.refs_5_), channel_id=1, source_target_pairs={{0,1},{1,0},{2,3},{3,2},{4,5},{5,4},{6,7},{7,6},{8,9},{9,8},{10,11... | collective-permute-start | bytes 638984 | tf_op jit(solution)/shard_map/ppermute | solution.py:480
  42.3 10.7 %collective-permute-start.10 = (f32[256,256]{1,0:T(8,128)S(1)}, f32[256,256]{1,0:T(8,128)S(1)}, u32[]{:S(2)}, u32[]{:S(2)}) collective-permute-start(f32[256,256]{1,0:T(8,128)S(1)} %get-tuple-element.47.re), channel_id=1, source_target_pairs={{0,4},{4,8},{8,12},{12,16},{16,20},{20,24},{24,28},{1,5},{5,9},{9,... | collective-permute-start | bytes 786440 | tf_op jit(solution)/shard_map/ppermute | solution.py:475
  46.3 10.3 %collective-permute-start.9 = (f32[256,256]{1,0:T(8,128)S(1)}, f32[256,256]{1,0:T(8,128)S(1)}, u32[]{:S(2)}, u32[]{:S(2)}) collective-permute-start(f32[256,256]{1,0:T(8,128)S(1)} %get-tuple-element.46.im), channel_id=1, source_target_pairs={{0,4},{4,8},{8,12},{12,16},{16,20},{20,24},{24,28},{1,5},{5,9},{9,... | collective-permute-start | bytes 786440 | tf_op jit(solution)/shard_map/ppermute | solution.py:475

commit v8 on v7

--- a/solution.py
+++ b/solution.py
@@ -209,46 +209,51 @@
     return [refs[i * chunks : (i + 1) * chunks] for i in range(patches)], refs[patches * chunks :]
 
 
-def early_waves(cut, patches, probe, cosine, sine, tables):
-    n = probe.shape[1]
+def early_wave(cut, s, patches, before, cosine, sine, tables):
+    n = before.shape[1]
     chunks = len(patches[0])
 
     def kernel(cut_ref, *refs):
         sources, rest = grouped(refs, 2, chunks)
-        probe, cosine, sine, right, left, waves, patch, first, phase, sems, phase_sem = rest
+        before, cosine, sine, right, left, wave, patch, first, phase, sem, first_sem = rest
         me = cut_ref[0]
-        pairs = ((probe, first), (cosine, phase.at[0]), (sine, phase.at[1]))
-        copies = [pltpu.make_async_copy(x, y, phase_sem.at[i]) for i, (x, y) in enumerate(pairs)]
+        pairs = ((before, first), (cosine, phase.at[0]), (sine, phase.at[1]))
+        copies = [pltpu.make_async_copy(x, y, first_sem.at[i]) for i, (x, y) in enumerate(pairs)]
+
+        for i in range(2):
+
+            @pl.when(me == s ^ i)
+            def _(i=i):
+                start_chunks(sources[i], patch, 0, sem)
 
         @pl.when(me < 2)
         def _():
-            fetch_patches(me, sources, patch, sems, (0, 1))
             for copy in copies:
                 copy.start()
-            before = first
-            for s in range(2):
-                wait_slot(patch, s, sems.at[s])
-                if s == 0:
-                    for copy in copies:
-                        copy.wait()
-                run_forward(s, before, patch.at[s], waves.at[s], phase.at[0], phase.at[1], (right, left))
-                before = waves.at[s]
-
-    return pl.pallas_call(
-        kernel,
-        out_shape=jax.ShapeDtypeStruct((2, 2, n, n), f32),
+            wait_slot(patch, 0, sem)
+            copies[0].wait()
+
+            def ready():
+                copies[1].wait()
+                copies[2].wait()
+
+            run_forward(s, first, patch.at[0], wave, phase.at[0], phase.at[1], (right, left), ready)
+
+    return pl.pallas_call(
+        kernel,
+        out_shape=jax.ShapeDtypeStruct((2, n, n), f32),
         in_specs=[SMEM] + [ANY] * (2 * chunks + 3) + [VMEM] * 2,
         out_specs=VMEM,
         scratch_shapes=[
-            pltpu.VMEM((2, 2, n, n), f32),
+            pltpu.VMEM((1, 2, n, n), f32),
             pltpu.VMEM((2, n, n), f32),
             pltpu.VMEM((2, n, n), f32),
-            pltpu.SemaphoreType.DMA((2,)),
+            pltpu.SemaphoreType.DMA,
             pltpu.SemaphoreType.DMA((3,)),
         ],
         compiler_params=PARAMS,
         cost_estimate=SHORT,
-    )(cut, *flatten(patches[:2]), *map(pinned, (probe, cosine, sine)), *tables)
+    )(cut, *flatten(patches[:2]), before, *map(pinned, (cosine, sine)), *tables)
 
 
 def flatten(patches):
@@ -259,7 +264,7 @@
     n = probe.shape[1]
     sections = len(patches)
     chunks = len(patches[0])
-    planes_in = [cosine, sine, observed, probe, early]
+    planes_in = [cosine, sine, observed, probe, *early]
 
     def kernel(cut_ref, *refs):
         sources, rest = grouped(refs, sections, chunks)
@@ -286,7 +291,7 @@
                     spectrum = by_phase(forward(gr, gi, tables), cosine[...], sine[...], conj_times)
                     back(s - 1, *inverse(spectrum, tables))
 
-        early_copies = [pltpu.make_async_copy(planes[4].at[s], waves.at[s], early_sem.at[s]) for s in range(2)]
+        early_copies = [pltpu.make_async_copy(planes[4 + s], waves.at[s], early_sem.at[s]) for s in range(2)]
         for odd in range(2):
 
             @pl.when(me % 2 == odd)
@@ -359,7 +364,7 @@
         ],
         compiler_params=PARAMS,
         cost_estimate=pl.CostEstimate(flops=10 * 24 * n**3, bytes_accessed=16 * n * n, transcendentals=0),
-    )(cut, *flatten(patches), *map(pinned, (cosine, sine, observed, probe)), early, *tables)
+    )(cut, *flatten(patches), *map(pinned, (cosine, sine, observed, probe)), *early, *tables)
 
 
 def window_start(column, width, columns):
@@ -514,9 +519,10 @@
         chunk = chunks[-1]
         across.append(swapped(chunk, 2))
     beside = [swapped(chunk, 1) for chunk in chunks]
-    across[0], beside[0] = after(across[0], beside[0])
-    early = early_waves(cut, [chunks, beside], probe, cosine, sine, tables)
-    across[1], early = after(across[1], early)
+    early = [early_wave(cut, 0, [chunks, beside], pinned(probe), cosine, sine, tables)]
+    across[0], early[0] = after(across[0], early[0])
+    early.append(early_wave(cut, 1, [chunks, beside], early[0], cosine, sine, tables))
+    across[1], early[1] = after(across[1], early[1])
     opposite = [swapped(chunk, 1) for chunk in across]
     planes = chain(cut, [chunks, beside, across, opposite], early, probe, cosine, sine, observed, tables)
 

time: 58.4 us -> 58.2 us (level)
  waiting for transfers between devices: 14.6 us -> 13.3 us
  Pallas kernels: 23.4 us -> 24.4 us
    pallas_call x1 -> x2, Pallas kernels: 4.2 us -> 5.18 us  [early_wave(): pl.pallas_call(kernel, out_shape=jax.ShapeDtypeStruct((2, n, n), f32), in...]
    ppermute x6, waiting for transfers between devices: 3.35 us -> 2.59 us  [swapped(): return lax.ppermute(value, 'cuts', [(i, i ^ bit) for i in range(devices)])]
  transfers between devices with their start and end apart: 11 -> 11, of which waited for: 6 -> 6; matrix products, arithmetic and copies ran while one was open for 0% -> 0% of each run, Pallas kernels for 23% -> 24%
where the time goes in v8:
time: 58.2 us; the launch traced here: 57.5 us
  Pallas kernels  24.4 us (42%)
  starting transfers between devices  18 us (31%)
  waiting for transfers between devices  13.3 us (23%)
  between operations  1.51 us (3%)
    ppermute x5, starting transfers between devices, shifted(): return lax.ppermute(value, 'tile', pairs)  14.3 us
    ppermute x5, waiting for transfers between devices, shifted(): return lax.ppermute(value, 'tile', pairs)  10.7 us
    pallas_call x1, Pallas kernels, chain(): pl.pallas_call(kernel, out_shape=[jax.ShapeDtypeStruct((n, n), f32)] * 2,...  7.92 us
    pallas_call x2, Pallas kernels, early_wave(): pl.pallas_call(kernel, out_shape=jax.ShapeDtypeStruct((2, n, n), f32), in...  5.18 us
    ppermute x6, starting transfers between devices, swapped(): return lax.ppermute(value, 'cuts', [(i, i ^ bit) for i in range(devices)])  3.76 us
    pallas_call x2, Pallas kernels, add_came(): pl.pallas_call(kernel, out_shape=jax.ShapeDtypeStruct(base.shape, f32), i...  2.95 us
    ppermute x6, waiting for transfers between devices, swapped(): return lax.ppermute(value, 'cuts', [(i, i ^ bit) for i in range(devices)])  2.59 us
    pallas_call x1, Pallas kernels, place_own(): pl.pallas_call(kernel, out_shape=[jax.ShapeDtypeStruct((1, 2, rows, colum...  2.49 us
  transfers between devices with their start and end apart: 11, of which 6 were waited for; matrix products, arithmetic and copies ran while one was open for 0% of the time, Pallas kernels for 24%

profile of v8, /device:TPU:0, one launch (start us, length us, event | category | flops | bytes accessed | tf_op | source)
XLA Modules:
  0.0 57.5 jit_solution(4897580469982513355)
XLA Ops:
  1.3 0.1 pad_add_fusion.offsets
  1.4 4.9 %collective-permute-start = (s32[2]{0:T(128)S(1)}, s32[2]{0:T(128)S(1)}, u32[]{:S(2)}, u32[]{:S(2)}) collective-permute-start(s32[2]{0:T(128)S(1)} %pad_add_fusion.offsets), channel_id=1, source_target_pairs={{0,4},{4,8},{8,12},{12,16},{16,20},{20,24},{24,28},{1,5},{5,9},{9,... | collective-permute-start | bytes 32 | tf_op jit(solution)/shard_map/ppermute | solution.py:480
  6.2 1.6 %shard_map.82.strip = f32[1,2,256,1024]{3,2,1,0:T(8,128)S(1)} custom-call(f32[1,2,256,1024]{3,2,1,0:T(8,128)} %strip.1), custom_call_target="tpu_custom_call" | custom-call | tf_op jit(solution)/shard_map/pallas_call | solution.py:381
  7.8 0.0 copy-start.2
  7.9 0.0 copy-start.3
  7.9 0.9 %shard_map.84 = (f32[2,152,256]{2,1,0:T(8,128)S(1)}, f32[2,104,256]{2,1,0:T(8,128)S(1)}) custom-call(s32[2]{0:T(128)S(1)} %collective-permute-done.offsets.came_offsets, f32[1,2,256,1024]{3,2,1,0:T(8,128)S(1)} %shard_map.82.strip), custom_call_target="tpu_custom_call" | custom-call | tf_op jit(solution)/shard_map/pallas_call | solution.py:405
  8.8 1.3 %collective-permute-start.2 = (f32[2,152,256]{2,1,0:T(8,128)S(1)}, f32[2,152,256]{2,1,0:T(8,128)S(1)}, u32[]{:S(2)}, u32[]{:S(2)}) collective-permute-start(f32[2,152,256]{2,1,0:T(8,128)S(1)} %get-tuple-element.31), channel_id=1, source_target_pairs={{4,0},{8,4},{12,8},{16,12},{20,16},{24,20},{28,24},{5,1},{9,5},{13... | collective-permute-start | bytes 933896 | tf_op jit(solution)/shard_map/ppermute | solution.py:480
  10.1 0.9 %shard_map.83 = (f32[2,152,256]{2,1,0:T(8,128)S(1)}, f32[2,104,256]{2,1,0:T(8,128)S(1)}) custom-call(s32[2]{0:T(128)S(1)} %pad_add_fusion.offsets, f32[1,2,256,1024]{3,2,1,0:T(8,128)S(1)} %shard_map.82.strip), custom_call_target="tpu_custom_call" | custom-call | tf_op jit(solution)/shard_map/pallas_call | solution.py:405
  11.1 0.0 copy-start
  11.1 0.0 copy-start.1
  11.1 2.4 %shard_map.85 = (f32[256,256]{1,0:T(8,128)}, f32[256,256]{1,0:T(8,128)}, f32[256,256]{1,0:T(8,128)}) custom-call(f32[256,256]{1,0:T(8,128)S(1)} %copy-done.2, f32[1,256,256]{2,1,0:T(8,128)S(1)} %copy-done.3), custom_call_target="tpu_custom_call" | custom-call | flops 603979776 | bytes 1966080 | tf_op jit(solution)/shard_map/pallas_call | solution.py:169
  13.5 1.3 %collective-permute-start.1 = (f32[2,104,256]{2,1,0:T(8,128)S(1)}, f32[2,104,256]{2,1,0:T(8,128)S(1)}, u32[]{:S(2)}, u32[]{:S(2)}) collective-permute-start(f32[2,104,256]{2,1,0:T(8,128)S(1)} %get-tuple-element.29), channel_id=1, source_target_pairs={{4,0},{8,4},{12,8},{16,12},{20,16},{24,20},{28,24},{5,1},{9,5},{13... | collective-permute-start | bytes 638984 | tf_op jit(solution)/shard_map/ppermute | solution.py:480
  14.8 6.0 %collective-permute-done.2 = f32[2,152,256]{2,1,0:T(8,128)S(1)} collective-permute-done((f32[2,152,256]{2,1,0:T(8,128)S(1)}, f32[2,152,256]{2,1,0:T(8,128)S(1)}, u32[]{:S(2)}, u32[]{:S(2)}) %collective-permute-start.2) | collective-permute-done | bytes 311328 | tf_op jit(solution)/shard_map/ppermute | solution.py:480
  20.8 0.1 broadcast_select_fusion.refs_0_
  20.9 1.6 %collective-permute-start.5 = (f32[2,152,256]{2,1,0:T(8,128)S(1)}, f32[2,152,256]{2,1,0:T(8,128)}, u32[]{:S(2)}, u32[]{:S(2)}) collective-permute-start(f32[2,152,256]{2,1,0:T(8,128)S(1)} %broadcast_select_fusion.refs_0_), channel_id=1, source_target_pairs={{0,2},{1,3},{2,0},{3,1},{4,6},{5,7},{6,4},{7,5},{8,10},{9,11},{10,... | collective-permute-start | bytes 933896 | tf_op jit(solution)/shard_map/ppermute | solution.py:485
  22.5 1.6 %collective-permute-done.1 = f32[2,104,256]{2,1,0:T(8,128)S(1)} collective-permute-done((f32[2,104,256]{2,1,0:T(8,128)S(1)}, f32[2,104,256]{2,1,0:T(8,128)S(1)}, u32[]{:S(2)}, u32[]{:S(2)}) %collective-permute-start.1) | collective-permute-done | bytes 213024 | tf_op jit(solution)/shard_map/ppermute | solution.py:480
  24.1 0.1 broadcast_select_fusion.1.refs_1_
  24.2 0.6 collective-permute-start.4
  24.8 1.5 %collective-permute-start.6 = (f32[2,104,256]{2,1,0:T(8,128)S(1)}, f32[2,104,256]{2,1,0:T(8,128)}, u32[]{:S(2)}, u32[]{:S(2)}) collective-permute-start(f32[2,104,256]{2,1,0:T(8,128)S(1)} %broadcast_select_fusion.1.refs_1_), channel_id=1, source_target_pairs={{0,2},{1,3},{2,0},{3,1},{4,6},{5,7},{6,4},{7,5},{8,10},{9,11},{10,... | collective-permute-start | bytes 638984 | tf_op jit(solution)/shard_map/ppermute | solution.py:485
  26.3 2.7 %shard_map.86.refs_4_.refs_12_ = f32[2,256,256]{2,1,0:T(8,128)S(1)} custom-call(s32[1]{0:T(128)} %bitcast.cut_ref, f32[2,152,256]{2,1,0:T(8,128)S(1)} %broadcast_select_fusion.refs_0_, f32[2,104,256]{2,1,0:T(8,128)S(1)} %broadcast_select_fusion.1.refs_1_, f32[2,152,256]{2,1,0:T(8,128)S(1)} %collective-permute-done.3.refs_2_, ...), custom_call_target="tpu_custom_call" | custom-call | flops 65536 | bytes 4096 | tf_op jit(solution)/shard_map/pallas_call | solution.py:242
  29.0 0.1 collective-permute-start.7
  29.2 2.5 %shard_map.87.refs_13_ = f32[2,256,256]{2,1,0:T(8,128)S(1)} custom-call(s32[1]{0:T(128)} %bitcast.cut_ref, f32[2,152,256]{2,1,0:T(8,128)S(1)} %broadcast_select_fusion.refs_0_, f32[2,104,256]{2,1,0:T(8,128)S(1)} %broadcast_select_fusion.1.refs_1_, f32[2,152,256]{2,1,0:T(8,128)S(1)} %collective-permute-done.3.refs_2_, ...), custom_call_target="tpu_custom_call" | custom-call | flops 65536 | bytes 4096 | tf_op jit(solution)/shard_map/pallas_call | solution.py:242
  31.6 0.9 %collective-permute-done.6.refs_5_ = f32[2,104,256]{2,1,0:T(8,128)} collective-permute-done((f32[2,104,256]{2,1,0:T(8,128)S(1)}, f32[2,104,256]{2,1,0:T(8,128)}, u32[]{:S(2)}, u32[]{:S(2)}) %collective-permute-start.6) | collective-permute-done | bytes 213024 | tf_op jit(solution)/shard_map/ppermute | solution.py:485
  32.5 1.7 %collective-permute-done.8.refs_7_ = f32[2,104,256]{2,1,0:T(8,128)S(1)} collective-permute-done((f32[2,104,256]{2,1,0:T(8,128)}, f32[2,104,256]{2,1,0:T(8,128)S(1)}, u32[]{:S(2)}, u32[]{:S(2)}) %collective-permute-start.8) | collective-permute-done | bytes 213024 | tf_op jit(solution)/shard_map/ppermute | solution.py:485
  34.2 7.9 %shard_map.88 = (f32[256,256]{1,0:T(8,128)S(1)}, f32[256,256]{1,0:T(8,128)S(1)}) custom-call(s32[1]{0:T(128)} %bitcast.cut_ref, f32[2,152,256]{2,1,0:T(8,128)S(1)} %broadcast_select_fusion.refs_0_, f32[2,104,256]{2,1,0:T(8,128)S(1)} %broadcast_select_fusion.1.refs_1_, f32[2,152,256]{2,1,0:T(8,128)S(1)} %collective-permute-done.3.refs_2_, ...), custom_call_target="tpu_custom_call" | custom-call | flops 4026531840 | bytes 1048576 | tf_op jit(solution)/shard_map/pallas_call | solution.py:351
  42.1 4.1 %collective-permute-start.10 = (f32[256,256]{1,0:T(8,128)S(1)}, f32[256,256]{1,0:T(8,128)S(1)}, u32[]{:S(2)}, u32[]{:S(2)}) collective-permute-start(f32[256,256]{1,0:T(8,128)S(1)} %get-tuple-element.47.re), channel_id=1, source_target_pairs={{0,4},{4,8},{8,12},{12,16},{16,20},{20,24},{24,28},{1,5},{5,9},{9,... | collective-permute-start | bytes 786440 | tf_op jit(solution)/shard_map/ppermute | solution.py:480
  46.3 2.7 %collective-permute-start.9 = (f32[256,256]{1,0:T(8,128)S(1)}, f32[256,256]{1,0:T(8,128)S(1)}, u32[]{:S(2)}, u32[]{:S(2)}) collective-permute-start(f32[256,256]{1,0:T(8,128)S(1)} %get-tuple-element.46.im), channel_id=1, source_target_pairs={{0,4},{4,8},{8,12},{12,16},{16,20},{20,24},{24,28},{1,5},{5,9},{9,... | collective-permute-start | bytes 786440 | tf_op jit(solution)/shard_map/ppermute | solution.py:480
  49.0 2.5 %shard_map.89 = (f32[1,2,256,1024]{3,2,1,0:T(8,128)}, f32[256,384]{1,0:T(8,128)S(1)}, f32[256,384]{1,0:T(8,128)S(1)}) custom-call(s32[2]{0:T(128)S(1)} %pad_add_fusion.offsets, s32[2]{0:T(128)S(1)} %collective-permute-done.offsets.came_offsets, f32[256,256]{1,0:T(8,128)S(1)} %get-tuple-element.47.re, f32[256,256]{1,0:T(8,128)S(1)} %get-tuple-element.46.im), custom_call_target="tpu_custom_call" | custom-call | tf_op jit(solution)/shard_map/pallas_call | solution.py:435
  51.5 1.5 %collective-permute-done.10.came = f32[256,256]{1,0:T(8,128)S(1)} collective-permute-done((f32[256,256]{1,0:T(8,128)S(1)}, f32[256,256]{1,0:T(8,128)S(1)}, u32[]{:S(2)}, u32[]{:S(2)}) %collective-permute-start.10) | collective-permute-done | bytes 262176 | tf_op jit(solution)/shard_map/ppermute | solution.py:480
  53.0 1.5 %shard_map.90.base = f32[1,2,256,1024]{3,2,1,0:T(8,128)} custom-call(s32[2]{0:T(128)S(1)} %collective-permute-done.offsets.came_offsets, f32[256,256]{1,0:T(8,128)S(1)} %collective-permute-done.10.came, f32[256,384]{1,0:T(8,128)S(1)} %get-tuple-element.49.run, f32[1,2,256,1024]{3,2,1,0:T(8,128)} %get-tuple-element.50.base), custom_call_target="tpu_custom_call", output_to_operand_aliasing={{}: (3, {})} | custom-call | tf_op jit(solution)/shard_map/pallas_call | solution.py:466
  54.5 1.6 %collective-permute-done.9.came = f32[256,256]{1,0:T(8,128)S(1)} collective-permute-done((f32[256,256]{1,0:T(8,128)S(1)}, f32[256,256]{1,0:T(8,128)S(1)}, u32[]{:S(2)}, u32[]{:S(2)}) %collective-permute-start.9) | collective-permute-done | bytes 262176 | tf_op jit(solution)/shard_map/ppermute | solution.py:480
  56.1 1.5 %shard_map.91 = f32[1,2,256,1024]{3,2,1,0:T(8,128)} custom-call(s32[2]{0:T(128)S(1)} %collective-permute-done.offsets.came_offsets, f32[256,256]{1,0:T(8,128)S(1)} %collective-permute-done.9.came, f32[256,384]{1,0:T(8,128)S(1)} %get-tuple-element.48.run, f32[1,2,256,1024]{3,2,1,0:T(8,128)} %shard_map.90.base), custom_call_target="tpu_custom_call", output_to_operand_aliasing={{}: (3, {})} | custom-call | tf_op jit(solution)/shard_map/pallas_call | solution.py:466
  (13 shorter events, 0.0 us)
Async XLA Ops:
  1.4 6.5 %collective-permute-start = (s32[2]{0:T(128)S(1)}, s32[2]{0:T(128)S(1)}, u32[]{:S(2)}, u32[]{:S(2)}) collective-permute-start(s32[2]{0:T(128)S(1)} %pad_add_fusion.offsets), channel_id=1, source_target_pairs={{0,4},{4,8},{8,12},{12,16},{16,20},{20,24},{24,28},{1,5},{5,9},{9,... | collective-permute-start | bytes 32 | tf_op jit(solution)/shard_map/ppermute | solution.py:480
  7.8 3.2 %copy-start.2 = (f32[256,256]{1,0:T(8,128)S(1)}, f32[256,256]{1,0:T(8,128)}, u32[]{:S(2)}) copy-start(f32[256,256]{1,0:T(8,128)} %phase.1) | copy-start | bytes 786436
  7.9 3.2 %copy-start.3 = (f32[1,256,256]{2,1,0:T(8,128)S(1)}, f32[1,256,256]{2,1,0:T(8,128)}, u32[]{:S(2)}) copy-start(f32[1,256,256]{2,1,0:T(8,128)} %refs_0_.1) | copy-start | bytes 786436
  8.8 12.0 %collective-permute-start.2 = (f32[2,152,256]{2,1,0:T(8,128)S(1)}, f32[2,152,256]{2,1,0:T(8,128)S(1)}, u32[]{:S(2)}, u32[]{:S(2)}) collective-permute-start(f32[2,152,256]{2,1,0:T(8,128)S(1)} %get-tuple-element.31), channel_id=1, source_target_pairs={{4,0},{8,4},{12,8},{16,12},{20,16},{24,20},{28,24},{5,1},{9,5},{13... | collective-permute-start | bytes 933896 | tf_op jit(solution)/shard_map/ppermute | solution.py:480
  11.1 15.2 %copy-start = (bf16[4,768,256]{2,1,0:T(8,128)(2,1)S(1)}, bf16[4,768,256]{2,1,0:T(8,128)(2,1)}, u32[]{:S(2)}) copy-start(bf16[4,768,256]{2,1,0:T(8,128)(2,1)} %constant.13.clone.refs_7_.refs_14_) | copy-start | bytes 4718596
  11.1 15.2 %copy-start.1 = (bf16[8,256,256]{2,1,0:T(8,128)(2,1)S(1)}, bf16[8,256,256]{2,1,0:T(8,128)(2,1)}, u32[]{:S(2)}) copy-start(bf16[8,256,256]{2,1,0:T(8,128)(2,1)} %constant.14.clone.refs_8_.refs_15_) | copy-start | bytes 3145732
  13.5 10.6 %collective-permute-start.1 = (f32[2,104,256]{2,1,0:T(8,128)S(1)}, f32[2,104,256]{2,1,0:T(8,128)S(1)}, u32[]{:S(2)}, u32[]{:S(2)}) collective-permute-start(f32[2,104,256]{2,1,0:T(8,128)S(1)} %get-tuple-element.29), channel_id=1, source_target_pairs={{4,0},{8,4},{12,8},{16,12},{20,16},{24,20},{28,24},{5,1},{9,5},{13... | collective-permute-start | bytes 638984 | tf_op jit(solution)/shard_map/ppermute | solution.py:480
  20.9 8.1 %collective-permute-start.5 = (f32[2,152,256]{2,1,0:T(8,128)S(1)}, f32[2,152,256]{2,1,0:T(8,128)}, u32[]{:S(2)}, u32[]{:S(2)}) collective-permute-start(f32[2,152,256]{2,1,0:T(8,128)S(1)} %broadcast_select_fusion.refs_0_), channel_id=1, source_target_pairs={{0,2},{1,3},{2,0},{3,1},{4,6},{5,7},{6,4},{7,5},{8,10},{9,11},{10,... | collective-permute-start | bytes 933896 | tf_op jit(solution)/shard_map/ppermute | solution.py:485
  24.1 2.2 %collective-permute-start.3 = (f32[2,152,256]{2,1,0:T(8,128)S(1)}, f32[2,152,256]{2,1,0:T(8,128)S(1)}, u32[]{:S(2)}, u32[]{:S(2)}) collective-permute-start(f32[2,152,256]{2,1,0:T(8,128)S(1)} %broadcast_select_fusion.refs_0_), channel_id=1, source_target_pairs={{0,1},{1,0},{2,3},{3,2},{4,5},{5,4},{6,7},{7,6},{8,9},{9,8},{10,11... | collective-permute-start | bytes 933896 | tf_op jit(solution)/shard_map/ppermute | solution.py:485
  24.2 2.1 %collective-permute-start.4 = (f32[2,104,256]{2,1,0:T(8,128)S(1)}, f32[2,104,256]{2,1,0:T(8,128)}, u32[]{:S(2)}, u32[]{:S(2)}) collective-permute-start(f32[2,104,256]{2,1,0:T(8,128)S(1)} %broadcast_select_fusion.1.refs_1_), channel_id=1, source_target_pairs={{0,1},{1,0},{2,3},{3,2},{4,5},{5,4},{6,7},{7,6},{8,9},{9,8},{10,11... | collective-permute-start | bytes 638984 | tf_op jit(solution)/shard_map/ppermute | solution.py:485
  24.8 7.8 %collective-permute-start.6 = (f32[2,104,256]{2,1,0:T(8,128)S(1)}, f32[2,104,256]{2,1,0:T(8,128)}, u32[]{:S(2)}, u32[]{:S(2)}) collective-permute-start(f32[2,104,256]{2,1,0:T(8,128)S(1)} %broadcast_select_fusion.1.refs_1_), channel_id=1, source_target_pairs={{0,2},{1,3},{2,0},{3,1},{4,6},{5,7},{6,4},{7,5},{8,10},{9,11},{10,... | collective-permute-start | bytes 638984 | tf_op jit(solution)/shard_map/ppermute | solution.py:485
  29.0 5.2 %collective-permute-start.7 = (f32[2,152,256]{2,1,0:T(8,128)}, f32[2,152,256]{2,1,0:T(8,128)S(1)}, u32[]{:S(2)}, u32[]{:S(2)}) collective-permute-start(f32[2,152,256]{2,1,0:T(8,128)} %collective-permute-done.5.refs_4_), channel_id=1, source_target_pairs={{0,1},{1,0},{2,3},{3,2},{4,5},{5,4},{6,7},{7,6},{8,9},{9,8},{10,11... | collective-permute-start | bytes 933896 | tf_op jit(solution)/shard_map/ppermute | solution.py:485
  32.5 1.7 %collective-permute-start.8 = (f32[2,104,256]{2,1,0:T(8,128)}, f32[2,104,256]{2,1,0:T(8,128)S(1)}, u32[]{:S(2)}, u32[]{:S(2)}) collective-permute-start(f32[2,104,256]{2,1,0:T(8,128)} %collective-permute-done.6.refs_5_), channel_id=1, source_target_pairs={{0,1},{1,0},{2,3},{3,2},{4,5},{5,4},{6,7},{7,6},{8,9},{9,8},{10,11... | collective-permute-start | bytes 638984 | tf_op jit(solution)/shard_map/ppermute | solution.py:485
  42.1 10.8 %collective-permute-start.10 = (f32[256,256]{1,0:T(8,128)S(1)}, f32[256,256]{1,0:T(8,128)S(1)}, u32[]{:S(2)}, u32[]{:S(2)}) collective-permute-start(f32[256,256]{1,0:T(8,128)S(1)} %get-tuple-element.47.re), channel_id=1, source_target_pairs={{0,4},{4,8},{8,12},{12,16},{16,20},{20,24},{24,28},{1,5},{5,9},{9,... | collective-permute-start | bytes 786440 | tf_op jit(solution)/shard_map/ppermute | solution.py:480
  46.3 9.8 %collective-permute-start.9 = (f32[256,256]{1,0:T(8,128)S(1)}, f32[256,256]{1,0:T(8,128)S(1)}, u32[]{:S(2)}, u32[]{:S(2)}) collective-permute-start(f32[256,256]{1,0:T(8,128)S(1)} %get-tuple-element.46.im), channel_id=1, source_target_pairs={{0,4},{4,8},{8,12},{12,16},{16,20},{20,24},{24,28},{1,5},{5,9},{9,... | collective-permute-start | bytes 786440 | tf_op jit(solution)/shard_map/ppermute | solution.py:480

commit v9 on v7

--- a/solution.py
+++ b/solution.py
@@ -440,7 +440,7 @@
     rows, width = came.shape
     columns = base.shape[3]
 
-    parts = 4
+    parts = 8
     step = rows // parts
 
     def kernel(offsets, came, run, base, out, wide, sem):

time: 58.4 us -> 58.4 us (level)
  no operation moved by 1% of the time
where the time goes in v9:
time: 58.4 us; the launch traced here: 58.1 us
  Pallas kernels  23.4 us (40%)
  starting transfers between devices  18.3 us (31%)
  waiting for transfers between devices  14.6 us (25%)
  between operations  1.5 us (3%)
    ppermute x5, starting transfers between devices, shifted(): return lax.ppermute(value, 'tile', pairs)  14.1 us
    ppermute x5, waiting for transfers between devices, shifted(): return lax.ppermute(value, 'tile', pairs)  11.2 us
    pallas_call x1, Pallas kernels, chain(): pl.pallas_call(kernel, out_shape=[jax.ShapeDtypeStruct((n, n), f32)] * 2,...  7.91 us
    pallas_call x1, Pallas kernels, early_waves(): pl.pallas_call(kernel, out_shape=jax.ShapeDtypeStruct((2, 2, n, n), f32),...  4.2 us
    ppermute x6, starting transfers between devices, swapped(): return lax.ppermute(value, 'cuts', [(i, i ^ bit) for i in range(devices)])  4.19 us
    ppermute x6, waiting for transfers between devices, swapped(): return lax.ppermute(value, 'cuts', [(i, i ^ bit) for i in range(devices)])  3.35 us
    pallas_call x2, Pallas kernels, add_came(): pl.pallas_call(kernel, out_shape=jax.ShapeDtypeStruct(base.shape, f32), i...  2.96 us
    pallas_call x1, Pallas kernels, place_own(): pl.pallas_call(kernel, out_shape=[jax.ShapeDtypeStruct((1, 2, rows, colum...  2.49 us
  transfers between devices with their start and end apart: 11, of which 6 were waited for; matrix products, arithmetic and copies ran while one was open for 0% of the time, Pallas kernels for 23%

profile of v9, /device:TPU:0, one launch (start us, length us, event | category | flops | bytes accessed | tf_op | source)
XLA Modules:
  0.0 58.1 jit_solution(12700065307406479172)
XLA Ops:
  1.3 0.1 pad_add_fusion.offsets
  1.4 4.9 %collective-permute-start = (s32[2]{0:T(128)S(1)}, s32[2]{0:T(128)S(1)}, u32[]{:S(2)}, u32[]{:S(2)}) collective-permute-start(s32[2]{0:T(128)S(1)} %pad_add_fusion.offsets), channel_id=1, source_target_pairs={{0,4},{4,8},{8,12},{12,16},{16,20},{20,24},{24,28},{1,5},{5,9},{9,... | collective-permute-start | bytes 32 | tf_op jit(solution)/shard_map/ppermute | solution.py:475
  6.2 1.6 %shard_map.82.strip = f32[1,2,256,1024]{3,2,1,0:T(8,128)S(1)} custom-call(f32[1,2,256,1024]{3,2,1,0:T(8,128)} %strip.1), custom_call_target="tpu_custom_call" | custom-call | tf_op jit(solution)/shard_map/pallas_call | solution.py:376
  7.8 0.0 copy-start.2
  7.9 0.0 copy-start.3
  7.9 0.9 %shard_map.84 = (f32[2,152,256]{2,1,0:T(8,128)S(1)}, f32[2,104,256]{2,1,0:T(8,128)S(1)}) custom-call(s32[2]{0:T(128)S(1)} %collective-permute-done.offsets.came_offsets, f32[1,2,256,1024]{3,2,1,0:T(8,128)S(1)} %shard_map.82.strip), custom_call_target="tpu_custom_call" | custom-call | tf_op jit(solution)/shard_map/pallas_call | solution.py:400
  8.8 1.3 %collective-permute-start.2 = (f32[2,152,256]{2,1,0:T(8,128)S(1)}, f32[2,152,256]{2,1,0:T(8,128)S(1)}, u32[]{:S(2)}, u32[]{:S(2)}) collective-permute-start(f32[2,152,256]{2,1,0:T(8,128)S(1)} %get-tuple-element.31), channel_id=1, source_target_pairs={{4,0},{8,4},{12,8},{16,12},{20,16},{24,20},{28,24},{5,1},{9,5},{13... | collective-permute-start | bytes 933896 | tf_op jit(solution)/shard_map/ppermute | solution.py:475
  10.1 0.9 %shard_map.83 = (f32[2,152,256]{2,1,0:T(8,128)S(1)}, f32[2,104,256]{2,1,0:T(8,128)S(1)}) custom-call(s32[2]{0:T(128)S(1)} %pad_add_fusion.offsets, f32[1,2,256,1024]{3,2,1,0:T(8,128)S(1)} %shard_map.82.strip), custom_call_target="tpu_custom_call" | custom-call | tf_op jit(solution)/shard_map/pallas_call | solution.py:400
  11.1 0.0 copy-start
  11.1 0.0 copy-start.1
  11.1 2.4 %shard_map.85 = (f32[256,256]{1,0:T(8,128)}, f32[256,256]{1,0:T(8,128)}, f32[256,256]{1,0:T(8,128)}) custom-call(f32[256,256]{1,0:T(8,128)S(1)} %copy-done.2, f32[1,256,256]{2,1,0:T(8,128)S(1)} %copy-done.3), custom_call_target="tpu_custom_call" | custom-call | flops 603979776 | bytes 1966080 | tf_op jit(solution)/shard_map/pallas_call | solution.py:169
  13.5 1.3 %collective-permute-start.1 = (f32[2,104,256]{2,1,0:T(8,128)S(1)}, f32[2,104,256]{2,1,0:T(8,128)S(1)}, u32[]{:S(2)}, u32[]{:S(2)}) collective-permute-start(f32[2,104,256]{2,1,0:T(8,128)S(1)} %get-tuple-element.29), channel_id=1, source_target_pairs={{4,0},{8,4},{12,8},{16,12},{20,16},{24,20},{28,24},{5,1},{9,5},{13... | collective-permute-start | bytes 638984 | tf_op jit(solution)/shard_map/ppermute | solution.py:475
  14.8 5.9 %collective-permute-done.2 = f32[2,152,256]{2,1,0:T(8,128)S(1)} collective-permute-done((f32[2,152,256]{2,1,0:T(8,128)S(1)}, f32[2,152,256]{2,1,0:T(8,128)S(1)}, u32[]{:S(2)}, u32[]{:S(2)}) %collective-permute-start.2) | collective-permute-done | bytes 311328 | tf_op jit(solution)/shard_map/ppermute | solution.py:475
  20.8 0.1 broadcast_select_fusion.refs_0_
  20.9 1.6 %collective-permute-start.3 = (f32[2,152,256]{2,1,0:T(8,128)S(1)}, f32[2,152,256]{2,1,0:T(8,128)}, u32[]{:S(2)}, u32[]{:S(2)}) collective-permute-start(f32[2,152,256]{2,1,0:T(8,128)S(1)} %broadcast_select_fusion.refs_0_), channel_id=1, source_target_pairs={{0,2},{1,3},{2,0},{3,1},{4,6},{5,7},{6,4},{7,5},{8,10},{9,11},{10,... | collective-permute-start | bytes 933896 | tf_op jit(solution)/shard_map/ppermute | solution.py:480
  22.4 1.7 %collective-permute-done.1 = f32[2,104,256]{2,1,0:T(8,128)S(1)} collective-permute-done((f32[2,104,256]{2,1,0:T(8,128)S(1)}, f32[2,104,256]{2,1,0:T(8,128)S(1)}, u32[]{:S(2)}, u32[]{:S(2)}) %collective-permute-start.1) | collective-permute-done | bytes 213024 | tf_op jit(solution)/shard_map/ppermute | solution.py:475
  24.1 0.1 broadcast_select_fusion.1.refs_1_
  24.2 0.6 collective-permute-start.5
  24.8 1.5 %collective-permute-start.6 = (f32[2,104,256]{2,1,0:T(8,128)S(1)}, f32[2,104,256]{2,1,0:T(8,128)}, u32[]{:S(2)}, u32[]{:S(2)}) collective-permute-start(f32[2,104,256]{2,1,0:T(8,128)S(1)} %broadcast_select_fusion.1.refs_1_), channel_id=1, source_target_pairs={{0,2},{1,3},{2,0},{3,1},{4,6},{5,7},{6,4},{7,5},{8,10},{9,11},{10,... | collective-permute-start | bytes 638984 | tf_op jit(solution)/shard_map/ppermute | solution.py:480
  26.3 2.0 %collective-permute-done.3.refs_4_ = f32[2,152,256]{2,1,0:T(8,128)} collective-permute-done((f32[2,152,256]{2,1,0:T(8,128)S(1)}, f32[2,152,256]{2,1,0:T(8,128)}, u32[]{:S(2)}, u32[]{:S(2)}) %collective-permute-start.3) | collective-permute-done | bytes 311328 | tf_op jit(solution)/shard_map/ppermute | solution.py:480
  28.3 0.0 collective-permute-start.7
  28.3 4.2 %shard_map.86.refs_12_ = f32[2,2,256,256]{3,2,1,0:T(8,128)S(1)} custom-call(s32[1]{0:T(128)} %bitcast.cut_ref, f32[2,152,256]{2,1,0:T(8,128)S(1)} %broadcast_select_fusion.refs_0_, f32[2,104,256]{2,1,0:T(8,128)S(1)} %broadcast_select_fusion.1.refs_1_, f32[2,152,256]{2,1,0:T(8,128)S(1)} %collective-permute-done.4.refs_2_, ...), custom_call_target="tpu_custom_call" | custom-call | flops 65536 | bytes 4096 | tf_op jit(solution)/shard_map/pallas_call | solution.py:237
  32.5 0.6 collective-permute-start.8
  33.1 1.3 %collective-permute-done.8.refs_7_ = f32[2,104,256]{2,1,0:T(8,128)S(1)} collective-permute-done((f32[2,104,256]{2,1,0:T(8,128)}, f32[2,104,256]{2,1,0:T(8,128)S(1)}, u32[]{:S(2)}, u32[]{:S(2)}) %collective-permute-start.8) | collective-permute-done | bytes 213024 | tf_op jit(solution)/shard_map/ppermute | solution.py:480
  34.4 7.9 %shard_map.87 = (f32[256,256]{1,0:T(8,128)S(1)}, f32[256,256]{1,0:T(8,128)S(1)}) custom-call(s32[1]{0:T(128)} %bitcast.cut_ref, f32[2,152,256]{2,1,0:T(8,128)S(1)} %broadcast_select_fusion.refs_0_, f32[2,104,256]{2,1,0:T(8,128)S(1)} %broadcast_select_fusion.1.refs_1_, f32[2,152,256]{2,1,0:T(8,128)S(1)} %collective-permute-done.4.refs_2_, ...), custom_call_target="tpu_custom_call" | custom-call | flops 4026531840 | bytes 1048576 | tf_op jit(solution)/shard_map/pallas_call | solution.py:346
  42.3 3.9 %collective-permute-start.10 = (f32[256,256]{1,0:T(8,128)S(1)}, f32[256,256]{1,0:T(8,128)S(1)}, u32[]{:S(2)}, u32[]{:S(2)}) collective-permute-start(f32[256,256]{1,0:T(8,128)S(1)} %get-tuple-element.47.re), channel_id=1, source_target_pairs={{0,4},{4,8},{8,12},{12,16},{16,20},{20,24},{24,28},{1,5},{5,9},{9,... | collective-permute-start | bytes 786440 | tf_op jit(solution)/shard_map/ppermute | solution.py:475
  46.3 2.7 %collective-permute-start.9 = (f32[256,256]{1,0:T(8,128)S(1)}, f32[256,256]{1,0:T(8,128)S(1)}, u32[]{:S(2)}, u32[]{:S(2)}) collective-permute-start(f32[256,256]{1,0:T(8,128)S(1)} %get-tuple-element.46.im), channel_id=1, source_target_pairs={{0,4},{4,8},{8,12},{12,16},{16,20},{20,24},{24,28},{1,5},{5,9},{9,... | collective-permute-start | bytes 786440 | tf_op jit(solution)/shard_map/ppermute | solution.py:475
  49.0 2.5 %shard_map.88 = (f32[1,2,256,1024]{3,2,1,0:T(8,128)}, f32[256,384]{1,0:T(8,128)S(1)}, f32[256,384]{1,0:T(8,128)S(1)}) custom-call(s32[2]{0:T(128)S(1)} %pad_add_fusion.offsets, s32[2]{0:T(128)S(1)} %collective-permute-done.offsets.came_offsets, f32[256,256]{1,0:T(8,128)S(1)} %get-tuple-element.47.re, f32[256,256]{1,0:T(8,128)S(1)} %get-tuple-element.46.im), custom_call_target="tpu_custom_call" | custom-call | tf_op jit(solution)/shard_map/pallas_call | solution.py:430
  51.5 1.5 %collective-permute-done.10.came = f32[256,256]{1,0:T(8,128)S(1)} collective-permute-done((f32[256,256]{1,0:T(8,128)S(1)}, f32[256,256]{1,0:T(8,128)S(1)}, u32[]{:S(2)}, u32[]{:S(2)}) %collective-permute-start.10) | collective-permute-done | bytes 262176 | tf_op jit(solution)/shard_map/ppermute | solution.py:475
  53.0 1.5 %shard_map.89.base = f32[1,2,256,1024]{3,2,1,0:T(8,128)} custom-call(s32[2]{0:T(128)S(1)} %collective-permute-done.offsets.came_offsets, f32[256,256]{1,0:T(8,128)S(1)} %collective-permute-done.10.came, f32[256,384]{1,0:T(8,128)S(1)} %get-tuple-element.49.run, f32[1,2,256,1024]{3,2,1,0:T(8,128)} %get-tuple-element.50.base), custom_call_target="tpu_custom_call", output_to_operand_aliasing={{}: (3, {})} | custom-call | tf_op jit(solution)/shard_map/pallas_call | solution.py:461
  54.5 2.1 %collective-permute-done.9.came = f32[256,256]{1,0:T(8,128)S(1)} collective-permute-done((f32[256,256]{1,0:T(8,128)S(1)}, f32[256,256]{1,0:T(8,128)S(1)}, u32[]{:S(2)}, u32[]{:S(2)}) %collective-permute-start.9) | collective-permute-done | bytes 262176 | tf_op jit(solution)/shard_map/ppermute | solution.py:475
  56.6 1.5 %shard_map.90 = f32[1,2,256,1024]{3,2,1,0:T(8,128)} custom-call(s32[2]{0:T(128)S(1)} %collective-permute-done.offsets.came_offsets, f32[256,256]{1,0:T(8,128)S(1)} %collective-permute-done.9.came, f32[256,384]{1,0:T(8,128)S(1)} %get-tuple-element.48.run, f32[1,2,256,1024]{3,2,1,0:T(8,128)} %shard_map.89.base), custom_call_target="tpu_custom_call", output_to_operand_aliasing={{}: (3, {})} | custom-call | tf_op jit(solution)/shard_map/pallas_call | solution.py:461
  (12 shorter events, 0.0 us)
Async XLA Ops:
  1.4 6.5 %collective-permute-start = (s32[2]{0:T(128)S(1)}, s32[2]{0:T(128)S(1)}, u32[]{:S(2)}, u32[]{:S(2)}) collective-permute-start(s32[2]{0:T(128)S(1)} %pad_add_fusion.offsets), channel_id=1, source_target_pairs={{0,4},{4,8},{8,12},{12,16},{16,20},{20,24},{24,28},{1,5},{5,9},{9,... | collective-permute-start | bytes 32 | tf_op jit(solution)/shard_map/ppermute | solution.py:475
  7.8 3.2 %copy-start.2 = (f32[256,256]{1,0:T(8,128)S(1)}, f32[256,256]{1,0:T(8,128)}, u32[]{:S(2)}) copy-start(f32[256,256]{1,0:T(8,128)} %phase.1) | copy-start | bytes 786436
  7.9 3.2 %copy-start.3 = (f32[1,256,256]{2,1,0:T(8,128)S(1)}, f32[1,256,256]{2,1,0:T(8,128)}, u32[]{:S(2)}) copy-start(f32[1,256,256]{2,1,0:T(8,128)} %refs_0_.1) | copy-start | bytes 786436
  8.8 12.0 %collective-permute-start.2 = (f32[2,152,256]{2,1,0:T(8,128)S(1)}, f32[2,152,256]{2,1,0:T(8,128)S(1)}, u32[]{:S(2)}, u32[]{:S(2)}) collective-permute-start(f32[2,152,256]{2,1,0:T(8,128)S(1)} %get-tuple-element.31), channel_id=1, source_target_pairs={{4,0},{8,4},{12,8},{16,12},{20,16},{24,20},{28,24},{5,1},{9,5},{13... | collective-permute-start | bytes 933896 | tf_op jit(solution)/shard_map/ppermute | solution.py:475
  11.1 17.3 %copy-start = (bf16[4,768,256]{2,1,0:T(8,128)(2,1)S(1)}, bf16[4,768,256]{2,1,0:T(8,128)(2,1)}, u32[]{:S(2)}) copy-start(bf16[4,768,256]{2,1,0:T(8,128)(2,1)} %constant.13.clone.refs_7_.refs_13_) | copy-start | bytes 4718596
  11.1 17.2 %copy-start.1 = (bf16[8,256,256]{2,1,0:T(8,128)(2,1)S(1)}, bf16[8,256,256]{2,1,0:T(8,128)(2,1)}, u32[]{:S(2)}) copy-start(bf16[8,256,256]{2,1,0:T(8,128)(2,1)} %constant.14.clone.refs_8_.refs_14_) | copy-start | bytes 3145732
  13.5 10.5 %collective-permute-start.1 = (f32[2,104,256]{2,1,0:T(8,128)S(1)}, f32[2,104,256]{2,1,0:T(8,128)S(1)}, u32[]{:S(2)}, u32[]{:S(2)}) collective-permute-start(f32[2,104,256]{2,1,0:T(8,128)S(1)} %get-tuple-element.29), channel_id=1, source_target_pairs={{4,0},{8,4},{12,8},{16,12},{20,16},{24,20},{28,24},{5,1},{9,5},{13... | collective-permute-start | bytes 638984 | tf_op jit(solution)/shard_map/ppermute | solution.py:475
  20.9 7.4 %collective-permute-start.3 = (f32[2,152,256]{2,1,0:T(8,128)S(1)}, f32[2,152,256]{2,1,0:T(8,128)}, u32[]{:S(2)}, u32[]{:S(2)}) collective-permute-start(f32[2,152,256]{2,1,0:T(8,128)S(1)} %broadcast_select_fusion.refs_0_), channel_id=1, source_target_pairs={{0,2},{1,3},{2,0},{3,1},{4,6},{5,7},{6,4},{7,5},{8,10},{9,11},{10,... | collective-permute-start | bytes 933896 | tf_op jit(solution)/shard_map/ppermute | solution.py:480
  24.1 2.2 %collective-permute-start.4 = (f32[2,152,256]{2,1,0:T(8,128)S(1)}, f32[2,152,256]{2,1,0:T(8,128)S(1)}, u32[]{:S(2)}, u32[]{:S(2)}) collective-permute-start(f32[2,152,256]{2,1,0:T(8,128)S(1)} %broadcast_select_fusion.refs_0_), channel_id=1, source_target_pairs={{0,1},{1,0},{2,3},{3,2},{4,5},{5,4},{6,7},{7,6},{8,9},{9,8},{10,11... | collective-permute-start | bytes 933896 | tf_op jit(solution)/shard_map/ppermute | solution.py:480
  24.2 4.1 %collective-permute-start.5 = (f32[2,104,256]{2,1,0:T(8,128)S(1)}, f32[2,104,256]{2,1,0:T(8,128)}, u32[]{:S(2)}, u32[]{:S(2)}) collective-permute-start(f32[2,104,256]{2,1,0:T(8,128)S(1)} %broadcast_select_fusion.1.refs_1_), channel_id=1, source_target_pairs={{0,1},{1,0},{2,3},{3,2},{4,5},{5,4},{6,7},{7,6},{8,9},{9,8},{10,11... | collective-permute-start | bytes 638984 | tf_op jit(solution)/shard_map/ppermute | solution.py:480
  24.8 7.8 %collective-permute-start.6 = (f32[2,104,256]{2,1,0:T(8,128)S(1)}, f32[2,104,256]{2,1,0:T(8,128)}, u32[]{:S(2)}, u32[]{:S(2)}) collective-permute-start(f32[2,104,256]{2,1,0:T(8,128)S(1)} %broadcast_select_fusion.1.refs_1_), channel_id=1, source_target_pairs={{0,2},{1,3},{2,0},{3,1},{4,6},{5,7},{6,4},{7,5},{8,10},{9,11},{10,... | collective-permute-start | bytes 638984 | tf_op jit(solution)/shard_map/ppermute | solution.py:480
  28.3 6.1 %collective-permute-start.7 = (f32[2,152,256]{2,1,0:T(8,128)}, f32[2,152,256]{2,1,0:T(8,128)}, u32[]{:S(2)}, u32[]{:S(2)}) collective-permute-start(f32[2,152,256]{2,1,0:T(8,128)} %collective-permute-done.3.refs_4_), channel_id=1, source_target_pairs={{0,1},{1,0},{2,3},{3,2},{4,5},{5,4},{6,7},{7,6},{8,9},{9,8},{10,11... | collective-permute-start | bytes 933896 | tf_op jit(solution)/shard_map/ppermute | solution.py:480
  32.5 1.9 %collective-permute-start.8 = (f32[2,104,256]{2,1,0:T(8,128)}, f32[2,104,256]{2,1,0:T(8,128)S(1)}, u32[]{:S(2)}, u32[]{:S(2)}) collective-permute-start(f32[2,104,256]{2,1,0:T(8,128)} %collective-permute-done.6.refs_5_), channel_id=1, source_target_pairs={{0,1},{1,0},{2,3},{3,2},{4,5},{5,4},{6,7},{7,6},{8,9},{9,8},{10,11... | collective-permute-start | bytes 638984 | tf_op jit(solution)/shard_map/ppermute | solution.py:480
  42.3 10.7 %collective-permute-start.10 = (f32[256,256]{1,0:T(8,128)S(1)}, f32[256,256]{1,0:T(8,128)S(1)}, u32[]{:S(2)}, u32[]{:S(2)}) collective-permute-start(f32[256,256]{1,0:T(8,128)S(1)} %get-tuple-element.47.re), channel_id=1, source_target_pairs={{0,4},{4,8},{8,12},{12,16},{16,20},{20,24},{24,28},{1,5},{5,9},{9,... | collective-permute-start | bytes 786440 | tf_op jit(solution)/shard_map/ppermute | solution.py:475
  46.3 10.3 %collective-permute-start.9 = (f32[256,256]{1,0:T(8,128)S(1)}, f32[256,256]{1,0:T(8,128)S(1)}, u32[]{:S(2)}, u32[]{:S(2)}) collective-permute-start(f32[256,256]{1,0:T(8,128)S(1)} %get-tuple-element.46.im), channel_id=1, source_target_pairs={{0,4},{4,8},{8,12},{12,16},{16,20},{20,24},{24,28},{1,5},{5,9},{9,... | collective-permute-start | bytes 786440 | tf_op jit(solution)/shard_map/ppermute | solution.py:475
